TPU v7x, 32 devices: a whole 2x2x4 slice. The times are simulated.
32 devices in a mesh: section: 2 (over core), seq: 4 (over z), dp: 4 (over y, x).
Axes of the slice: x: 2, y: 2, z: 4, core: 2. Of those that a mesh axis runs over, the one named last changes fastest.
Arguments:
- hidden_in: bfloat16 [8, 1024, 1536], P('dp', 'seq'), may hold values from -6 to 6
- doc_starts: int32 [8, 4], P('dp'), may hold values from 0 to 1023, as said below
- cotangent: bfloat16 [8, 1024, 1536], P('dp', 'seq'), may hold values from -6 to 6
- norm_gain: bfloat16 [2, 1536], P('section', 'seq'), may hold values from 0.5 to 1.5
- in_weight: bfloat16 [2, 1536, 6448], P('section', 'seq'), may hold values from -0.15625 to 0.15625
- conv_weight: bfloat16 [2, 4, 3328], P('section', None, 'seq'), may hold values from -3 to 3
- conv_bias: bfloat16 [2, 3328], P('section', 'seq'), may hold values from -3 to 3
- step_bias: bfloat16 [2, 48], P('section', 'seq'), may hold values from -6 to -2
- decay_log: bfloat16 [2, 48], P('section', 'seq'), may hold values from -5 to 2
- skip_gain: bfloat16 [2, 48], P('section', 'seq'), may hold values from 0.099609375 to 1.8984375
- gate_gain: bfloat16 [2, 3072], P('section', 'seq'), may hold values from 0.5 to 1.5
- out_weight: bfloat16 [2, 3072, 1536], P('section', 'seq'), may hold values from -0.109375 to 0.109375
Outputs:
- layer_out: bfloat16 [2, 8, 1024, 1536], P('section', 'dp', 'seq')
- input_grads: float32 [2, 8, 1024, 1536], P('section', 'dp', 'seq')
- grad_norm_gain: float32 [2, 1536], P('section', 'seq')
- grad_in_weight: float32 [2, 1536, 6448], P('section', 'seq')
- grad_conv_weight: float32 [2, 4, 3328], P('section', None, 'seq')
- grad_conv_bias: float32 [2, 3328], P('section', 'seq')
- grad_step_bias: float32 [2, 48], P('section', 'seq')
- grad_decay_log: float32 [2, 48], P('section', 'seq')
- grad_skip_gain: float32 [2, 48], P('section', 'seq')
- grad_gate_gain: float32 [2, 3072], P('section', 'seq')
- grad_out_weight: float32 [2, 3072, 1536], P('section', 'seq')
Inputs may be any that keep to these rules, and one draw needn't show every extreme that they name: `doc_starts`: entries are positions within a stream. Among the 2 streams of each index of dp, one drawn from the seed has all entries 0 (a single document); every other stream has entry 0 equal to 0.
All inputs are finite; a program needn't handle non-finite values.
Results may differ from a plain program's by a relative error of at most 0.04.
Values may be sent and summed in bfloat16 or wider, within the bound.
A program may use at most 320 MiB of HBM per device.

v0:
```python
import jax
import jax.numpy as jnp
from jax import lax
from jax.sharding import PartitionSpec as P

SPAN = 256


EPSILON = 1e-05
HIGHEST = lax.Precision.HIGHEST


def shifted_2(array, axis, by):
    count = lax.axis_size(axis)
    pairs = [(i, i + by) for i in range(count) if 0 <= i + by < count]
    return lax.ppermute(array, axis, pairs)


def norm_rows(rows_in, gain_vec):
    return (
        rows_in
        * lax.rsqrt(jnp.mean(rows_in * rows_in, axis=-1, keepdims=True) + EPSILON)
        * gain_vec
    )


def gate_norm(mixed_rows, gate_in, gain_vec):
    return norm_rows(mixed_rows * jax.nn.silu(gate_in), gain_vec)


def causal_conv(signal, kernel, offset, segment_ids):
    tap_count = kernel.shape[0]
    summed = signal * kernel[tap_count - 1] + offset
    for lag_size in range(1, tap_count):
        shifted = jnp.pad(signal, ((lag_size, 0), (0, 0)))[:-lag_size]
        shifted_ids = jnp.pad(segment_ids, (lag_size, 0), constant_values=-1)[:-lag_size]
        same_doc = (shifted_ids == segment_ids).astype(signal.dtype)
        summed = summed + shifted * same_doc[:, None] * kernel[tap_count - 1 - lag_size]
    return summed


def ssd_scan(values, deltas, log_rates, b_rows, c_rows, segment_ids):
    length, n_heads, head_width = values.shape
    blocks = length // SPAN
    float_kind = values.dtype
    indices = jnp.arange(SPAN)
    causal = indices[:, None] >= indices[None, :]
    inputs = (
        values.reshape(blocks, SPAN, n_heads, head_width),
        deltas.reshape(blocks, SPAN, n_heads),
        log_rates.reshape(blocks, SPAN, n_heads),
        b_rows.reshape(blocks, SPAN, -1),
        c_rows.reshape(blocks, SPAN, -1),
        segment_ids.reshape(blocks, SPAN),
    )

    def advance(state_pair, block_in):
        memory, last_id = state_pair
        block_vals, block_deltas, block_rates, block_b, block_c, block_ids = block_in
        cumulative = jnp.cumsum(block_rates, axis=0)
        same_doc = causal & (block_ids[:, None] == block_ids[None, :])
        doc_mask = same_doc.astype(float_kind)[:, :, None]
        decay_mat = (
            jnp.exp(
                jnp.where(
                    same_doc[:, :, None], cumulative[:, None, :] - cumulative[None, :, :], 0.0
                )
            )
            * doc_mask
        )
        scores = jnp.dot(block_c, block_b.T, precision=HIGHEST)
        mix_weights = scores[:, :, None] * decay_mat * block_deltas[None, :, :]
        local_out = jnp.einsum("ijh,jhp->ihp", mix_weights, block_vals, precision=HIGHEST)
        carried = (block_ids == last_id).astype(float_kind)
        from_memory = (
            jnp.einsum("in,hpn->ihp", block_c, memory, precision=HIGHEST)
            * (carried[:, None] * jnp.exp(cumulative))[:, :, None]
        )
        to_end = (
            (block_ids == block_ids[-1]).astype(float_kind)[:, None]
            * jnp.exp(cumulative[-1][None, :] - cumulative)
            * block_deltas
        )
        fresh_state = jnp.einsum("jh,jhp,jn->hpn", to_end, block_vals, block_b, precision=HIGHEST)
        memory = memory * (carried[-1] * jnp.exp(cumulative[-1]))[:, None, None] + fresh_state
        return ((memory, block_ids[-1]), local_out + from_memory)

    initial = (
        jnp.zeros((n_heads, head_width, b_rows.shape[1]), float_kind),
        jnp.array(-1, dtype=jnp.int32),
    )
    _, outputs = lax.scan(jax.checkpoint(advance), initial, inputs)
    return outputs.reshape(length, n_heads, head_width)


def mix_heads(
    proj_x, proj_dt, proj_bc, kernel, offset, dt_offset, rate_log, skip_part, segment_ids
):
    channels = proj_x.shape[1]
    n_heads = proj_dt.shape[1]
    n_state = proj_bc.shape[1] // 2
    length = proj_x.shape[0]
    activated = jax.nn.silu(
        causal_conv(jnp.concatenate([proj_x, proj_bc], axis=1), kernel, offset, segment_ids)
    )
    values = activated[:, :channels].reshape(length, n_heads, channels // n_heads)
    b_rows = activated[:, channels : channels + n_state]
    c_rows = activated[:, channels + n_state :]
    deltas = jax.nn.softplus(proj_dt + dt_offset)
    log_rates = -jnp.exp(rate_log) * deltas
    scanned = (
        ssd_scan(values, deltas, log_rates, b_rows, c_rows, segment_ids)
        + skip_part[None, :, None] * values
    )
    return scanned.reshape(length, channels)


def own_params(weights, seq_rank, seq_count):
    (
        norm_gain,
        in_weight,
        conv_weight,
        conv_bias,
        step_bias,
        decay_log,
        skip_gain,
        gate_gain,
        out_weight,
    ) = weights
    inner_width = out_weight.shape[0]
    per_device = inner_width // seq_count
    heads_here = step_bias.shape[0] // seq_count
    kernel = jnp.concatenate(
        [
            lax.dynamic_slice_in_dim(conv_weight, seq_rank * per_device, per_device, 1),
            conv_weight[:, inner_width:],
        ],
        axis=1,
    )
    offset = jnp.concatenate(
        [
            lax.dynamic_slice_in_dim(conv_bias, seq_rank * per_device, per_device, 0),
            conv_bias[inner_width:],
        ],
        axis=0,
    )
    picked = [
        lax.dynamic_slice_in_dim(head_param, seq_rank * heads_here, heads_here, 0)
        for head_param in (step_bias, decay_log, skip_gain)
    ]
    return tuple(
        (
            head_param.astype(jnp.float32)
            for head_param in (kernel, offset, picked[0], picked[1], picked[2])
        )
    )


def forward_layer(stream_in, segment_ids, weights, seq_rank, seq_count):
    (
        norm_gain,
        in_weight,
        conv_weight,
        conv_bias,
        step_bias,
        decay_log,
        skip_gain,
        gate_gain,
        out_weight,
    ) = weights
    inner_width = out_weight.shape[0]
    n_heads = step_bias.shape[0]
    normed = norm_rows(stream_in, norm_gain.astype(jnp.float32)).astype(jnp.bfloat16)
    projected = jnp.dot(normed, in_weight, preferred_element_type=jnp.float32).astype(jnp.bfloat16)
    total_width = projected.shape[1]
    gate_in = projected[:, :inner_width]
    proj_x = projected[:, inner_width : 2 * inner_width]
    proj_bc = projected[:, 2 * inner_width : total_width - n_heads]
    proj_dt = projected[:, total_width - n_heads :]
    head_x, head_dt = (
        lax.all_to_all(proj_x, "seq", split_axis=1, concat_axis=0, tiled=True),
        lax.all_to_all(proj_dt, "seq", split_axis=1, concat_axis=0, tiled=True),
    )
    shared_bc = lax.all_gather(proj_bc, "seq", axis=0, tiled=True)
    local_params = own_params(weights, seq_rank, seq_count)
    mixed_heads = mix_heads(
        head_x.astype(jnp.float32),
        head_dt.astype(jnp.float32),
        shared_bc.astype(jnp.float32),
        local_params[0],
        local_params[1],
        local_params[2],
        local_params[3],
        local_params[4],
        segment_ids,
    ).astype(jnp.bfloat16)
    mixed_rows = lax.all_to_all(mixed_heads, "seq", split_axis=0, concat_axis=1, tiled=True)
    gated_rows = gate_norm(
        mixed_rows.astype(jnp.float32), gate_in.astype(jnp.float32), gate_gain.astype(jnp.float32)
    ).astype(jnp.bfloat16)
    result = stream_in + jnp.dot(gated_rows, out_weight, preferred_element_type=jnp.float32)
    saved_data = (
        stream_in,
        normed,
        projected,
        head_x,
        head_dt,
        shared_bc,
        mixed_rows,
        gated_rows,
        segment_ids,
    )
    return (result, saved_data)


def backward_layer(saved_data, weights, grad_out, seq_rank, seq_count):
    (
        stream_in,
        normed,
        projected,
        head_x,
        head_dt,
        shared_bc,
        mixed_rows,
        gated_rows,
        segment_ids,
    ) = saved_data
    (
        norm_gain,
        in_weight,
        conv_weight,
        conv_bias,
        step_bias,
        decay_log,
        skip_gain,
        gate_gain,
        out_weight,
    ) = weights
    inner_width = out_weight.shape[0]
    n_heads = step_bias.shape[0]
    grad_low = grad_out.astype(jnp.bfloat16)
    grad_out_weight = jnp.einsum(
        "ti,td->id", gated_rows, grad_low, preferred_element_type=jnp.float32
    )
    grad_gated = jnp.einsum("td,id->ti", grad_low, out_weight, preferred_element_type=jnp.float32)
    gate_in = projected[:, :inner_width].astype(jnp.float32)
    _, pull_gate = jax.vjp(
        gate_norm, mixed_rows.astype(jnp.float32), gate_in, gate_gain.astype(jnp.float32)
    )
    grad_mixed, grad_gate_in, grad_gate_gain = pull_gate(grad_gated)
    grad_heads = lax.all_to_all(
        grad_mixed.astype(jnp.bfloat16), "seq", split_axis=1, concat_axis=0, tiled=True
    )
    local_params = own_params(weights, seq_rank, seq_count)

    def head_part(part_x, part_dt, part_bc, kernel, offset, dt_offset, rate_log, skip_part):
        return mix_heads(
            part_x, part_dt, part_bc, kernel, offset, dt_offset, rate_log, skip_part, segment_ids
        )

    _, pull_heads = jax.vjp(
        head_part,
        head_x.astype(jnp.float32),
        head_dt.astype(jnp.float32),
        shared_bc.astype(jnp.float32),
        local_params[0],
        local_params[1],
        local_params[2],
        local_params[3],
        local_params[4],
    )
    grad_x, grad_dt, grad_bc, grad_kernel, grad_offset, grad_dt_offset, grad_rate_log, grad_skip = (
        pull_heads(grad_heads.astype(jnp.float32))
    )
    back_x, back_dt = (
        lax.all_to_all(grad_x.astype(jnp.bfloat16), "seq", split_axis=0, concat_axis=1, tiled=True),
        lax.all_to_all(
            grad_dt.astype(jnp.bfloat16), "seq", split_axis=0, concat_axis=1, tiled=True
        ),
    )
    back_bc = lax.psum_scatter(grad_bc, "seq", scatter_dimension=0, tiled=True)
    grad_proj = jnp.concatenate(
        [grad_gate_in.astype(jnp.bfloat16), back_x, back_bc.astype(jnp.bfloat16), back_dt], axis=1
    )
    grad_in_weight = jnp.einsum("td,tp->dp", normed, grad_proj, preferred_element_type=jnp.float32)
    grad_normed = jnp.einsum("tp,dp->td", grad_proj, in_weight, preferred_element_type=jnp.float32)
    _, pull_norm = jax.vjp(norm_rows, stream_in, norm_gain.astype(jnp.float32))
    grad_stream, grad_norm_gain = pull_norm(grad_normed)
    per_device = inner_width // seq_count
    heads_here = n_heads // seq_count
    conv_grad = jnp.concatenate(
        [
            lax.dynamic_update_slice_in_dim(
                jnp.zeros((grad_kernel.shape[0], inner_width), jnp.float32),
                grad_kernel[:, :per_device],
                seq_rank * per_device,
                1,
            ),
            grad_kernel[:, per_device:],
        ],
        axis=1,
    )
    bias_grad = jnp.concatenate(
        [
            lax.dynamic_update_slice_in_dim(
                jnp.zeros((inner_width,), jnp.float32),
                grad_offset[:per_device],
                seq_rank * per_device,
                0,
            ),
            grad_offset[per_device:],
        ],
        axis=0,
    )

    def spread(head_grad):
        return lax.dynamic_update_slice_in_dim(
            jnp.zeros((n_heads,), jnp.float32), head_grad, seq_rank * heads_here, 0
        )

    grads = (
        grad_norm_gain,
        grad_in_weight,
        conv_grad,
        bias_grad,
        spread(grad_dt_offset),
        spread(grad_rate_log),
        spread(grad_skip),
        grad_gate_gain,
        grad_out_weight,
    )
    return (grad_out + grad_stream, grads)


def pick(flag, first_tree, second_tree):
    return jax.tree.map(
        lambda first_leaf, second_leaf: jnp.where(flag, first_leaf, second_leaf),
        first_tree,
        second_tree,
    )


def local(
    hidden_in,
    doc_starts,
    cotangent,
    norm_gain,
    in_weight,
    conv_weight,
    conv_bias,
    step_bias,
    decay_log,
    skip_gain,
    gate_gain,
    out_weight,
):
    section_rank = lax.axis_index("section")
    seq_rank = lax.axis_index("seq")
    seq_count = lax.axis_size("seq")
    first_section = section_rank == 0
    last_section = section_rank == 1
    weights = (
        lax.all_gather(norm_gain[0], "seq", axis=0, tiled=True),
        lax.all_gather(in_weight[0], "seq", axis=0, tiled=True),
        lax.all_gather(conv_weight[0], "seq", axis=1, tiled=True),
        lax.all_gather(conv_bias[0], "seq", axis=0, tiled=True),
        lax.all_gather(step_bias[0], "seq", axis=0, tiled=True),
        lax.all_gather(decay_log[0], "seq", axis=0, tiled=True),
        lax.all_gather(skip_gain[0], "seq", axis=0, tiled=True),
        lax.all_gather(gate_gain[0], "seq", axis=0, tiled=True),
        lax.all_gather(out_weight[0], "seq", axis=0, tiled=True),
    )
    micro_count, token_count, model_width = hidden_in.shape
    positions = jnp.arange(token_count * seq_count, dtype=jnp.int32)
    doc_ids = [
        jnp.sum(
            (doc_starts[item_index][:, None] <= positions[None, :]).astype(jnp.int32),
            axis=0,
            dtype=jnp.int32,
        )
        for item_index in range(micro_count)
    ]
    carried = jnp.zeros((token_count, model_width), jnp.bfloat16)
    results = []
    saved_steps = []
    for moment in range(micro_count + 1):
        own_input = hidden_in[min(moment, micro_count - 1)]
        layer_input = jnp.where(first_section, own_input, carried)
        doc_here = jnp.where(
            first_section, doc_ids[min(moment, micro_count - 1)], doc_ids[max(moment - 1, 0)]
        )
        result, saved_data = forward_layer(
            layer_input.astype(jnp.float32), doc_here, weights, seq_rank, seq_count
        )
        result_low = result.astype(jnp.bfloat16)
        if moment < micro_count:
            carried = shifted_2(result_low, "section", 1)
        results.append(result_low)
        saved_steps.append(saved_data)
    layer_out = jnp.stack(
        [
            jnp.where(first_section, results[item_index], results[item_index + 1])
            for item_index in range(micro_count)
        ]
    )
    kept_steps = [
        pick(first_section, saved_steps[item_index], saved_steps[item_index + 1])
        for item_index in range(micro_count)
    ]
    back_weights = (
        lax.all_gather(norm_gain[0], "seq", axis=0, tiled=True),
        lax.all_gather(in_weight[0], "seq", axis=0, tiled=True),
        lax.all_gather(conv_weight[0], "seq", axis=1, tiled=True),
        lax.all_gather(conv_bias[0], "seq", axis=0, tiled=True),
        lax.all_gather(step_bias[0], "seq", axis=0, tiled=True),
        lax.all_gather(decay_log[0], "seq", axis=0, tiled=True),
        lax.all_gather(skip_gain[0], "seq", axis=0, tiled=True),
        lax.all_gather(gate_gain[0], "seq", axis=0, tiled=True),
        lax.all_gather(out_weight[0], "seq", axis=0, tiled=True),
    )
    grad_carry = jnp.zeros((token_count, model_width), jnp.bfloat16)
    grad_totals = None
    grad_steps = []
    for moment in range(micro_count + 1):
        late_index = max(micro_count - 1 - moment, 0)
        early_index = min(micro_count - moment, micro_count - 1)
        saved_data = pick(last_section, kept_steps[late_index], kept_steps[early_index])
        incoming = jnp.where(last_section, cotangent[late_index], grad_carry).astype(jnp.float32)
        if moment == micro_count:
            incoming = jnp.where(last_section, 0.0, incoming)
        grad_stream, grads = backward_layer(saved_data, back_weights, incoming, seq_rank, seq_count)
        grad_totals = grads if grad_totals is None else jax.tree.map(jnp.add, grad_totals, grads)
        if moment < micro_count:
            grad_carry = shifted_2(grad_stream.astype(jnp.bfloat16), "section", -1)
        grad_steps.append(grad_stream)
    input_grads = jnp.stack(
        [
            jnp.where(
                last_section,
                grad_steps[micro_count - 1 - item_index],
                grad_steps[micro_count - item_index],
            )
            for item_index in range(micro_count)
        ]
    )
    reduced = (
        lax.psum_scatter(grad_totals[0], "seq", scatter_dimension=0, tiled=True),
        lax.psum_scatter(grad_totals[1], "seq", scatter_dimension=0, tiled=True),
        lax.psum_scatter(grad_totals[2], "seq", scatter_dimension=1, tiled=True),
        lax.psum_scatter(grad_totals[3], "seq", scatter_dimension=0, tiled=True),
        lax.psum_scatter(grad_totals[4], "seq", scatter_dimension=0, tiled=True),
        lax.psum_scatter(grad_totals[5], "seq", scatter_dimension=0, tiled=True),
        lax.psum_scatter(grad_totals[6], "seq", scatter_dimension=0, tiled=True),
        lax.psum_scatter(grad_totals[7], "seq", scatter_dimension=0, tiled=True),
        lax.psum_scatter(grad_totals[8], "seq", scatter_dimension=0, tiled=True),
    )
    summed = lax.psum(
        (
            reduced[0],
            reduced[1],
            reduced[2],
            reduced[3],
            reduced[4],
            reduced[5],
            reduced[6],
            reduced[7],
            reduced[8],
        ),
        "dp",
    )
    return (
        layer_out[None],
        input_grads[None],
        summed[0][None],
        summed[1][None],
        summed[2][None],
        summed[3][None],
        summed[4][None],
        summed[5][None],
        summed[6][None],
        summed[7][None],
        summed[8][None],
    )


def solution(mesh):
    return jax.shard_map(
        local,
        mesh=mesh,
        in_specs=(
            P("dp", "seq", None),
            P("dp", None),
            P("dp", "seq", None),
            P("section", "seq"),
            P("section", "seq", None),
            P("section", None, "seq"),
            P("section", "seq"),
            P("section", "seq"),
            P("section", "seq"),
            P("section", "seq"),
            P("section", "seq"),
            P("section", "seq", None),
        ),
        out_specs=(
            P("section", "dp", "seq", None),
            P("section", "dp", "seq", None),
            P("section", "seq"),
            P("section", "seq", None),
            P("section", None, "seq"),
            P("section", "seq"),
            P("section", "seq"),
            P("section", "seq"),
            P("section", "seq"),
            P("section", "seq"),
            P("section", "seq", None),
        ),
        check_vma=False,
    )
```

profile of v0, /device:TPU:0, one launch (start us, length us, event | category | flops | bytes accessed | tf_op | source)
XLA Modules:
  0.0 4050.3 jit_solution(8791595692710877802)
XLA Ops:
  21.8 328.4 %all-gather.12.cloned.1.call-done = bf16[1,1536,6448]{1,2,0:T(8,128)(2,1)} async-done(((bf16[1,384,6448]{1,2,0:T(8,128)(2,1)}), bf16[1,1536,6448]{1,2,0:T(8,128)(2,1)}) %all-gather.12.cloned.1.call-update) | async-done | bytes 19808272 | tf_op jit(solution)/shard_map/all_gather | solution.py:364
  380.7 105.6 %all-gather.4 = bf16[1,4,3328]{1,0,2:T(2,128)(2,1)} all-gather(bf16[1,4,832]{1,0,2:T(2,128)(2,1)S(1)} %copy.607), channel_id=6, replica_groups=mesh['section'=2,'seq'=4,'dp'=4] {'seq'}, dimensions={2}, use_global_device_ids=true | all-gather | bytes 33280 | tf_op jit(solution)/shard_map/all_gather | solution.py:365
  490.9 23.9 all-reduce.85
  518.3 26.3 all_gather.49
  564.9 157.1 %while.171 = (s32[]{:T(128)}, f32[12,64,128]{2,1,0:T(8,128)S(1)}, s32[]{:T(128)}, f32[4,256,12,64]{1,0,3,2:T(4,128)}, s32[4,256]{1,0:T(4,128)}, /*index=5*/f32[4...) while((s32[]{:T(128)}, f32[12,64,128]{2,1,0:T(8,128)S(1)}, ...), condition=%wide.region_5.6_spmd.clone, body=%wide.region_2.0_spmd.clone.sunk | while | flops 1314206720 | bytes 11876828 | solution.py:92
  585.7 17.9 dynamic_update_slice.306
  624.9 17.9 dynamic_update_slice.306
  664.2 17.9 dynamic_update_slice.306
  703.5 17.9 dynamic_update_slice.306
  731.6 29.6 all-gather.7
  806.1 44.8 %all_gather.55 = bf16[1024,256]{0,1:T(8,128)(2,1)S(1)} all-gather(bf16[256,256]{0,1:T(8,128)(2,1)S(1)} %slice-done.10), channel_id=1, replica_groups=mesh['section'=2,'seq'=4,'dp'=4] {'seq'}, dimensions={0}, use_global_device_ids=true | all-gather | bytes 655360 | tf_op jit(solution)/shard_map/all_gather | solution.py:184
  873.1 162.0 %while.172 = (s32[]{:T(128)}, f32[12,64,128]{2,1,0:T(8,128)S(1)}, s32[]{:T(128)}, f32[4,256,12,64]{1,0,3,2:T(4,128)}, s32[4,256]{1,0:T(4,128)}, /*index=5*/f32[4...) while((s32[]{:T(128)}, f32[12,64,128]{2,1,0:T(8,128)S(1)}, ...), condition=%wide.region_12.13_spmd.clone, body=%wide.region_9.12_spmd.clone.sunk | while | flops 1314206720 | bytes 11876828 | solution.py:92
  895.0 17.9 dynamic_update_slice.307
  935.5 17.9 dynamic_update_slice.307
  976.0 17.9 dynamic_update_slice.307
  1016.5 17.9 dynamic_update_slice.307
  1038.7 38.1 all_to_all.270
  1114.9 45.8 %all_gather.56 = bf16[1024,256]{0,1:T(8,128)(2,1)S(1)} all-gather(bf16[256,256]{0,1:T(8,128)(2,1)S(1)} %slice.829), channel_id=1, replica_groups=mesh['section'=2,'seq'=4,'dp'=4] {'seq'}, dimensions={0}, use_global_device_ids=true | all-gather | bytes 655360 | tf_op jit(solution)/shard_map/all_gather | solution.py:184
  1190.0 132.4 %while.173 = (s32[]{:T(128)}, f32[12,64,128]{2,1,0:T(8,128)S(1)}, s32[]{:T(128)}, f32[4,256,12,64]{1,0,3,2:T(4,128)}, s32[4,256]{1,0:T(4,128)}, /*index=5*/f32[4...) while((s32[]{:T(128)}, f32[12,64,128]{2,1,0:T(8,128)S(1)}, ...), condition=%wide.region_18.19_spmd.clone, body=%wide.region_15.18_spmd.clone.sunk | while | flops 1314206720 | bytes 11872948 | solution.py:92
  1204.5 17.9 dynamic_update_slice.308
  1237.6 17.9 dynamic_update_slice.308
  1270.6 17.9 dynamic_update_slice.308
  1303.7 17.9 dynamic_update_slice.308
  1407.8 20.3 all-to-all-done.9
  1443.6 42.6 %while.174 = (s32[]{:T(128)}, f32[12,64,128]{2,1,0:T(8,128)S(1)}, s32[]{:T(128)}, f32[4,12,64,128]{3,2,1,0:T(8,128)}, s32[4]{0:T(128)}, /*index=5*/s32[4,256]{1,...) while((s32[]{:T(128)}, f32[12,64,128]{2,1,0:T(8,128)S(1)}, ...), condition=%wide.region_25.27_spmd.clone, body=%wide.region_22.26_spmd.clone.sunk | while | flops 302982720 | bytes 2754277 | solution.py:92
  1491.4 232.3 %while.175 = (s32[]{:T(128)}, f32[12,64,128]{2,1,0:T(8,128)}, f32[4,256,12,64]{1,0,3,2:T(4,128)}, f32[4,256,12]{1,0,2:T(4,128)}, f32[4,256,12]{1,0,2:T(4,128)}, ...) while((s32[]{:T(128)}, f32[12,64,128]{2,1,0:T(8,128)}, ...), condition=%wide.region_38.40_spmd.clone, body=%wide.region_26.39_spmd.clone.sunk | while | flops 3038993408 | bytes 28852212 | solution.py:92
  1519.2 17.9 dynamic_update_slice.313
  1577.4 17.9 dynamic_update_slice.313
  1635.6 17.9 dynamic_update_slice.313
  1693.8 17.9 dynamic_update_slice.313
  1765.9 47.6 %reduce-scatter.9.cloned.1.call-done = f32[256,256]{0,1:T(8,128)} async-done(((f32[1024,256]{0,1:T(8,128)}), f32[256,256]{0,1:T(8,128)}) %reduce-scatter.9.cloned.1.call-update) | async-done | bytes 262160 | tf_op jit(solution)/shard_map/reduce_scatter | solution.py:281
  1860.0 32.9 all-to-all-done.12
  1908.3 42.6 %while.176 = (s32[]{:T(128)}, f32[12,64,128]{2,1,0:T(8,128)S(1)}, s32[]{:T(128)}, f32[4,12,64,128]{3,2,1,0:T(8,128)}, s32[4]{0:T(128)}, /*index=5*/s32[4,256]{1,...) while((s32[]{:T(128)}, f32[12,64,128]{2,1,0:T(8,128)S(1)}, ...), condition=%wide.region_47.49_spmd.clone, body=%wide.region_44.48_spmd.clone.sunk | while | flops 302982720 | bytes 2754277 | solution.py:92
  1956.1 232.0 %while.177 = (s32[]{:T(128)}, f32[12,64,128]{2,1,0:T(8,128)}, f32[4,256,12,64]{1,0,3,2:T(4,128)}, f32[4,256,12]{1,0,2:T(4,128)}, f32[4,256,12]{1,0,2:T(4,128)}, ...) while((s32[]{:T(128)}, f32[12,64,128]{2,1,0:T(8,128)}, ...), condition=%wide.region_60.62_spmd.clone, body=%wide.region_48.61_spmd.clone.sunk | while | flops 3038993408 | bytes 28852212 | solution.py:92
  1983.9 17.9 dynamic_update_slice.320
  2042.0 17.9 dynamic_update_slice.320
  2230.4 47.9 %reduce-scatter.11.cloned.1.call-done = f32[256,256]{0,1:T(8,128)} async-done(((f32[1024,256]{0,1:T(8,128)}), f32[256,256]{0,1:T(8,128)}) %reduce-scatter.11.cloned.1.call-update) | async-done | bytes 262160 | tf_op jit(solution)/shard_map/reduce_scatter | solution.py:281
  2376.3 42.9 %while.178 = (s32[]{:T(128)}, f32[12,64,128]{2,1,0:T(8,128)S(1)}, s32[]{:T(128)}, f32[4,12,64,128]{3,2,1,0:T(8,128)}, s32[4]{0:T(128)}, /*index=5*/s32[4,256]{1,...) while((s32[]{:T(128)}, f32[12,64,128]{2,1,0:T(8,128)S(1)}, ...), condition=%wide.region_69.71_spmd.clone, body=%wide.region_66.70_spmd.clone.sunk | while | flops 302982720 | bytes 2754277 | solution.py:92
  2424.4 232.1 %while.179 = (s32[]{:T(128)}, f32[12,64,128]{2,1,0:T(8,128)}, f32[4,256,12,64]{1,0,3,2:T(4,128)}, f32[4,256,12]{1,0,2:T(4,128)}, f32[4,256,12]{1,0,2:T(4,128)}, ...) while((s32[]{:T(128)}, f32[12,64,128]{2,1,0:T(8,128)}, ...), condition=%wide.region_82.84_spmd.clone, body=%wide.region_70.83_spmd.clone.sunk | while | flops 3038993408 | bytes 28852212 | solution.py:92
  2568.2 17.9 dynamic_update_slice.327
  2694.9 22.0 add_add_fusion.1
  2752.2 20.9 fusion.439
  2774.2 38.6 all-to-all-done.16
  2812.8 42.5 %add_add_fusion = f32[1536,6448]{0,1:T(8,128)} fusion(f32[1536,6448]{0,1:T(8,128)} %fusion.446, f32[1536,6448]{0,1:T(8,128)} %fusion.439, bf16[256,48]{0,1:T(8,128)(2,1)S(1)} %all_to_all.251, bf16[256,256]{0,1:T(8,128)(2,1)S(1)} %convert_element_type.787, bf16[256,3072]{0,1:T(8,128)(2,1)} %bitcast.85, bf16[256,3072]{0,1:T(8,128)(2,1)} %get-tuple-element.2865, ...), kind=kOutput, calls=%fused_computation.447 | convolution fusion | flops 5107859456 | bytes 123732992 | tf_op jit(solution)/shard_map/td,tp->dp/dot_general | solution.py:285
  2858.1 198.4 %reduce-scatter.17.cloned.1.call-done = f32[768,1536]{1,0:T(8,128)} async-done(((f32[3072,1536]{1,0:T(8,128)}), f32[768,1536]{1,0:T(8,128)}) %reduce-scatter.17.cloned.1.call-update) | async-done | bytes 4718608 | tf_op jit(solution)/shard_map/reduce_scatter | solution.py:455
  3056.5 656.5 %reduce-scatter.15.cloned.1.call-done = f32[384,6448]{0,1:T(8,128)} async-done(((f32[1536,6448]{0,1:T(8,128)}), f32[384,6448]{0,1:T(8,128)}) %reduce-scatter.15.cloned.1.call-update) | async-done | bytes 9904144 | tf_op jit(solution)/shard_map/reduce_scatter | solution.py:448
  3727.8 27.6 reduce-scatter.19.cloned.1.call-done
  3812.4 220.5 %all-reduce.88.cloned.1.call-done = (f32[1,384,6448]{1,2,0:T(8,128)}, f32[1,768,1536]{2,1,0:T(8,128)}) async-done(((f32[1,384,6448]{1,2,0:T(8,128)}, f32[1,768,1536]{2,1,0:T(8,128)}), (f32[1,384,6448]{1,2,0:T(8,128)}, f32[1,768,1536]{2,1,0:T(8,128)})) %all-reduce.88.cloned.1.call-update) | async-done | bytes 14622736 | tf_op jit(solution)/shard_map/psum | solution.py:457
  (2278 shorter events, 1640.5 us)
Async XLA Ops:
  7.2 343.0 %all-gather.12.cloned.1.call-start = ((), (), s32[]{:S(2)}) async-start(), calls=%async_computation.29 | async-start | bytes 24760320 | tf_op jit(solution)/shard_map/all_gather | solution.py:364
  21.5 338.8 %copy-start.111 = (f32[1536]{0:T(1024)}, f32[1536]{0:T(1024)S(1)}, u32[]{:S(2)}) copy-start(f32[1536]{0:T(1024)S(1)} %convert_reduce_fusion.2) | copy-start | bytes 18436
  21.8 328.4 %copy-start.229 = (f32[256]{0:T(256)}, f32[256]{0:T(256)S(1)}, u32[]{:S(2)}) copy-start(f32[256]{0:T(256)S(1)} %add_rsqrt_fusion.5) | copy-start | bytes 3076
  362.6 8.9 all-to-all-start
  371.5 173.1 %copy-start.117 = (bf16[256,4,12]{0,2,1:T(8,128)(2,1)}, bf16[256,4,12]{0,2,1:T(8,128)(2,1)S(1)}, u32[]{:S(2)}) copy-start(bf16[256,4,12]{0,2,1:T(8,128)(2,1)S(1)} %all-to-all-done) | copy-start | bytes 73732
  371.5 174.0 %all-to-all-start.1 = ((bf16[256,4,768]{0,2,1:T(8,128)(2,1)}), bf16[256,4,768]{0,2,1:T(8,128)(2,1)}, u32[]{:S(2)}, u32[]{:S(2)}) async-start(bf16[256,4,768]{0,2,1:T(8,128)(2,1)} %bitcast.8), calls=%async_computation.1 | async-start | bytes 3145728 | tf_op jit(solution)/shard_map/all_to_all | solution.py:181
  375.9 114.0 %copy-start.250 = (bf16[1,12]{1,0:T(2,128)(2,1)S(1)}, bf16[1,12]{1,0:T(2,128)(2,1)}, u32[]{:S(2)}) copy-start(bf16[1,12]{1,0:T(2,128)(2,1)} %param.39) | copy-start | bytes 76
  375.9 114.2 %copy-start.251 = (bf16[1,12]{1,0:T(2,128)(2,1)S(1)}, bf16[1,12]{1,0:T(2,128)(2,1)}, u32[]{:S(2)}) copy-start(bf16[1,12]{1,0:T(2,128)(2,1)} %param.38) | copy-start | bytes 76
  376.0 114.5 %copy-start.242 = (bf16[1,832]{1,0:T(2,128)(2,1)S(1)}, bf16[1,832]{1,0:T(2,128)(2,1)}, u32[]{:S(2)}) copy-start(bf16[1,832]{1,0:T(2,128)(2,1)} %param.37) | copy-start | bytes 4996
  376.0 114.5 %copy-start.252 = (bf16[1,12]{1,0:T(2,128)(2,1)S(1)}, bf16[1,12]{1,0:T(2,128)(2,1)}, u32[]{:S(2)}) copy-start(bf16[1,12]{1,0:T(2,128)(2,1)} %param.40) | copy-start | bytes 76
  376.0 391.3 %all-gather.14.cloned.1.call-start = ((), (), s32[]{:S(2)}) async-start(), calls=%async_computation.30 | async-start | bytes 11796480 | tf_op jit(solution)/shard_map/all_gather | solution.py:371
  376.7 141.6 %slice-start.9 = ((bf16[256,6448]{0,1:T(8,128)(2,1)}), bf16[256,256]{0,1:T(8,128)(2,1)S(1)}, s32[]{:S(2)}) async-start(bf16[256,6448]{0,1:T(8,128)(2,1)} %copy-done.54), calls=%async_computation.42 | async-start | bytes 262144 | tf_op jit(solution)/shard_map/slice | solution.py:178
  377.4 140.8 %copy-start.188 = (s32[1024]{0:T(1024)}, s32[1024]{0:T(1024)S(1)}, u32[]{:S(2)}) copy-start(s32[1024]{0:T(1024)S(1)} %convert_reduce_fusion.1) | copy-start | bytes 12292
  726.8 34.5 all-to-all-start.2
  774.1 3.2 collective-permute-start
  777.7 307.8 %copy-start = (bf16[256,1536]{1,0:T(8,128)(2,1)}, bf16[256,1536]{1,0:T(8,128)(2,1)S(1)}, u32[]{:S(2)}) copy-start(bf16[256,1536]{1,0:T(8,128)(2,1)S(1)} %get-tuple-element.2797) | copy-start | bytes 2359300
  790.7 8.9 all-to-all-start.3
  799.6 52.2 %all-to-all-start.4 = ((bf16[256,4,768]{0,2,1:T(8,128)(2,1)}), bf16[256,4,768]{0,2,1:T(8,128)(2,1)}, u32[]{:S(2)}, u32[]{:S(2)}) async-start(bf16[256,4,768]{0,2,1:T(8,128)(2,1)} %bitcast.1523), calls=%async_computation.4 | async-start | bytes 3145728 | tf_op jit(solution)/shard_map/all_to_all | solution.py:181
  1082.2 3.3 collective-permute-start.1
  1101.2 8.9 all-to-all-start.6
  1110.2 53.0 %all-to-all-start.7 = ((bf16[256,4,768]{0,2,1:T(8,128)(2,1)}), bf16[256,4,768]{0,2,1:T(8,128)(2,1)S(1)}, u32[]{:S(2)}, u32[]{:S(2)}) async-start(bf16[256,4,768]{0,2,1:T(8,128)(2,1)} %bitcast.1524), calls=%async_computation.7 | async-start | bytes 3145728 | tf_op jit(solution)/shard_map/all_to_all | solution.py:181
  1327.1 38.0 all-to-all-start.8
  1388.1 40.0 all-to-all-start.9
  1728.2 29.9 all-to-all-start.11
  1758.1 58.2 %copy-start.20 = (bf16[256,1536]{1,0:T(8,128)(2,1)S(1)}, bf16[256,1536]{1,0:T(8,128)(2,1)}, u32[]{:S(2)}) copy-start(bf16[256,1536]{1,0:T(8,128)(2,1)} %copy-done.19) | copy-start | bytes 2359300
  1758.2 81.7 %slice-start.3 = ((s8[9437184]{0:T(1024)(128)(4,1)}), s8[1048576]{0:T(1024)(128)(4,1)S(1)}, s32[]{:S(2)}) async-start(s8[9437184]{0:T(1024)(128)(4,1)} %bitcast.1485), calls=%async_computation.36 | async-start | bytes 2097152
  1758.2 58.2 %all-to-all-start.10 = ((bf16[4,256,768]{1,2,0:T(8,128)(2,1)}), bf16[4,256,768]{1,2,0:T(8,128)(2,1)}, u32[]{:S(2)}, u32[]{:S(2)}) async-start(bf16[4,256,768]{1,2,0:T(8,128)(2,1)} %bitcast.1525), calls=%async_computation.10 | async-start | bytes 3145728 | tf_op jit(solution)/shard_map/all_to_all | solution.py:276
  1763.5 50.0 %reduce-scatter.9.cloned.1.call-start = ((), (), s32[]{:S(2)}) async-start(), calls=%async_computation.24 | async-start | bytes 1310720 | tf_op jit(solution)/shard_map/reduce_scatter | solution.py:281
  1765.9 66.0 %copy-start.172 = (bf16[256,48]{0,1:T(8,128)(2,1)}, bf16[256,48]{0,1:T(8,128)(2,1)S(1)}, u32[]{:S(2)}) copy-start(bf16[256,48]{0,1:T(8,128)(2,1)S(1)} %all_to_all.231) | copy-start | bytes 73732
  1835.4 4.3 collective-permute-start.2
  1851.7 41.2 %all-to-all-start.12 = ((bf16[256,4,768]{0,2,1:T(8,128)(2,1)}), bf16[256,4,768]{0,2,1:T(8,128)(2,1)S(1)}, u32[]{:S(2)}, u32[]{:S(2)}) async-start(bf16[256,4,768]{0,2,1:T(8,128)(2,1)} %bitcast.65), calls=%async_computation.13 | async-start | bytes 3145728 | tf_op jit(solution)/shard_map/all_to_all | solution.py:251
  2192.6 30.1 all-to-all-start.14
  2222.7 58.4 %copy-start.2 = (bf16[256,1536]{1,0:T(8,128)(2,1)S(1)}, bf16[256,1536]{1,0:T(8,128)(2,1)}, u32[]{:S(2)}) copy-start(bf16[256,1536]{1,0:T(8,128)(2,1)} %copy-done) | copy-start | bytes 2359300
  2222.7 58.4 %copy-start.21 = (bf16[256,1536]{1,0:T(8,128)(2,1)S(1)}, bf16[256,1536]{1,0:T(8,128)(2,1)}, u32[]{:S(2)}) copy-start(bf16[256,1536]{1,0:T(8,128)(2,1)} %copy-done.19) | copy-start | bytes 2359300
  2222.7 58.4 %copy-start.115 = (f32[1536]{0:T(1024)S(1)}, f32[1536]{0:T(1024)}, u32[]{:S(2)}) copy-start(f32[1536]{0:T(1024)} %copy-done.111) | copy-start | bytes 18436
  2222.7 81.9 %slice-start.6 = ((s8[9437184]{0:T(1024)(128)(4,1)}), s8[1048576]{0:T(1024)(128)(4,1)S(1)}, s32[]{:S(2)}) async-start(s8[9437184]{0:T(1024)(128)(4,1)} %bitcast.1487), calls=%async_computation.39 | async-start | bytes 2097152
  2222.7 58.4 %all-to-all-start.13 = ((bf16[4,256,768]{1,2,0:T(8,128)(2,1)}), bf16[4,256,768]{1,2,0:T(8,128)(2,1)}, u32[]{:S(2)}, u32[]{:S(2)}) async-start(bf16[4,256,768]{1,2,0:T(8,128)(2,1)} %bitcast.1526), calls=%async_computation.14 | async-start | bytes 3145728 | tf_op jit(solution)/shard_map/all_to_all | solution.py:276
  2228.0 50.2 %reduce-scatter.11.cloned.1.call-start = ((), (), s32[]{:S(2)}) async-start(), calls=%async_computation.25 | async-start | bytes 1310720 | tf_op jit(solution)/shard_map/reduce_scatter | solution.py:281
  2230.4 66.3 %copy-start.174 = (bf16[256,48]{0,1:T(8,128)(2,1)}, bf16[256,48]{0,1:T(8,128)(2,1)S(1)}, u32[]{:S(2)}) copy-start(bf16[256,48]{0,1:T(8,128)(2,1)S(1)} %all_to_all.241) | copy-start | bytes 73732
  2300.5 4.2 collective-permute-start.3
  2313.3 42.2 %all-to-all-start.15 = ((bf16[256,4,768]{0,2,1:T(8,128)(2,1)}), bf16[256,4,768]{0,2,1:T(8,128)(2,1)}, u32[]{:S(2)}, u32[]{:S(2)}) async-start(bf16[256,4,768]{0,2,1:T(8,128)(2,1)} %bitcast.1539), calls=%async_computation.17 | async-start | bytes 3145728 | tf_op jit(solution)/shard_map/all_to_all | solution.py:251
  2317.9 455.3 %reduce-scatter.13.cloned.1.call-start = ((), (), s32[]{:S(2)}) async-start(), calls=%async_computation.26 | async-start | bytes 1310720 | tf_op jit(solution)/shard_map/reduce_scatter | solution.py:281
  2683.1 373.4 %reduce-scatter.17.cloned.1.call-start = ((), (), s32[]{:S(2)}) async-start(), calls=%async_computation.28 | async-start | bytes 23592960 | tf_op jit(solution)/shard_map/reduce_scatter | solution.py:455
  2718.9 11.0 all-to-all-start.17
  2729.9 82.9 %all-to-all-start.16 = ((bf16[4,256,768]{1,2,0:T(8,128)(2,1)}), bf16[4,256,768]{1,2,0:T(8,128)(2,1)}, u32[]{:S(2)}, u32[]{:S(2)}) async-start(bf16[4,256,768]{1,2,0:T(8,128)(2,1)} %bitcast.1527), calls=%async_computation.18 | async-start | bytes 3145728 | tf_op jit(solution)/shard_map/all_to_all | solution.py:276
  2734.5 978.6 %reduce-scatter.15.cloned.1.call-start = ((), (), s32[]{:S(2)}) async-start(), calls=%async_computation.27 | async-start | bytes 49520640 | tf_op jit(solution)/shard_map/reduce_scatter | solution.py:448
  2855.3 900.0 %reduce-scatter.19.cloned.1.call-start = ((), (), s32[]{:S(2)}) async-start(), calls=%async_computation.31 | async-start | bytes 2129920
  2858.0 1174.9 %all-reduce.88.cloned.1.call-start = ((), (), s32[]{:S(2)}) async-start(), calls=%async_computation.32 | async-start | bytes 29245440 | tf_op jit(solution)/shard_map/psum | solution.py:457
  (321 other events, 2819.5 us)
Sparse Core Ops, SparseCore 0:
  9.6 340.5 all-gather.11
  378.4 222.2 all-gather.13
  1767.2 46.2 reduce-scatter.8
  2231.5 46.7 reduce-scatter.10
  2683.2 26.1 reduce-scatter.12
  2717.1 339.3 reduce-scatter.16
  3058.9 654.0 reduce-scatter.14
  3715.9 39.4 reduce-scatter.18
  3759.1 273.7 all-reduce.87
where the time goes:
time: 4080 us; the launch traced here: 4050 us
  waiting for transfers between devices  1680 us (41%)
  local copies, waits for them, and re-layouts  917 us (22%)
  matrix products  594 us (15%)
  other arithmetic  369 us (9%)
  blocking collectives  363 us (9%)
  starting transfers between devices  74.9 us (2%)
    reduce_scatter x1, waiting for transfers between devices, local(): lax.psum_scatter(grad_totals[1], 'seq', scatter_dimension=0, tiled=True)  657 us
    dynamic_update_slice x108, local copies, waits for them, and re-layouts, ssd_scan(): _, outputs = lax.scan(jax.checkpoint(advance), initial, inputs)  500 us
    all_gather x1, waiting for transfers between devices, local(): lax.all_gather(in_weight[0], 'seq', axis=0, tiled=True)  328 us
    psum x1, waiting for transfers between devices, local(): lax.psum((reduced[0], reduced[1], reduced[2], reduced[3], reduced[4], red...  221 us
    reduce_scatter x1, waiting for transfers between devices, local(): lax.psum_scatter(grad_totals[8], 'seq', scatter_dimension=0, tiled=True)  198 us
    dot_general x36, matrix products, advance(): jnp.einsum('ijh,jhp->ihp', mix_weights, block_vals, precision=HIGHEST)  164 us
    all_gather x3, blocking collectives, forward_layer(): shared_bc = lax.all_gather(proj_bc, 'seq', axis=0, tiled=True)  117 us
    all_gather x1, blocking collectives, local(): lax.all_gather(conv_weight[0], 'seq', axis=1, tiled=True)  106 us
  transfers between devices with their start and end apart: 30, of which 22 were waited for; matrix products, arithmetic and copies ran while one was open for 12% of the time, Pallas kernels for 0%

commit v1 on v0

v1 whole, which is shorter than its diff:
```python
import functools

import jax
import jax.numpy as jnp
from jax import lax
from jax.experimental import pallas as pl
from jax.experimental.pallas import tpu as pltpu
from jax.sharding import PartitionSpec as P

SPAN = 256
HEAD = 64
STATE = 128
TAPS = 4
EPSILON = 1e-05
HIGHEST = lax.Precision.HIGHEST
F32 = jnp.float32
BF16 = jnp.bfloat16
FAR = -1e30


def mm(a, b):
    return jnp.dot(a, b, preferred_element_type=F32)


def mm_nt(a, b):
    return lax.dot_general(a, b, (((1,), (1,)), ((), ())), preferred_element_type=F32)


def mm_tn(a, b):
    return lax.dot_general(a, b, (((0,), (0,)), ((), ())), preferred_element_type=F32)


def exact(a, b):
    return lax.dot_general(
        a, b, (((1,), (0,)), ((), ())), precision=HIGHEST, preferred_element_type=F32
    )


def doc_of(starts_ref, position):
    total = jnp.zeros(position.shape, jnp.int32)
    for entry in range(starts_ref.shape[0]):
        total = total + (starts_ref[entry] <= position).astype(jnp.int32)
    return total


def tiles_of(width):
    return [(low, min(low + 128, width)) for low in range(0, width, 128)]


def spread_pair(columns, tile, width):
    rows = columns.shape[0]
    first = jnp.broadcast_to(columns[:, 2 * tile : 2 * tile + 1], (rows, width))
    if width <= HEAD:
        return first
    second = jnp.broadcast_to(columns[:, 2 * tile + 1 : 2 * tile + 2], (rows, width))
    lane = lax.broadcasted_iota(jnp.int32, (rows, width), 1)
    return jnp.where(lane < HEAD, first, second)


def block_facts(starts_ref, block, length):
    base = block * SPAN
    column = base + lax.broadcasted_iota(jnp.int32, (SPAN, 128), 0)
    doc_col = doc_of(starts_ref, column)
    before = []
    for lag in range(1, TAPS):
        same = (doc_of(starts_ref, column - lag) == doc_col) & (column >= lag)
        before.append(same.astype(F32))
    row = base + lax.broadcasted_iota(jnp.int32, (8, SPAN), 1)
    doc_row = doc_of(starts_ref, row)
    same_square = doc_col[:, 0:1] == doc_row[0:1, :]
    edge_before = jnp.full((8, 128), base - 1, jnp.int32)
    last_doc_before = doc_of(starts_ref, edge_before)[0:1, :]
    last_doc = doc_of(starts_ref, jnp.full((8, 128), base + SPAN - 1, jnp.int32))[0:1, :]
    carried = ((doc_col == last_doc_before) & (base > 0)).astype(F32)
    to_last = (doc_col == last_doc).astype(F32)
    return doc_col, column, before, same_square, carried, to_last


def taps_sum(ext_ref, low, high, before, kernel, bias):
    summed = ext_ref[pl.ds(8, SPAN), low:high] * kernel[TAPS - 1 : TAPS, low:high] + bias[0:1, low:high]
    for lag in range(1, TAPS):
        summed = summed + (
            ext_ref[pl.ds(8 - lag, SPAN), low:high]
            * before[lag - 1][:, : high - low]
            * kernel[TAPS - 1 - lag : TAPS - lag, low:high]
        )
    return summed


def sigmoid(value):
    return 1.0 / (1.0 + jnp.exp(-value))


def softplus(value):
    small = jnp.exp(-jnp.abs(value))
    series = small * (1.0 - small * (0.5 - small * (1.0 / 3.0)))
    return jnp.maximum(value, 0.0) + jnp.where(small < 0.01, series, jnp.log(1.0 + small))


def lower_ones():
    row = lax.broadcasted_iota(jnp.int32, (SPAN, SPAN), 0)
    col = lax.broadcasted_iota(jnp.int32, (SPAN, SPAN), 1)
    return row, col


def forward_kernel(
    with_back,
    length,
    starts_ref,
    normed_ref,
    wg_ref,
    wx_ref,
    wbc_ref,
    wdt_ref,
    kx_ref,
    kbc_ref,
    heads_ref,
    gain_ref,
    wo_ref,
    *rest,
):
    if with_back:
        dh_ref, rest = rest[0], rest[1:]
    (
        gate_ref,
        x_ref,
        bc_ref,
        dt_ref,
        scan_ref,
        state_ref,
        part_ref,
        stat_ref,
        ext_x,
        ext_bc,
        memory,
        gu_ref,
        y_ref,
    ) = rest
    block = pl.program_id(0)
    inner = wx_ref.shape[1]

    @pl.when(block == 0)
    def _():
        ext_x[...] = jnp.zeros_like(ext_x)
        ext_bc[...] = jnp.zeros_like(ext_bc)
        memory[...] = jnp.zeros_like(memory)

    @pl.when(block > 0)
    def _():
        ext_x[0:8, :] = ext_x[SPAN : SPAN + 8, :]
        ext_bc[0:8, :] = ext_bc[SPAN : SPAN + 8, :]

    normed = normed_ref[...]
    bc_low = mm(normed, wbc_ref[...]).astype(BF16)
    bc_ref[...] = bc_low
    ext_bc[8 : SPAN + 8, :] = bc_low.astype(F32)
    dt_low = mm(normed, wdt_ref[...]).astype(BF16).astype(F32)
    dt_ref[...] = dt_low
    x_low = mm(normed, wx_ref[...]).astype(BF16)
    x_ref[...] = x_low
    ext_x[8 : SPAN + 8, :] = x_low.astype(F32)
    gate_low = mm(normed, wg_ref[...]).astype(BF16)
    gate_ref[...] = gate_low

    _, _, before, same_square, carried, to_last = block_facts(starts_ref, block, length)
    row, col = lower_ones()
    lower = (row >= col).astype(F32)
    keep = jnp.where(same_square & (row >= col), 0.0, FAR)

    delta = softplus(dt_low + heads_ref[0:1, :])
    rate = -jnp.exp(heads_ref[1:2, :]) * delta
    total = exact(lower, rate)
    total_rows = jnp.transpose(total)
    grown = carried * jnp.exp(total)
    last_total = total[SPAN - 1 : SPAN, :]
    ending = to_last * jnp.exp(last_total - total)
    carry_last = grown[SPAN - 1 : SPAN, :]

    kbc = kbc_ref[...]
    b_conv = taps_sum(ext_bc, 0, STATE, before, kbc, kbc[TAPS : TAPS + 1])
    c_conv = taps_sum(ext_bc, STATE, 2 * STATE, before, kbc, kbc[TAPS : TAPS + 1])
    b_low = (b_conv * sigmoid(b_conv)).astype(BF16)
    c_low = (c_conv * sigmoid(c_conv)).astype(BF16)
    scores = mm_nt(c_low, b_low)
    b_flip = jnp.transpose(b_low.astype(F32)).astype(BF16)

    state_ref[0] = memory[...].astype(BF16)
    kx = kx_ref[...]
    squares = jnp.zeros((SPAN, 128), F32)
    for tile, (low, high) in enumerate(tiles_of(inner)):
        width = high - low
        lane = lax.broadcasted_iota(jnp.int32, (SPAN, width), 1)
        conv = taps_sum(ext_x, low, high, before, kx, kx[TAPS : TAPS + 1])
        values = conv * sigmoid(conv)
        weighted = spread_pair(delta, tile, width) * values
        w_low = weighted.astype(BF16)
        mixed = None
        for half in range(width // HEAD):
            head = 2 * tile + half
            decay = jnp.exp(total[:, head : head + 1] - total_rows[head : head + 1, :] + keep)
            part = mm((scores * decay).astype(BF16), w_low)
            mixed = part if mixed is None else jnp.where(lane < HEAD, mixed, part)
        mem = memory[:, low:high]
        mixed = mixed + mm(c_low, mem.astype(BF16)) * spread_pair(grown, tile, width)
        scan_ref[:, low:high] = mixed
        fresh = mm(b_flip, (weighted * spread_pair(ending, tile, width)).astype(BF16))
        memory[:, low:high] = mem * spread_pair(carry_last, tile, width) + fresh
        mixed = (
            (mixed + spread_pair(heads_ref[2:3, :], tile, width) * values).astype(BF16).astype(F32)
        )
        gate = gate_ref[:, low:high].astype(F32)
        g = mixed * (gate * sigmoid(gate))
        if width == 128:
            squares = squares + g * g
        else:
            squares = squares + jnp.concatenate([g * g, jnp.zeros((SPAN, 128 - width), F32)], axis=1)
        gu_ref[:, low:high] = (g * gain_ref[0:1, low:high]).astype(BF16)

    stats = jnp.sum(squares, axis=1, keepdims=True)
    gu = gu_ref[...]
    part_ref[...] = mm(gu, wo_ref[...]).astype(BF16)
    if with_back:
        dgated = mm_nt(dh_ref[...], wo_ref[...])
        along = jnp.sum(dgated * gu.astype(F32), axis=1, keepdims=True)
        lane = lax.broadcasted_iota(jnp.int32, (SPAN, 128), 1)
        both = jnp.where(lane == 0, stats, jnp.where(lane == 1, along, 0.0))
    else:
        both = jnp.broadcast_to(stats, (SPAN, 128))
    stat_ref[...] = jnp.transpose(both)[0:8, :]


def backward_kernel(
    length,
    starts_ref,
    dh_ref,
    stat_ref,
    wg_ref,
    wx_ref,
    wbc_ref,
    wdt_ref,
    kx_ref,
    kbc_ref,
    heads_ref,
    gain_ref,
    wo_ref,
    gate_ref,
    x_ref,
    xh_ref,
    bc_ref,
    bch_ref,
    dt_ref,
    scan_ref,
    state_ref,
    dgate_ref,
    dx_ref,
    dbc_ref,
    ddt_ref,
    gated_ref,
    dnormed_ref,
    gx_ref,
    gbc_ref,
    gheads_ref,
    ext_x,
    ext_bc,
    ext_dx,
    ext_dbc,
    dmemory,
    dscore,
):
    blocks = pl.num_programs(0)
    block = blocks - 1 - pl.program_id(0)
    inner = wx_ref.shape[1]

    @pl.when(pl.program_id(0) == 0)
    def _():
        ext_dx[...] = jnp.zeros_like(ext_dx)
        ext_dbc[...] = jnp.zeros_like(ext_dbc)
        dmemory[...] = jnp.zeros_like(dmemory)
        gx_ref[...] = jnp.zeros_like(gx_ref)
        gbc_ref[...] = jnp.zeros_like(gbc_ref)
        gheads_ref[...] = jnp.zeros_like(gheads_ref)

    @pl.when(pl.program_id(0) > 0)
    def _():
        ext_dx[SPAN : SPAN + 8, :] = ext_dx[0:8, :]
        ext_dbc[SPAN : SPAN + 8, :] = ext_dbc[0:8, :]

    ext_x[0:8, :] = xh_ref[8:16, :].astype(F32)
    ext_x[8 : SPAN + 8, :] = x_ref[...].astype(F32)
    ext_bc[0:8, :] = bch_ref[8:16, :].astype(F32)
    ext_bc[8 : SPAN + 8, :] = bc_ref[...].astype(F32)

    doc_col, column, before, same_square, carried, to_last = block_facts(starts_ref, block, length)
    after = []
    for lag in range(1, TAPS):
        same = (doc_of(starts_ref, column + lag) == doc_col) & (column + lag < length)
        after.append(same.astype(F32))
    row, col = lower_ones()
    lower = (row >= col).astype(F32)
    upper = (row <= col).astype(F32)
    keep = jnp.where(same_square & (row <= col), 0.0, FAR)

    dt = dt_ref[...] + heads_ref[0:1, :]
    delta = softplus(dt)
    slope = -jnp.exp(heads_ref[1:2, :])
    rate = slope * delta
    total = exact(lower, rate)
    total_rows = jnp.transpose(total)
    grown = carried * jnp.exp(total)
    last_total = total[SPAN - 1 : SPAN, :]
    ending = to_last * jnp.exp(last_total - total)
    carry_last = grown[SPAN - 1 : SPAN, :]

    kbc = kbc_ref[...]
    b_conv = taps_sum(ext_bc, 0, STATE, before, kbc, kbc[TAPS : TAPS + 1])
    c_conv = taps_sum(ext_bc, STATE, 2 * STATE, before, kbc, kbc[TAPS : TAPS + 1])
    b_sig = sigmoid(b_conv)
    c_sig = sigmoid(c_conv)
    b_low = (b_conv * b_sig).astype(BF16)
    c_low = (c_conv * c_sig).astype(BF16)
    scores = mm_nt(b_low, c_low)
    c_flip = jnp.transpose(c_low.astype(F32)).astype(BF16)

    stat_cols = jnp.transpose(jnp.broadcast_to(stat_ref[0:1, :], (128, SPAN)))
    mean_cols = jnp.transpose(jnp.broadcast_to(stat_ref[1:2, :], (128, SPAN)))
    dgated = mm_nt(dh_ref[...], wo_ref[...])
    dscore[...] = jnp.zeros_like(dscore)
    kx = kx_ref[...]
    db = jnp.zeros((SPAN, STATE), F32)
    dc = jnp.zeros((SPAN, STATE), F32)
    dtotal = jnp.zeros((SPAN, 128), F32)
    ddelta = jnp.zeros((SPAN, 128), F32)
    dlast = jnp.zeros((8, 128), F32)
    for tile, (low, high) in enumerate(tiles_of(inner)):
        width = high - low
        lane = lax.broadcasted_iota(jnp.int32, (SPAN, width), 1)
        picker = (
            lax.broadcasted_iota(jnp.int32, (width, 128), 1)
            == 2 * tile + lax.broadcasted_iota(jnp.int32, (width, 128), 0) // HEAD
        ).astype(F32)
        skip = spread_pair(heads_ref[2:3, :], tile, width)
        conv = taps_sum(ext_x, low, high, before, kx, kx[TAPS : TAPS + 1])
        sig = sigmoid(conv)
        values = conv * sig
        delta_t = spread_pair(delta, tile, width)
        weighted = delta_t * values
        w_low = weighted.astype(BF16)
        scanned = scan_ref[:, low:high]
        mixed = (scanned + skip * values).astype(BF16).astype(F32)
        gate = gate_ref[:, low:high].astype(F32)
        gate_sig = sigmoid(gate)
        silu = gate * gate_sig
        g = mixed * silu
        scale = stat_cols[:, :width]
        n = g * scale
        gain = gain_ref[0:1, low:high]
        dgated_t = dgated[:, low:high]
        gated_ref[:, low:high] = (n * gain).astype(BF16)
        dg = scale * (dgated_t * gain - n * mean_cols[:, :width])
        dgate_ref[:, low:high] = (
            dg * mixed * (gate_sig * (1.0 + gate * (1.0 - gate_sig)))
        ).astype(BF16)
        dy_low = (dg * silu).astype(BF16)
        dy = dy_low.astype(F32)
        grad_w = None
        for half in range(width // HEAD):
            head = 2 * tile + half
            decay = jnp.exp(total_rows[head : head + 1, :] - total[:, head : head + 1] + keep)
            mine = (lane // HEAD) == half
            pairs = mm_nt(jnp.where(mine, w_low, jnp.zeros_like(w_low)), dy_low)
            dscore[...] += decay * pairs
            part = mm((scores * decay).astype(BF16), dy_low)
            grad_w = part if grad_w is None else jnp.where(lane < HEAD, grad_w, part)
        dmem = dmemory[:, low:high]
        dmem_low = dmem.astype(BF16)
        mem_low = state_ref[0, :, low:high]
        ending_t = spread_pair(ending, tile, width)
        from_state = mm(b_low, dmem_low) * ending_t
        grad_w = grad_w + from_state
        db = db + mm_nt((weighted * ending_t).astype(BF16), dmem_low)
        dy_grown = (dy * spread_pair(grown, tile, width)).astype(BF16)
        dc = dc + mm_nt(dy_grown, mem_low)
        carry_t = spread_pair(carry_last, tile, width)
        w_round = w_low.astype(F32)
        at_last = jnp.sum(w_round * from_state, axis=0, keepdims=True) + jnp.sum(
            dmem * mem_low.astype(F32) * carry_t, axis=0, keepdims=True
        )
        dlast = dlast + exact(jnp.broadcast_to(at_last, (8, width)), picker)
        dmemory[:, low:high] = dmem * carry_t + mm(c_flip, dy_grown)
        dtotal = dtotal + exact(dy * scanned - w_round * grad_w, picker)
        ddelta = ddelta + exact(values * grad_w, picker)
        dconv = (delta_t * grad_w + skip * dy) * (sig * (1.0 + conv * (1.0 - sig)))
        ext_dx[0:SPAN, low:high] = dconv
        sums = [jnp.sum(dconv * ext_x[pl.ds(8, SPAN), low:high], axis=0, keepdims=True)]
        for lag in range(1, TAPS):
            sums.append(
                jnp.sum(
                    dconv * before[lag - 1][:, :width] * ext_x[pl.ds(8 - lag, SPAN), low:high],
                    axis=0,
                    keepdims=True,
                )
            )
        sums = sums[::-1] + [
            jnp.sum(dconv, axis=0, keepdims=True),
            jnp.sum(dy * values, axis=0, keepdims=True),
            jnp.sum(dgated_t * n, axis=0, keepdims=True),
            jnp.zeros((1, width), F32),
        ]
        gx_ref[:, low:high] += jnp.concatenate(sums, axis=0)
        back = ext_dx[0:SPAN, low:high] * kx[TAPS - 1 : TAPS, low:high]
        for lag in range(1, TAPS):
            back = back + (
                ext_dx[pl.ds(lag, SPAN), low:high]
                * after[lag - 1][:, :width]
                * kx[TAPS - 1 - lag : TAPS - lag, low:high]
            )
        dx_ref[:, low:high] = back.astype(BF16)

    score_grad = dscore[...]
    db = db + mm(score_grad.astype(BF16), c_low)
    dc = dc + mm(jnp.transpose(score_grad).astype(BF16), b_low)
    for part, (conv, sig, grad) in enumerate(((b_conv, b_sig, db), (c_conv, c_sig, dc))):
        low, high = part * STATE, (part + 1) * STATE
        dconv = grad * (sig * (1.0 + conv * (1.0 - sig)))
        ext_dbc[0:SPAN, low:high] = dconv
        sums = [jnp.sum(dconv * ext_bc[pl.ds(8, SPAN), low:high], axis=0, keepdims=True)]
        for lag in range(1, TAPS):
            sums.append(
                jnp.sum(
                    dconv * before[lag - 1] * ext_bc[pl.ds(8 - lag, SPAN), low:high],
                    axis=0,
                    keepdims=True,
                )
            )
        sums = sums[::-1] + [jnp.sum(dconv, axis=0, keepdims=True), jnp.zeros((3, STATE), F32)]
        gbc_ref[:, low:high] += jnp.concatenate(sums, axis=0)
        back = dconv * kbc[TAPS - 1 : TAPS, low:high]
        for lag in range(1, TAPS):
            back = back + (
                ext_dbc[pl.ds(lag, SPAN), low:high]
                * after[lag - 1]
                * kbc[TAPS - 1 - lag : TAPS - lag, low:high]
            )
        dbc_ref[:, low:high] = back.astype(BF16)

    drate = exact(upper, dtotal) + dlast[0:1, :]
    ddt = (ddelta + slope * drate) * sigmoid(dt)
    ddt_low = ddt.astype(BF16)
    ddt_ref[...] = ddt_low
    gheads_ref[...] += jnp.concatenate(
        [
            jnp.sum(ddt, axis=0, keepdims=True),
            jnp.sum(drate * rate, axis=0, keepdims=True),
            jnp.zeros((6, 128), F32),
        ],
        axis=0,
    )
    dnormed_ref[...] = (
        mm_nt(dgate_ref[...], wg_ref[...])
        + mm_nt(dx_ref[...], wx_ref[...])
        + mm_nt(dbc_ref[...], wbc_ref[...])
        + mm_nt(ddt_low, wdt_ref[...])
    ).astype(BF16)


def whole(array):
    return pl.BlockSpec(array.shape, lambda i: (0,) * array.ndim, pipeline_mode=pl.Buffered(1))


def cost(length, width, inner, passes):
    flops = 2 * length * width * (3 * inner + 384) * passes
    return pl.CostEstimate(flops=flops, bytes_accessed=length * width * 16, transcendentals=0)


VMEM_LIMIT = 48 * 2**20


def run_forward(starts, normed, weights, dh=None):
    wg, wx, wbc, wdt, kx, kbc, heads, gain, wo = weights
    length, width = normed.shape
    inner = wx.shape[1]
    blocks = length // SPAN
    rows = lambda cols: pl.BlockSpec((SPAN, cols), lambda i: (i, 0))
    operands = [starts, normed, wg, wx, wbc, wdt, kx, kbc, heads, gain, wo]
    in_specs = [pl.BlockSpec(memory_space=pltpu.SMEM), rows(width)] + [
        whole(array) for array in operands[2:]
    ]
    if dh is not None:
        operands.append(dh)
        in_specs.append(rows(width))
    out_shape = [
        jax.ShapeDtypeStruct((length, inner), BF16),
        jax.ShapeDtypeStruct((length, inner), BF16),
        jax.ShapeDtypeStruct((length, 2 * STATE), BF16),
        jax.ShapeDtypeStruct((length, 128), F32),
        jax.ShapeDtypeStruct((length, inner), F32),
        jax.ShapeDtypeStruct((blocks, STATE, inner), BF16),
        jax.ShapeDtypeStruct((length, width), BF16),
        jax.ShapeDtypeStruct((8, length), F32),
    ]
    out_specs = [
        rows(inner),
        rows(inner),
        rows(2 * STATE),
        rows(128),
        rows(inner),
        pl.BlockSpec((1, STATE, inner), lambda i: (i, 0, 0)),
        rows(width),
        pl.BlockSpec((8, SPAN), lambda i: (0, i)),
    ]
    return pl.pallas_call(
        functools.partial(forward_kernel, dh is not None, length),
        grid=(blocks,),
        in_specs=in_specs,
        out_specs=out_specs,
        out_shape=out_shape,
        scratch_shapes=[
            pltpu.VMEM((SPAN + 8, inner), F32),
            pltpu.VMEM((SPAN + 8, 2 * STATE), F32),
            pltpu.VMEM((STATE, inner), F32),
            pltpu.VMEM((SPAN, inner), BF16),
            pltpu.VMEM((SPAN, inner), F32),
        ],
        compiler_params=pltpu.CompilerParams(
            dimension_semantics=("arbitrary",), vmem_limit_bytes=VMEM_LIMIT
        ),
        cost_estimate=cost(length, width, inner, 1),
        name="layer_forward",
    )(*operands)


def run_backward(starts, dh, stats, weights, saved):
    wg, wx, wbc, wdt, kx, kbc, heads, gain, wo = weights
    gate, x, bc, dt, scanned, states = saved
    length, width = dh.shape
    inner = wx.shape[1]
    blocks = length // SPAN
    rows = lambda cols: pl.BlockSpec((SPAN, cols), lambda i: (blocks - 1 - i, 0))
    halo = lambda cols: pl.BlockSpec(
        (16, cols), lambda i: (jnp.maximum((blocks - 1 - i) * (SPAN // 16) - 1, 0), 0)
    )
    fixed = lambda shape: pl.BlockSpec(shape, lambda i: (0,) * len(shape))
    operands = [starts, dh, stats, wg, wx, wbc, wdt, kx, kbc, heads, gain, wo]
    in_specs = [
        pl.BlockSpec(memory_space=pltpu.SMEM),
        rows(width),
        pl.BlockSpec((8, SPAN), lambda i: (0, blocks - 1 - i)),
    ] + [whole(array) for array in operands[3:]]
    operands += [gate, x, x, bc, bc, dt, scanned, states]
    in_specs += [
        rows(inner),
        rows(inner),
        halo(inner),
        rows(2 * STATE),
        halo(2 * STATE),
        rows(128),
        rows(inner),
        pl.BlockSpec((1, STATE, inner), lambda i: (blocks - 1 - i, 0, 0)),
    ]
    out_shape = [
        jax.ShapeDtypeStruct((length, inner), BF16),
        jax.ShapeDtypeStruct((length, inner), BF16),
        jax.ShapeDtypeStruct((length, 2 * STATE), BF16),
        jax.ShapeDtypeStruct((length, 128), BF16),
        jax.ShapeDtypeStruct((length, inner), BF16),
        jax.ShapeDtypeStruct((length, width), BF16),
        jax.ShapeDtypeStruct((8, inner), F32),
        jax.ShapeDtypeStruct((8, 2 * STATE), F32),
        jax.ShapeDtypeStruct((8, 128), F32),
    ]
    out_specs = [
        rows(inner),
        rows(inner),
        rows(2 * STATE),
        rows(128),
        rows(inner),
        rows(width),
        fixed((8, inner)),
        fixed((8, 2 * STATE)),
        fixed((8, 128)),
    ]
    return pl.pallas_call(
        functools.partial(backward_kernel, length),
        grid=(blocks,),
        in_specs=in_specs,
        out_specs=out_specs,
        out_shape=out_shape,
        scratch_shapes=[
            pltpu.VMEM((SPAN + 8, inner), F32),
            pltpu.VMEM((SPAN + 8, 2 * STATE), F32),
            pltpu.VMEM((SPAN + 8, inner), F32),
            pltpu.VMEM((SPAN + 8, 2 * STATE), F32),
            pltpu.VMEM((STATE, inner), F32),
            pltpu.VMEM((SPAN, SPAN), F32),
        ],
        compiler_params=pltpu.CompilerParams(
            dimension_semantics=("arbitrary",), vmem_limit_bytes=VMEM_LIMIT
        ),
        cost_estimate=cost(length, width, inner, 2),
        name="layer_backward",
    )(*operands)


def norm_rows(rows_in, gain_vec):
    return (
        rows_in
        * lax.rsqrt(jnp.mean(rows_in * rows_in, axis=-1, keepdims=True) + EPSILON)
        * gain_vec
    )


def norm_back(rows_in, gain_vec, grad):
    inverse = lax.rsqrt(jnp.mean(rows_in * rows_in, axis=-1, keepdims=True) + EPSILON)
    unit = rows_in * inverse
    scaled = grad * gain_vec
    back = inverse * (scaled - unit * jnp.mean(scaled * unit, axis=-1, keepdims=True))
    return back, jnp.sum(grad * unit, axis=0)


def other_core(array):
    return lax.ppermute(array, "section", [(0, 1), (1, 0)])


def both_layers(array):
    core = lax.axis_index("section")
    theirs = other_core(array)
    return (
        jnp.where(core == 0, array, theirs),
        jnp.where(core == 0, theirs, array),
    )


def layer_weights(in_weight, conv_weight, conv_bias, step_bias, decay_log, skip_gain, gate_gain, out_weight, norm_gain):
    count = lax.axis_size("seq")
    rank = lax.axis_index("seq")
    inner = out_weight.shape[1]
    heads = step_bias.shape[1]
    whole_inner = inner * count
    depth = in_weight.shape[1]
    rows = in_weight[0]
    gate = rows[:, :whole_inner].reshape(depth, count, inner)
    x = rows[:, whole_inner : 2 * whole_inner].reshape(depth, count, inner)
    bc = rows[:, 2 * whole_inner : 2 * whole_inner + 2 * STATE]
    dt = rows[:, 2 * whole_inner + 2 * STATE :].reshape(depth, count, heads)
    bundle = jnp.concatenate(
        [
            gate,
            x,
            jnp.broadcast_to(bc[:, None, :], (depth, count, 2 * STATE)),
            jnp.pad(dt, ((0, 0), (0, 0), (0, 128 - heads))),
        ],
        axis=2,
    ).transpose(1, 0, 2)
    mine = lax.all_to_all(bundle, "seq", split_axis=0, concat_axis=0, tiled=True)
    mine = mine.reshape(count * depth, -1)
    in_both = both_layers(mine)
    out_both = both_layers(out_weight[0])
    small = jnp.concatenate(
        [
            conv_weight[0].reshape(-1),
            conv_bias[0],
            norm_gain[0],
        ]
    )
    gathered = lax.all_gather(small, "seq", axis=0)
    part = conv_bias.shape[1]
    kernel = gathered[:, : TAPS * part].reshape(count, TAPS, part).transpose(1, 0, 2).reshape(TAPS, -1)
    bias = gathered[:, TAPS * part : (TAPS + 1) * part].reshape(-1)
    gain = gathered[:, (TAPS + 1) * part :].reshape(-1)
    taps = jnp.concatenate([kernel, bias[None], jnp.zeros((3, bias.shape[0]), BF16)], axis=0)
    own = jnp.concatenate([step_bias, decay_log, skip_gain], axis=0)
    own = jnp.pad(own, ((0, 5), (0, 128 - heads)))
    packed = [
        lax.dynamic_slice_in_dim(taps, rank * inner, inner, 1).astype(F32),
        taps[:, whole_inner:].astype(F32),
        own.astype(F32),
        jnp.broadcast_to(gate_gain, (8, inner)).astype(F32),
        jnp.broadcast_to(gain[None], (8, gain.shape[0])).astype(F32),
    ]
    shared = [both_layers(array) for array in packed]
    layers = []
    for layer in range(2):
        w = in_both[layer]
        kx, kbc, head_rows, gain_rows, norm_gain_rows = (pair[layer] for pair in shared)
        layers.append(
            (
                (
                    w[:, :inner],
                    w[:, inner : 2 * inner],
                    w[:, 2 * inner : 2 * inner + 2 * STATE],
                    w[:, 2 * inner + 2 * STATE :],
                    kx,
                    kbc,
                    head_rows,
                    gain_rows,
                    out_both[layer],
                ),
                norm_gain_rows[0],
            )
        )
    return layers


def local(
    hidden_in,
    doc_starts,
    cotangent,
    norm_gain,
    in_weight,
    conv_weight,
    conv_bias,
    step_bias,
    decay_log,
    skip_gain,
    gate_gain,
    out_weight,
):
    core = lax.axis_index("section")
    rank = lax.axis_index("seq")
    count = lax.axis_size("seq")
    inner = out_weight.shape[1]
    heads = step_bias.shape[1]
    whole_inner = inner * count
    layers = layer_weights(
        in_weight, conv_weight, conv_bias, step_bias, decay_log, skip_gain, gate_gain, out_weight, norm_gain
    )
    stream = lax.dynamic_index_in_dim(hidden_in, core, 0, keepdims=False).astype(F32)
    outer = lax.dynamic_index_in_dim(cotangent, core, 0, keepdims=False)
    starts = lax.dynamic_index_in_dim(doc_starts, core, 0, keepdims=False)
    tokens = stream.shape[0]

    gather = lambda array: lax.all_gather(array, "seq", axis=0, tiled=True)
    scatter = lambda array: lax.psum_scatter(array, "seq", scatter_dimension=0, tiled=True)
    own_tokens = lambda row: lax.dynamic_slice_in_dim(row, rank * tokens, tokens, 0)

    dh_whole = gather(outer)
    normed_0 = gather(norm_rows(stream, layers[0][1]).astype(BF16))
    fwd_0 = run_forward(starts, normed_0, layers[0][0])
    square_0 = lax.psum(fwd_0[7][0], "seq")
    scale_0 = lax.rsqrt(square_0 / whole_inner + EPSILON)
    product_0 = scatter(fwd_0[6]).astype(F32) * own_tokens(scale_0)[:, None]
    hidden_1 = (stream + product_0).astype(BF16)
    stream_1 = hidden_1.astype(F32)
    normed_1 = gather(norm_rows(stream_1, layers[1][1]).astype(BF16))
    fwd_1 = run_forward(starts, normed_1, layers[1][0], dh_whole)
    sums_1 = lax.psum(fwd_1[7][:2], "seq")
    scale_1 = lax.rsqrt(sums_1[0] / whole_inner + EPSILON)
    stats_1 = jnp.concatenate(
        [scale_1[None], (sums_1[1] * scale_1 / whole_inner)[None], jnp.zeros((6, scale_1.shape[0]), F32)]
    )
    hidden_2 = (
        stream_1 + scatter(fwd_1[6]).astype(F32) * own_tokens(scale_1)[:, None]
    ).astype(BF16)

    def weight_grads(normed, dh, back):
        return (
            jnp.concatenate([mm_tn(normed, part) for part in back[:4]], axis=1).astype(BF16),
            mm_tn(back[4], dh).astype(BF16),
        )

    back_1 = run_backward(starts, dh_whole, stats_1, layers[1][0], fwd_1[:6])
    dnormed_1 = scatter(back_1[5]).astype(F32)
    through_1, gain_grad_1 = norm_back(stream_1, layers[1][1], dnormed_1)
    input_grad_1 = outer.astype(F32) + through_1
    dh_low = input_grad_1.astype(BF16)
    mean_0 = jnp.sum(dh_low.astype(F32) * product_0, axis=1) / whole_inner
    dh_0 = gather(dh_low)
    means_0 = gather(mean_0)
    stats_0 = jnp.concatenate([scale_0[None], means_0[None], jnp.zeros((6, scale_0.shape[0]), F32)])
    back_0 = run_backward(starts, dh_0, stats_0, layers[0][0], fwd_0[:6])
    dnormed_0 = scatter(back_0[5]).astype(F32)
    through_0, gain_grad_0 = norm_back(stream, layers[0][1], dnormed_0)
    input_grad_0 = dh_low.astype(F32) + through_0

    grads_1 = weight_grads(normed_1, dh_whole, back_1)
    grads_0 = weight_grads(normed_0, dh_0, back_0)

    def to_core(pair):
        theirs = other_core(jnp.where(core == 0, pair[1], pair[0]))
        return jnp.where(core == 0, pair[0], pair[1]).astype(F32) + theirs.astype(F32)

    in_grad = to_core((grads_0[0], grads_1[0])).astype(BF16)
    out_grad = to_core((grads_0[1], grads_1[1])).astype(BF16)
    depth = in_weight.shape[1]
    in_grad = lax.all_to_all(
        in_grad.reshape(count, depth, -1), "seq", split_axis=0, concat_axis=0, tiled=True
    )
    in_grad = lax.psum(in_grad, "dp")
    out_grad = lax.psum(out_grad, "dp")
    in_grad = in_grad.astype(F32)
    grad_in_weight = jnp.concatenate(
        [
            in_grad[:, :, :inner].transpose(1, 0, 2).reshape(depth, whole_inner),
            in_grad[:, :, inner : 2 * inner].transpose(1, 0, 2).reshape(depth, whole_inner),
            jnp.sum(in_grad[:, :, 2 * inner : 2 * inner + 2 * STATE], axis=0),
            in_grad[:, :, 2 * inner + 2 * STATE : 2 * inner + 2 * STATE + heads]
            .transpose(1, 0, 2)
            .reshape(depth, heads * count),
        ],
        axis=1,
    )

    def small(back, gain_grad):
        gx, gbc, gheads = back[6:9]
        channels = jnp.concatenate(
            [
                lax.dynamic_update_slice_in_dim(
                    jnp.zeros((TAPS + 1, whole_inner), F32), gx[: TAPS + 1], rank * inner, 1
                ),
                gbc[: TAPS + 1],
            ],
            axis=1,
        )
        own = jnp.concatenate(
            [
                gheads[0, :heads],
                gheads[1, :heads],
                jnp.sum(gx[TAPS + 1].reshape(heads, HEAD), axis=1),
                gx[TAPS + 2],
            ]
        )
        return channels, gain_grad, own

    channels, norm_grad, own = (
        to_core(pair)
        for pair in zip(small(back_0, gain_grad_0), small(back_1, gain_grad_1))
    )
    channels, norm_grad = lax.psum((channels, norm_grad), ("dp", "seq"))
    own = lax.psum(own, "dp")
    part = conv_bias.shape[1]
    channels = lax.dynamic_slice_in_dim(channels, rank * part, part, 1)
    norm_grad = lax.dynamic_slice_in_dim(norm_grad, rank * norm_gain.shape[1], norm_gain.shape[1], 0)

    def by_layer(first, second):
        mine = jnp.where(core == 0, first, second)
        theirs = other_core(jnp.where(core == 0, second, first))
        return jnp.stack([jnp.where(core == 0, mine, theirs), jnp.where(core == 0, theirs, mine)])

    return (
        by_layer(hidden_1, hidden_2)[None],
        by_layer(input_grad_0, input_grad_1)[None],
        norm_grad[None],
        grad_in_weight[None],
        channels[None, :TAPS],
        channels[TAPS:],
        own[None, :heads],
        own[None, heads : 2 * heads],
        own[None, 2 * heads : 3 * heads],
        own[None, 3 * heads :],
        out_grad.astype(F32)[None],
    )


def solution(mesh):
    return jax.shard_map(
        local,
        mesh=mesh,
        in_specs=(
            P("dp", "seq", None),
            P("dp", None),
            P("dp", "seq", None),
            P("section", "seq"),
            P("section", "seq", None),
            P("section", None, "seq"),
            P("section", "seq"),
            P("section", "seq"),
            P("section", "seq"),
            P("section", "seq"),
            P("section", "seq"),
            P("section", "seq", None),
        ),
        out_specs=(
            P("section", "dp", "seq", None),
            P("section", "dp", "seq", None),
            P("section", "seq"),
            P("section", "seq", None),
            P("section", None, "seq"),
            P("section", "seq"),
            P("section", "seq"),
            P("section", "seq"),
            P("section", "seq"),
            P("section", "seq"),
            P("section", "seq", None),
        ),
        check_vma=False,
    )
```

time: 4080 us -> 1290 us (0.32)
  waiting for transfers between devices: 1680 us -> 702 us
  local copies, waits for them, and re-layouts: 917 us -> 66.3 us
  matrix products: 594 us -> 31.2 us
  other arithmetic: 369 us -> 75.2 us
  Pallas kernels: 0 us -> 146 us
  blocking collectives: 363 us -> 235 us
  starting transfers between devices: 74.9 us -> 8.74 us
    reduce_scatter x5 -> x4, waiting for transfers between devices: 950 us -> 106 us  [local(): lax.psum_scatter(array, 'seq', scatter_dimension=0, tiled=True)]
    dot_general x198 -> x10, matrix products: 594 us -> 31.2 us  [mm_tn(): lax.dot_general(a, b, (((0,), (0,)), ((), ())), preferred_element_type=F32)]
    dynamic_update_slice x116 -> x2, local copies, waits for them, and re-layouts: 501 us -> 0.01 us  [small(): lax.dynamic_update_slice_in_dim(jnp.zeros((TAPS + 1, whole_inner), F32),...]
    all_gather x6 -> x1, blocking collectives: 266 us -> 9.87 us  [local(): gather = lambda array: lax.all_gather(array, 'seq', axis=0, tiled=True)]
    pallas_call x0 -> x4, Pallas kernels: none -> 146 us  [the longest x2 91.9 us: run_backward(): pl.pallas_call(functools.partial(backward_kernel, length), grid=(blocks,)...]
    all_gather x2 -> x4, waiting for transfers between devices: 328 us -> 196 us  [local(): gather = lambda array: lax.all_gather(array, 'seq', axis=0, tiled=True)]
    all_to_all x1, blocking collectives: 38.1 us -> 136 us  [layer_weights(): lax.all_to_all(bundle, 'seq', split_axis=0, concat_axis=0, tiled=True)]
    mul x91 -> x0, other arithmetic: 92 us -> none  [the longest x48 36 us: advance(): carried[-1] * jnp.exp(cumulative[-1])]
  transfers between devices with their start and end apart: 30 -> 25, of which waited for: 22 -> 15; matrix products, arithmetic and copies ran while one was open for 12% -> 8% of each run, Pallas kernels for 0% -> 0%
where the time goes in v1:
time: 1290 us; the launch traced here: 1280 us
  waiting for transfers between devices  702 us (54%)
  blocking collectives  235 us (18%)
  Pallas kernels  146 us (11%)
  other arithmetic  75.2 us (6%)
  local copies, waits for them, and re-layouts  66.3 us (5%)
  matrix products  31.2 us (2%)
  between operations  16 us (1%)
    all_gather x4, waiting for transfers between devices, local(): gather = lambda array: lax.all_gather(array, 'seq', axis=0, tiled=True)  196 us
    all_to_all x1, waiting for transfers between devices, local(): lax.all_to_all(in_grad.reshape(count, depth, -1), 'seq', split_axis=0, co...  182 us
    all_to_all x1, blocking collectives, layer_weights(): lax.all_to_all(bundle, 'seq', split_axis=0, concat_axis=0, tiled=True)  136 us
    psum x1, waiting for transfers between devices, local(): in_grad = lax.psum(in_grad, 'dp')  125 us
    reduce_scatter x4, waiting for transfers between devices, local(): lax.psum_scatter(array, 'seq', scatter_dimension=0, tiled=True)  106 us
    pallas_call x2, Pallas kernels, run_backward(): pl.pallas_call(functools.partial(backward_kernel, length), grid=(blocks,)...  91.9 us
    psum x1, waiting for transfers between devices, local(): channels, norm_grad = lax.psum((channels, norm_grad), ('dp', 'seq'))  73.1 us
    pallas_call x2, Pallas kernels, run_forward(): pl.pallas_call(functools.partial(forward_kernel, dh is not None, length),...  54.1 us
  transfers between devices with their start and end apart: 25, of which 15 were waited for; matrix products, arithmetic and copies ran while one was open for 8% of the time, Pallas kernels for 0%

profile of v1, /device:TPU:0, one launch (start us, length us, event | category | flops | bytes accessed | tf_op | source)
XLA Modules:
  0.0 1280.9 jit_solution(9390536589344226870)
XLA Ops:
  9.0 4.3 fusion.56
  13.6 4.3 copy.54
  17.9 2.6 copy.55
  20.6 3.2 fusion.2
  23.9 136.0 %all_to_all.10 = bf16[4,384,1920]{2,1,0:T(8,128)(2,1)} all-to-all(bf16[4,384,1920]{2,1,0:T(8,128)(2,1)S(1)} %fusion.2), channel_id=1, replica_groups=mesh['section'=2,'seq'=4,'dp'=4] {'seq'}, dimensions={0} | all-to-all | bytes 11796480 | tf_op jit(solution)/shard_map/all_to_all | solution.py:654
  162.4 17.7 %all-reduce.2 = bf16[18176]{0:T(1024)(128)(2,1)S(1)} all-reduce(bf16[18176]{0:T(1024)(128)(2,1)S(1)} %dynamic-update-slice), channel_id=2, replica_groups=mesh['section'=2,'seq'=4,'dp'=4] {'seq'}, use_global_device_ids=true, to_apply=%add.2 | all-reduce | flops 18176 | bytes 72704
  185.5 5.0 broadcast_select_fusion.4
  190.5 9.9 broadcast_select_fusion.1
  202.6 4.9 fusion.55
  207.5 37.3 %all-gather.8.cloned.1.call-done.normed_ref = bf16[1024,1536]{1,0:T(8,128)(2,1)} async-done(((bf16[256,1536]{1,0:T(8,128)(2,1)}), bf16[1024,1536]{1,0:T(8,128)(2,1)}) %all-gather.8.cloned.1.call-update) | async-done | bytes 3145744 | tf_op jit(solution)/shard_map/all_gather | solution.py:732
  244.8 25.3 %layer_forward.2 = (bf16[1024,768]{1,0:T(8,128)(2,1)S(1)}, bf16[1024,768]{1,0:T(8,128)(2,1)}, bf16[1024,256]{1,0:T(8,128)(2,1)S(1)}, f32[1024,128]{1,0:T(8,128)S...) custom-call(s32[4]{0:T(128)S(1)} %fusion.48.starts_ref, ...), custom_call_target="tpu_custom_call" | custom-call | flops 8455716864 | bytes 25165824 | tf_op jit(solution)/shard_map/layer_forward/pallas_call | solution.py:511
  272.1 2.5 constant_dynamic-slice_fusion.1
  274.7 9.5 psum.49
  284.3 46.9 %reduce-scatter.5.cloned.1.call-done = bf16[256,1536]{1,0:T(8,128)(2,1)} async-done(((bf16[1024,1536]{1,0:T(8,128)(2,1)}), bf16[256,1536]{1,0:T(8,128)(2,1)}) %reduce-scatter.5.cloned.1.call-update) | async-done | bytes 786448 | tf_op jit(solution)/shard_map/reduce_scatter | solution.py:733
  336.6 4.9 fusion.54
  341.5 54.8 %all-gather.14.cloned.1.call-done = bf16[1,1024,1536]{2,1,0:T(8,128)(2,1)} async-done(((bf16[1,256,1536]{2,1,0:T(8,128)(2,1)}), bf16[1,1024,1536]{2,1,0:T(8,128)(2,1)}) %all-gather.14.cloned.1.call-update) | async-done | bytes 3145744 | tf_op jit(solution)/shard_map/all_gather | solution.py:732
  396.4 64.2 %all-gather.10.cloned.1.call-done.normed_ref = bf16[1024,1536]{1,0:T(8,128)(2,1)} async-done(((bf16[256,1536]{1,0:T(8,128)(2,1)}), bf16[1024,1536]{1,0:T(8,128)(2,1)}) %all-gather.10.cloned.1.call-update) | async-done | bytes 3145744 | tf_op jit(solution)/shard_map/all_gather | solution.py:732
  460.5 28.8 %layer_forward.3 = (bf16[1024,768]{1,0:T(8,128)(2,1)S(1)}, bf16[1024,768]{1,0:T(8,128)(2,1)}, bf16[1024,256]{1,0:T(8,128)(2,1)S(1)}, f32[1024,128]{1,0:T(8,128)S...) custom-call(s32[4]{0:T(128)S(1)} %fusion.48.starts_ref, ...), custom_call_target="tpu_custom_call" | custom-call | flops 8455716864 | bytes 25165824 | tf_op jit(solution)/shard_map/layer_forward/pallas_call | solution.py:511
  493.0 9.7 psum.50
  506.0 45.8 %layer_backward.2 = (bf16[1024,768]{1,0:T(8,128)(2,1)S(1)}, bf16[1024,768]{1,0:T(8,128)(2,1)}, bf16[1024,256]{1,0:T(8,128)(2,1)S(1)}, bf16[1024,128]{1,0:T(8,128...) custom-call(s32[4]{0:T(128)S(1)} %fusion.48.starts_ref, ...), custom_call_target="tpu_custom_call" | custom-call | flops 16911433728 | bytes 25165824 | tf_op jit(solution)/shard_map/layer_backward/pallas_call | solution.py:582
  553.1 59.2 %reduce-scatter.9.cloned.1.call-done = bf16[256,1536]{1,0:T(8,128)(2,1)} async-done(((bf16[1024,1536]{1,0:T(8,128)(2,1)}), bf16[256,1536]{1,0:T(8,128)(2,1)}) %reduce-scatter.9.cloned.1.call-update) | async-done | bytes 786448 | tf_op jit(solution)/shard_map/reduce_scatter | solution.py:733
  618.9 3.8 convolution_convert_fusion.8
  624.7 4.0 convolution_convert_fusion.3
  628.7 4.0 convolution_convert_fusion.2
  632.7 9.9 all-gather.2
  642.6 39.8 %all-gather.12.cloned.1.call-done.dh_ref = bf16[1024,1536]{1,0:T(8,128)(2,1)} async-done(((bf16[256,1536]{1,0:T(8,128)(2,1)}), bf16[1024,1536]{1,0:T(8,128)(2,1)}) %all-gather.12.cloned.1.call-update) | async-done | bytes 3145744 | tf_op jit(solution)/shard_map/all_gather | solution.py:732
  682.4 46.1 %layer_backward.3 = (bf16[1024,768]{1,0:T(8,128)(2,1)S(1)}, bf16[1024,768]{1,0:T(8,128)(2,1)}, bf16[1024,256]{1,0:T(8,128)(2,1)S(1)}, bf16[1024,128]{1,0:T(8,128...) custom-call(s32[4]{0:T(128)S(1)} %fusion.48.starts_ref, ...), custom_call_target="tpu_custom_call" | custom-call | flops 16911433728 | bytes 25165824 | tf_op jit(solution)/shard_map/layer_backward/pallas_call | solution.py:582
  730.6 3.2 convolution_convert_fusion.5
  733.8 3.0 convolution_convert_fusion.4
  737.3 3.8 broadcast_select_fusion
  741.1 9.9 collective-permute-done.10
  751.0 9.1 add_convert_fusion
  760.2 8.5 copy.66
  768.7 5.2 all-to-all-start.1
  775.3 4.9 convolution_convert_fusion.1
  780.3 4.4 broadcast_select_fusion.3
  785.3 4.0 collective-permute-done.11
  790.1 4.7 fusion.11
  794.8 181.9 %all-to-all-done.1 = bf16[4,384,1920]{1,2,0:T(8,128)(2,1)} async-done(((bf16[4,384,1920]{1,2,0:T(8,128)(2,1)}), bf16[4,384,1920]{1,2,0:T(8,128)(2,1)}, u32[]{:S(2)}, u32[]{:S(2)}) %all-to-all-start.1) | async-done | bytes 5898272 | tf_op jit(solution)/shard_map/all_to_all | solution.py:785
  982.8 3.2 select_bitcast_fusion.3
  988.3 3.2 fusion.30
  994.9 9.9 psum.54
  1006.0 73.1 %all-reduce.7.cloned.1.call-done = f32[5,3328]{1,0:T(8,128)} async-done(((f32[5,3328]{1,0:T(8,128)}), f32[5,3328]{1,0:T(8,128)}) %all-reduce.7.cloned.1.call-update) | async-done | bytes 66576 | tf_op jit(solution)/shard_map/psum | solution.py:828
  1081.9 42.4 %psum.51 = f32[1536]{0:T(1024)S(1)} all-reduce(f32[1536]{0:T(1024)S(1)} %select_add_fusion.1), channel_id=1, replica_groups=mesh['section'=2,'seq'=4,'dp'=4] {'dp','seq'}, use_global_device_ids=true, to_apply=%region_13.14 | all-reduce | flops 1536 | bytes 12288 | tf_op jit(solution)/shard_map/psum | solution.py:828
  1129.1 124.8 %all-reduce.9.cloned.1.call-done = (bf16[4,384,1920]{1,2,0:T(8,128)(2,1)}, bf16[1,768,1536]{2,1,0:T(8,128)(2,1)}) async-done(((bf16[4,384,1920]{1,2,0:T(8,128)(2,1)}, bf16[1,768,1536]{2,1,0:T(8,128)(2,1)}), (bf16[4,384,1920]{1,2,0:T(8,128)(2,1)}, bf16[1,768,1536]{2,1,0:T(8,128)(2,1)})) %all-reduce.9.cloned.1.call-update) | async-done | bytes 8257552 | tf_op jit(solution)/shard_map/psum | solution.py:788
  1253.9 6.7 fusion.53
  1262.3 2.8 broadcast_in_dim.84
  1265.1 8.5 maximum_bitcast_fusion
  (250 shorter events, 63.5 us)
Async XLA Ops:
  7.2 176.1 %copy-start = (s32[2,4]{1,0:T(2,128)S(1)}, s32[2,4]{1,0:T(2,128)}, u32[]{:S(2)}) copy-start(s32[2,4]{1,0:T(2,128)} %param.13) | copy-start | bytes 100
  7.2 237.6 %all-gather.8.cloned.1.call-start = ((), (), s32[]{:S(2)}) async-start(), calls=%async_computation.6 | async-start | bytes 3932160 | tf_op jit(solution)/shard_map/all_gather | solution.py:732
  23.8 136.1 %copy-start.41 = (bf16[1,12]{1,0:T(2,128)(2,1)S(1)}, bf16[1,12]{1,0:T(2,128)(2,1)}, u32[]{:S(2)}) copy-start(bf16[1,12]{1,0:T(2,128)(2,1)} %param.21) | copy-start | bytes 76
  23.8 136.1 %copy-start.42 = (bf16[1,12]{1,0:T(2,128)(2,1)S(1)}, bf16[1,12]{1,0:T(2,128)(2,1)}, u32[]{:S(2)}) copy-start(bf16[1,12]{1,0:T(2,128)(2,1)} %param.20) | copy-start | bytes 76
  23.8 136.1 %copy-start.43 = (bf16[1,12]{1,0:T(2,128)(2,1)S(1)}, bf16[1,12]{1,0:T(2,128)(2,1)}, u32[]{:S(2)}) copy-start(bf16[1,12]{1,0:T(2,128)(2,1)} %param.19) | copy-start | bytes 76
  23.8 136.7 %copy-start.40 = (bf16[1,768]{1,0:T(2,128)(2,1)S(1)}, bf16[1,768]{1,0:T(2,128)(2,1)}, u32[]{:S(2)}) copy-start(bf16[1,768]{1,0:T(2,128)(2,1)} %param.22) | copy-start | bytes 4612
  23.8 136.8 %copy-start.44 = (bf16[1,384]{1,0:T(2,128)(2,1)S(1)}, bf16[1,384]{1,0:T(2,128)(2,1)}, u32[]{:S(2)}) copy-start(bf16[1,384]{1,0:T(2,128)(2,1)} %param.15) | copy-start | bytes 2308
  23.8 136.8 %copy-start.39 = (bf16[1,832]{1,0:T(2,128)(2,1)S(1)}, bf16[1,832]{1,0:T(2,128)(2,1)}, u32[]{:S(2)}) copy-start(bf16[1,832]{1,0:T(2,128)(2,1)} %param.18) | copy-start | bytes 4996
  23.8 136.8 %copy-start.38 = (bf16[1,4,832]{2,1,0:T(4,128)(2,1)S(1)}, bf16[1,4,832]{2,1,0:T(4,128)(2,1)}, u32[]{:S(2)}) copy-start(bf16[1,4,832]{2,1,0:T(4,128)(2,1)} %param.17) | copy-start | bytes 19972
  23.8 136.9 %copy-start.46 = (u32[32]{0:T(128)S(1)}, u32[32]{0:T(128)}, u32[]{:S(2)}) copy-start(u32[32]{0:T(128)} %constant.82) | copy-start | bytes 388
  23.9 157.1 %copy-start.24 = (bf16[2,256,1536]{2,1,0:T(8,128)(2,1)S(1)}, bf16[2,256,1536]{2,1,0:T(8,128)(2,1)}, u32[]{:S(2)}) copy-start(bf16[2,256,1536]{2,1,0:T(8,128)(2,1)} %param.12) | copy-start | bytes 4718596
  159.9 30.6 %collective-permute-start.1 = (bf16[1536,1920]{1,0:T(8,128)(2,1)}, bf16[1536,1920]{1,0:T(8,128)(2,1)}, u32[]{:S(2)}, u32[]{:S(2)}) collective-permute-start(bf16[1536,1920]{1,0:T(8,128)(2,1)} %bitcast.8), channel_id=1, source_target_pairs={{0,16},{16,0},{1,17},{17,1},{2,18},{18,2},{3,19},{19,3},{4,20},{20... | collective-permute-start | bytes 17694728 | tf_op jit(solution)/shard_map/ppermute | solution.py:621
  159.9 23.3 %collective-permute-start.4 = (f32[8,128]{1,0:T(8,128)S(1)}, f32[8,128]{1,0:T(8,128)S(1)}, u32[]{:S(2)}, u32[]{:S(2)}) collective-permute-start(f32[8,128]{1,0:T(8,128)S(1)} %fusion.47), channel_id=1, source_target_pairs={{0,16},{16,0},{1,17},{17,1},{2,18},{18,2},{3,19},{19,3},{4,20},{20... | collective-permute-start | bytes 12296 | tf_op jit(solution)/shard_map/ppermute | solution.py:621
  160.5 24.7 %collective-permute-start.5 = (f32[8,768]{1,0:T(8,128)S(1)}, f32[8,768]{1,0:T(8,128)S(1)}, u32[]{:S(2)}, u32[]{:S(2)}) collective-permute-start(f32[8,768]{1,0:T(8,128)S(1)} %broadcast_in_dim.71), channel_id=1, source_target_pairs={{0,16},{16,0},{1,17},{17,1},{2,18},{18,2},{3,19},{19,3},{4,20},{20... | collective-permute-start | bytes 73736 | tf_op jit(solution)/shard_map/ppermute | solution.py:621
  180.4 1.3 collective-permute-start
  180.5 5.0 collective-permute-start.6
  182.9 148.3 %reduce-scatter.5.cloned.1.call-start = ((), (), s32[]{:S(2)}) async-start(), calls=%async_computation.7 | async-start | bytes 3932160 | tf_op jit(solution)/shard_map/reduce_scatter | solution.py:733
  183.0 2.1 collective-permute-start.3
  183.3 1.9 collective-permute-start.2
  272.0 124.3 %all-gather.14.cloned.1.call-start = ((), (), s32[]{:S(2)}) async-start(), calls=%async_computation.14 | async-start | bytes 3932160 | tf_op jit(solution)/shard_map/all_gather | solution.py:732
  274.6 185.9 %all-gather.10.cloned.1.call-start = ((), (), s32[]{:S(2)}) async-start(), calls=%async_computation.8 | async-start | bytes 3932160 | tf_op jit(solution)/shard_map/all_gather | solution.py:732
  334.2 278.1 %reduce-scatter.9.cloned.1.call-start = ((), (), s32[]{:S(2)}) async-start(), calls=%async_computation.10 | async-start | bytes 3932160 | tf_op jit(solution)/shard_map/reduce_scatter | solution.py:733
  553.0 59.3 %copy-start.20 = (bf16[256,1536]{1,0:T(8,128)(2,1)S(1)}, bf16[256,1536]{1,0:T(8,128)(2,1)}, u32[]{:S(2)}) copy-start(bf16[256,1536]{1,0:T(8,128)(2,1)} %copy-done.19) | copy-start | bytes 2359300
  553.0 129.4 %all-gather.12.cloned.1.call-start = ((), (), s32[]{:S(2)}) async-start(), calls=%async_computation.11 | async-start | bytes 3932160 | tf_op jit(solution)/shard_map/all_gather | solution.py:732
  618.7 358.0 %reduce-scatter.7.cloned.1.call-start = ((), (), s32[]{:S(2)}) async-start(), calls=%async_computation.9 | async-start | bytes 3932160 | tf_op jit(solution)/shard_map/reduce_scatter | solution.py:733
  624.7 4.0 copy-start.49
  628.7 53.7 %copy-start.9 = (bf16[4,128,768]{2,1,0:T(8,128)(2,1)S(1)}, bf16[4,128,768]{2,1,0:T(8,128)(2,1)}, u32[]{:S(2)}) copy-start(bf16[4,128,768]{2,1,0:T(8,128)(2,1)} %copy-done.8) | copy-start | bytes 2359300
  628.7 53.7 %copy-start.15 = (bf16[1024,256]{1,0:T(8,128)(2,1)S(1)}, bf16[1024,256]{1,0:T(8,128)(2,1)}, u32[]{:S(2)}) copy-start(bf16[1024,256]{1,0:T(8,128)(2,1)} %copy-done.14) | copy-start | bytes 1572868
  628.7 53.7 %copy-start.17 = (f32[1024,128]{1,0:T(8,128)S(1)}, f32[1024,128]{1,0:T(8,128)}, u32[]{:S(2)}) copy-start(f32[1024,128]{1,0:T(8,128)} %copy-done.16) | copy-start | bytes 1572868
  682.4 46.1 %copy-start.30 = (bf16[1024,1536]{1,0:T(8,128)(2,1)S(1)}, bf16[1024,1536]{1,0:T(8,128)(2,1)}, u32[]{:S(2)}) copy-start(bf16[1024,1536]{1,0:T(8,128)(2,1)} %all-gather.8.cloned.1.call-done.normed_ref) | copy-start | bytes 9437188
  741.1 9.9 collective-permute-start.10
  768.7 208.0 %all-to-all-start.1 = ((bf16[4,384,1920]{1,2,0:T(8,128)(2,1)}), bf16[4,384,1920]{1,2,0:T(8,128)(2,1)}, u32[]{:S(2)}, u32[]{:S(2)}) async-start(bf16[4,384,1920]{1,2,0:T(8,128)(2,1)} %copy.66), calls=%async_computation.5 | async-start | bytes 11796480 | tf_op jit(solution)/shard_map/all_to_all | solution.py:785
  773.9 212.3 %reduce-scatter.11.cloned.1.call-start = ((), (), s32[]{:S(2)}) async-start(), calls=%async_computation.12 | async-start | bytes 3932160 | tf_op jit(solution)/shard_map/reduce_scatter | solution.py:733
  774.7 304.4 %all-reduce.7.cloned.1.call-start = ((), (), s32[]{:S(2)}) async-start(), calls=%async_computation.13 | async-start | bytes 212992 | tf_op jit(solution)/shard_map/psum | solution.py:828
  775.3 4.9 copy-start.45
  775.3 4.9 copy-start.48
  780.2 4.4 copy-start.37
  784.7 5.4 collective-permute-start.13
  784.9 4.4 collective-permute-start.11
  790.0 463.9 %all-reduce.9.cloned.1.call-start = ((), (), s32[]{:S(2)}) async-start(), calls=%async_computation.15 | async-start | bytes 16515072 | tf_op jit(solution)/shard_map/psum | solution.py:788
  980.2 2.6 collective-permute-start.7
  980.4 7.9 copy-start.23
  991.4 133.5 %copy-start.29 = (bf16[256,1536]{1,0:T(8,128)(2,1)S(1)}, bf16[256,1536]{1,0:T(8,128)(2,1)}, u32[]{:S(2)}) copy-start(bf16[256,1536]{1,0:T(8,128)(2,1)} %reduce-scatter.11.cloned.1.call-done) | copy-start | bytes 2359300
  991.4 133.5 %collective-permute-start.8 = (f32[256,1536]{1,0:T(8,128)}, f32[256,1536]{1,0:T(8,128)}, u32[]{:S(2)}, u32[]{:S(2)}) collective-permute-start(f32[256,1536]{1,0:T(8,128)} %fusion.30), channel_id=1, source_target_pairs={{0,16},{16,0},{1,17},{17,1},{2,18},{18,2},{3,19},{19,3},{4,20},{20... | collective-permute-start | bytes 4718600 | tf_op jit(solution)/shard_map/ppermute | solution.py:621
  991.7 3.2 collective-permute-start.12
  1006.0 75.9 %collective-permute-start.9 = (f32[1536]{0:T(1024)S(1)}, f32[1536]{0:T(1024)S(1)}, u32[]{:S(2)}, u32[]{:S(2)}) collective-permute-start(f32[1536]{0:T(1024)S(1)} %broadcast_select_fusion.10), channel_id=1, source_target_pairs={{0,16},{16,0},{1,17},{17,1},{2,18},{18,2},{3,19},{19,3},{4,20},{20... | collective-permute-start | bytes 18440 | tf_op jit(solution)/shard_map/ppermute | solution.py:621
  1253.9 6.7 copy-start.18
  1265.1 8.5 copy-start.1
  (28 other events, 58.2 us)
Sparse Core Ops, SparseCore 0:
  183.0 61.7 all-gather.7
  272.1 59.0 reduce-scatter.4
  332.8 63.5 all-gather.13
  398.3 62.1 all-gather.9
  553.1 59.1 reduce-scatter.8
  618.8 63.5 all-gather.11
  741.3 100.6 reduce-scatter.6
  844.8 114.2 reduce-scatter.10
  964.6 114.4 all-reduce.6
  1083.3 170.5 all-reduce.8

commit v2 on v1

--- a/solution.py
+++ b/solution.py
@@ -103,15 +103,23 @@
     return row, col
 
 
+def split_weights(inner, refs):
+    if refs[0].shape[1] > inner:
+        parts = [(0, inner), (inner, 2 * inner), (2 * inner, 2 * inner + 3 * STATE)]
+        return [refs[0].at[:, low:high] for low, high in parts] + [refs[1:]]
+    return [refs[0], refs[1], refs[2], refs[3:]]
+
+
+def own_heads(columns, heads, sign):
+    shift = lax.rem(128 + sign * heads * lax.axis_index("seq"), 128)
+    return pltpu.roll(columns, shift, 1)
+
+
 def forward_kernel(
     with_back,
     length,
     starts_ref,
     normed_ref,
-    wg_ref,
-    wx_ref,
-    wbc_ref,
-    wdt_ref,
     kx_ref,
     kbc_ref,
     heads_ref,
@@ -119,6 +127,8 @@
     wo_ref,
     *rest,
 ):
+    inner = kx_ref.shape[1]
+    wg_ref, wx_ref, wbc_ref, rest = split_weights(inner, rest)
     if with_back:
         dh_ref, rest = rest[0], rest[1:]
     (
@@ -134,10 +144,8 @@
         ext_bc,
         memory,
         gu_ref,
-        y_ref,
     ) = rest
     block = pl.program_id(0)
-    inner = wx_ref.shape[1]
 
     @pl.when(block == 0)
     def _():
@@ -151,10 +159,10 @@
         ext_bc[0:8, :] = ext_bc[SPAN : SPAN + 8, :]
 
     normed = normed_ref[...]
-    bc_low = mm(normed, wbc_ref[...]).astype(BF16)
-    bc_ref[...] = bc_low
-    ext_bc[8 : SPAN + 8, :] = bc_low.astype(F32)
-    dt_low = mm(normed, wdt_ref[...]).astype(BF16).astype(F32)
+    bcdt = mm(normed, wbc_ref[...]).astype(BF16)
+    bc_ref[...] = bcdt[:, : 2 * STATE]
+    ext_bc[8 : SPAN + 8, :] = bcdt[:, : 2 * STATE].astype(F32)
+    dt_low = own_heads(bcdt[:, 2 * STATE :].astype(F32), inner // HEAD, -1)
     dt_ref[...] = dt_low
     x_low = mm(normed, wx_ref[...]).astype(BF16)
     x_ref[...] = x_low
@@ -218,7 +226,7 @@
 
     stats = jnp.sum(squares, axis=1, keepdims=True)
     gu = gu_ref[...]
-    part_ref[...] = mm(gu, wo_ref[...]).astype(BF16)
+    part_ref[...] = mm(gu, wo_ref[...]).astype(part_ref.dtype)
     if with_back:
         dgated = mm_nt(dh_ref[...], wo_ref[...])
         along = jnp.sum(dgated * gu.astype(F32), axis=1, keepdims=True)
@@ -229,15 +237,32 @@
     stat_ref[...] = jnp.transpose(both)[0:8, :]
 
 
+def carry_on(sources, slots, sems):
+    turn, turns = pl.program_id(0), pl.num_programs(0)
+    copies = lax.axis_size("dp")
+    member = lax.axis_index("dp")
+    square = Square(member, sources, slots, sems)
+    holds = lax.axis_index("section") == 1
+
+    @pl.when(turn == 0)
+    def _():
+        greet_all({"dp": copies}, {"dp": member})
+
+    for when, stage in ((0, square.begin), (turns // 2, square.middle), (turns - 1, square.end)):
+
+        @pl.when((turn == when) & holds)
+        def _():
+            stage(0)
+            stage(1)
+
+
 def backward_kernel(
+    carries,
     length,
     starts_ref,
     dh_ref,
-    stat_ref,
-    wg_ref,
-    wx_ref,
-    wbc_ref,
-    wdt_ref,
+    scale_ref,
+    mean_ref,
     kx_ref,
     kbc_ref,
     heads_ref,
@@ -251,25 +276,27 @@
     dt_ref,
     scan_ref,
     state_ref,
-    dgate_ref,
-    dx_ref,
-    dbc_ref,
-    ddt_ref,
-    gated_ref,
-    dnormed_ref,
-    gx_ref,
-    gbc_ref,
-    gheads_ref,
-    ext_x,
-    ext_bc,
-    ext_dx,
-    ext_dbc,
-    dmemory,
-    dscore,
+    *rest,
 ):
+    inner = kx_ref.shape[1]
+    wg_ref, wx_ref, wbc_ref, rest = split_weights(inner, rest)
+    if carries:
+        sources, rest = rest[:2], rest[2:]
+    dgate_ref, dx_ref, dbc_ref, rest = split_weights(inner, rest)
+    gated_ref, dnormed_ref, gx_ref, gbc_ref, gheads_ref, *rest = rest
+    if carries:
+        slots, sems, rest = rest[:2], rest[-3:], rest[2:-3]
+        carry_on(sources, slots, sems)
+    (
+        ext_x,
+        ext_bc,
+        ext_dx,
+        ext_dbc,
+        dmemory,
+        dscore,
+    ) = rest
     blocks = pl.num_programs(0)
     block = blocks - 1 - pl.program_id(0)
-    inner = wx_ref.shape[1]
 
     @pl.when(pl.program_id(0) == 0)
     def _():
@@ -321,8 +348,8 @@
     scores = mm_nt(b_low, c_low)
     c_flip = jnp.transpose(c_low.astype(F32)).astype(BF16)
 
-    stat_cols = jnp.transpose(jnp.broadcast_to(stat_ref[0:1, :], (128, SPAN)))
-    mean_cols = jnp.transpose(jnp.broadcast_to(stat_ref[1:2, :], (128, SPAN)))
+    stat_cols = row_to_columns(scale_ref[0, 0:1, :])
+    mean_cols = row_to_columns(mean_ref[0, 0:1, :])
     dgated = mm_nt(dh_ref[...], wo_ref[...])
     dscore[...] = jnp.zeros_like(dscore)
     kx = kx_ref[...]
@@ -445,8 +472,9 @@
 
     drate = exact(upper, dtotal) + dlast[0:1, :]
     ddt = (ddelta + slope * drate) * sigmoid(dt)
-    ddt_low = ddt.astype(BF16)
-    ddt_ref[...] = ddt_low
+    lane = lax.broadcasted_iota(jnp.int32, (SPAN, 128), 1)
+    own_ddt = jnp.where(lane < inner // HEAD, ddt, 0.0)
+    dbc_ref[:, 2 * STATE :] = own_heads(own_ddt, inner // HEAD, 1).astype(BF16)
     gheads_ref[...] += jnp.concatenate(
         [
             jnp.sum(ddt, axis=0, keepdims=True),
@@ -459,12 +487,19 @@
         mm_nt(dgate_ref[...], wg_ref[...])
         + mm_nt(dx_ref[...], wx_ref[...])
         + mm_nt(dbc_ref[...], wbc_ref[...])
-        + mm_nt(ddt_low, wdt_ref[...])
-    ).astype(BF16)
+    ).astype(dnormed_ref.dtype)
 
 
 def whole(array):
     return pl.BlockSpec(array.shape, lambda i: (0,) * array.ndim, pipeline_mode=pl.Buffered(1))
+
+
+def of_layer(array, layer):
+    return pl.BlockSpec(
+        (None,) + array.shape[1:],
+        lambda i: (layer,) + (0,) * (array.ndim - 1),
+        pipeline_mode=pl.Buffered(1),
+    )
 
 
 def cost(length, width, inner, passes):
@@ -475,16 +510,21 @@
 VMEM_LIMIT = 48 * 2**20
 
 
+def part_kind(length, width):
+    return F32 if length * width * 4 <= 8 * 2**20 else BF16
+
+
 def run_forward(starts, normed, weights, dh=None):
-    wg, wx, wbc, wdt, kx, kbc, heads, gain, wo = weights
+    columns, kx, kbc, heads, gain, wo = weights
     length, width = normed.shape
-    inner = wx.shape[1]
+    inner = kx.shape[1]
     blocks = length // SPAN
     rows = lambda cols: pl.BlockSpec((SPAN, cols), lambda i: (i, 0))
-    operands = [starts, normed, wg, wx, wbc, wdt, kx, kbc, heads, gain, wo]
-    in_specs = [pl.BlockSpec(memory_space=pltpu.SMEM), rows(width)] + [
-        whole(array) for array in operands[2:]
-    ]
+    small = [kx, kbc, heads, gain]
+    given = [wo] + list(columns)
+    operands = [starts, normed] + small + [array for array, _ in given]
+    in_specs = [pl.BlockSpec(memory_space=pltpu.SMEM), rows(width)]
+    in_specs += [whole(array) for array in small] + [spec for _, spec in given]
     if dh is not None:
         operands.append(dh)
         in_specs.append(rows(width))
@@ -495,7 +535,7 @@
         jax.ShapeDtypeStruct((length, 128), F32),
         jax.ShapeDtypeStruct((length, inner), F32),
         jax.ShapeDtypeStruct((blocks, STATE, inner), BF16),
-        jax.ShapeDtypeStruct((length, width), BF16),
+        jax.ShapeDtypeStruct((length, width), part_kind(length, width)),
         jax.ShapeDtypeStruct((8, length), F32),
     ]
     out_specs = [
@@ -519,7 +559,6 @@
             pltpu.VMEM((SPAN + 8, 2 * STATE), F32),
             pltpu.VMEM((STATE, inner), F32),
             pltpu.VMEM((SPAN, inner), BF16),
-            pltpu.VMEM((SPAN, inner), F32),
         ],
         compiler_params=pltpu.CompilerParams(
             dimension_semantics=("arbitrary",), vmem_limit_bytes=VMEM_LIMIT
@@ -529,23 +568,22 @@
     )(*operands)
 
 
-def run_backward(starts, dh, stats, weights, saved):
-    wg, wx, wbc, wdt, kx, kbc, heads, gain, wo = weights
+def run_backward(starts, dh, scales, means, weights, saved, carried=()):
+    columns, kx, kbc, heads, gain, wo = weights
     gate, x, bc, dt, scanned, states = saved
     length, width = dh.shape
-    inner = wx.shape[1]
+    inner = kx.shape[1]
     blocks = length // SPAN
     rows = lambda cols: pl.BlockSpec((SPAN, cols), lambda i: (blocks - 1 - i, 0))
     halo = lambda cols: pl.BlockSpec(
         (16, cols), lambda i: (jnp.maximum((blocks - 1 - i) * (SPAN // 16) - 1, 0), 0)
     )
     fixed = lambda shape: pl.BlockSpec(shape, lambda i: (0,) * len(shape))
-    operands = [starts, dh, stats, wg, wx, wbc, wdt, kx, kbc, heads, gain, wo]
-    in_specs = [
-        pl.BlockSpec(memory_space=pltpu.SMEM),
-        rows(width),
-        pl.BlockSpec((8, SPAN), lambda i: (0, blocks - 1 - i)),
-    ] + [whole(array) for array in operands[3:]]
+    stat = pl.BlockSpec((1, 8, SPAN), lambda i: (blocks - 1 - i, 0, 0))
+    small = [kx, kbc, heads, gain]
+    operands = [starts, dh, scales, means] + small + [wo[0]]
+    in_specs = [pl.BlockSpec(memory_space=pltpu.SMEM), rows(width), stat, stat]
+    in_specs += [whole(array) for array in small] + [wo[1]]
     operands += [gate, x, x, bc, bc, dt, scanned, states]
     in_specs += [
         rows(inner),
@@ -557,30 +595,33 @@
         rows(inner),
         pl.BlockSpec((1, STATE, inner), lambda i: (blocks - 1 - i, 0, 0)),
     ]
-    out_shape = [
+    operands += [array for array, _ in columns]
+    in_specs += [spec for _, spec in columns]
+    operands += list(carried)
+    in_specs += [whole(array) for array in carried]
+    widths = [2 * inner + 3 * STATE] if len(columns) == 1 else [inner, inner, 3 * STATE]
+    out_shape = [jax.ShapeDtypeStruct((length, cols), BF16) for cols in widths] + [
         jax.ShapeDtypeStruct((length, inner), BF16),
-        jax.ShapeDtypeStruct((length, inner), BF16),
-        jax.ShapeDtypeStruct((length, 2 * STATE), BF16),
-        jax.ShapeDtypeStruct((length, 128), BF16),
-        jax.ShapeDtypeStruct((length, inner), BF16),
-        jax.ShapeDtypeStruct((length, width), BF16),
+        jax.ShapeDtypeStruct((length, width), part_kind(length, width)),
         jax.ShapeDtypeStruct((8, inner), F32),
         jax.ShapeDtypeStruct((8, 2 * STATE), F32),
         jax.ShapeDtypeStruct((8, 128), F32),
     ]
-    out_specs = [
-        rows(inner),
-        rows(inner),
-        rows(2 * STATE),
-        rows(128),
+    out_specs = [rows(cols) for cols in widths] + [
         rows(inner),
         rows(width),
         fixed((8, inner)),
         fixed((8, 2 * STATE)),
         fixed((8, 128)),
     ]
+    sems, settings = [], {}
+    if carried:
+        copies = lax.axis_size("dp")
+        out_shape += [jax.ShapeDtypeStruct((copies,) + c.shape, c.dtype) for c in carried]
+        out_specs += [IN_HBM, IN_HBM]
+        sems, settings = square_sems(), {"collective_id": 6, "has_side_effects": True}
     return pl.pallas_call(
-        functools.partial(backward_kernel, length),
+        functools.partial(backward_kernel, bool(carried), length),
         grid=(blocks,),
         in_specs=in_specs,
         out_specs=out_specs,
@@ -592,9 +633,10 @@
             pltpu.VMEM((SPAN + 8, 2 * STATE), F32),
             pltpu.VMEM((STATE, inner), F32),
             pltpu.VMEM((SPAN, SPAN), F32),
-        ],
+        ]
+        + sems,
         compiler_params=pltpu.CompilerParams(
-            dimension_semantics=("arbitrary",), vmem_limit_bytes=VMEM_LIMIT
+            dimension_semantics=("arbitrary",), vmem_limit_bytes=VMEM_LIMIT, **settings
         ),
         cost_estimate=cost(length, width, inner, 2),
         name="layer_backward",
@@ -614,7 +656,396 @@
     unit = rows_in * inverse
     scaled = grad * gain_vec
     back = inverse * (scaled - unit * jnp.mean(scaled * unit, axis=-1, keepdims=True))
-    return back, jnp.sum(grad * unit, axis=0)
+    return back, jnp.sum(grad * unit, axis=0, keepdims=True)
+
+
+MESH = pl.DeviceIdType.MESH
+PIECE = 16
+HOP = 1
+
+
+def along(axis, index):
+    return {axis: index}
+
+
+def greet(axis, count, rank):
+    barrier = pltpu.get_barrier_semaphore()
+    for step in range(1, count):
+        pl.semaphore_signal(
+            barrier, inc=1, device_id=along(axis, lax.rem(rank + step, count)), device_id_type=MESH
+        )
+    pl.semaphore_wait(barrier, count - 1)
+
+
+def send_to(axis, index, source, target, send_sem, recv_sem):
+    return pltpu.make_async_remote_copy(
+        src_ref=source,
+        dst_ref=target,
+        send_sem=send_sem,
+        recv_sem=recv_sem,
+        device_id=along(axis, index),
+        device_id_type=MESH,
+    )
+
+
+def share_with_all(count, rank, source, slots, send_sems, recv_sems):
+    for step in range(1, count):
+        to = lax.rem(rank + step, count)
+        send_to("seq", to, source, slots.at[rank], send_sems.at[step], recv_sems.at[rank]).start()
+
+
+def share_wait_recv(count, rank, source, slots, send_sems, recv_sems):
+    for step in range(1, count):
+        origin = lax.rem(rank + step, count)
+        send_to(
+            "seq", origin, source, slots.at[origin], send_sems.at[step], recv_sems.at[origin]
+        ).wait_recv()
+
+
+def share_wait_send(count, rank, source, slots, send_sems, recv_sems):
+    for step in range(1, count):
+        to = lax.rem(rank + step, count)
+        send_to("seq", to, source, slots.at[rank], send_sems.at[step], recv_sems.at[rank]).wait_send()
+
+
+class Line:
+    def __init__(self, count, rank, part, inbox, spread, sems):
+        self.count, self.rank = count, rank
+        self.part, self.inbox, self.spread = part, inbox, spread
+        self.sum_send, self.sum_recv, self.out_right, self.out_left, self.out_recv = sems
+
+    def sum_copy(self, slot, target_slot, to, piece):
+        rows = pl.ds(piece * PIECE, PIECE)
+        return send_to(
+            "seq",
+            to,
+            self.inbox.at[slot, rows],
+            self.inbox.at[target_slot, rows],
+            self.sum_send.at[slot, piece],
+            self.sum_recv.at[target_slot, piece],
+        )
+
+    def arrived(self, slot, piece):
+        self.sum_copy(slot, slot, self.rank, piece).wait_recv()
+
+    def own_part(self, block, piece):
+        start = pl.multiple_of(block * SPAN + piece * PIECE, PIECE)
+        return self.part[pl.ds(start, PIECE), :].astype(F32)
+
+    def pass_sum(self, piece, away, sign):
+        count, rank = self.count, self.rank
+        rows = pl.ds(pl.multiple_of(piece * PIECE, PIECE), PIECE)
+        block = rank + sign * away
+        first = rank == 0 if sign > 0 else rank == count - 1
+
+        @pl.when(first)
+        def _():
+            self.inbox[block, rows, :] = self.own_part(block, piece).astype(BF16)
+
+        @pl.when(jnp.logical_not(first))
+        def _():
+            self.arrived(block, piece)
+            total = self.own_part(block, piece) + self.inbox[block, rows, :].astype(F32)
+            self.inbox[block, rows, :] = total.astype(BF16)
+
+        target = count if sign < 0 and away == 1 else block
+        self.sum_copy(block, target, rank + sign, piece).start()
+
+    def pass_sums(self, turn, pieces):
+        count, rank = self.count, self.rank
+        for away in range(count - 1, 0, -1):
+            for sign in (1, -1):
+                block = rank + sign * away
+                inside = block < count if sign > 0 else block >= 0
+                piece = turn - HOP * (rank if sign > 0 else count - 1 - rank)
+
+                @pl.when(inside & (piece >= 0) & (piece < pieces))
+                def _():
+                    self.pass_sum(piece, away, sign)
+
+    def own_lag(self, block):
+        return HOP * jnp.maximum(block, self.count - 1 - block)
+
+    def own_total(self, piece):
+        count, rank = self.count, self.rank
+        rows = pl.ds(pl.multiple_of(piece * PIECE, PIECE), PIECE)
+
+        @pl.when(rank > 0)
+        def _():
+            self.arrived(rank, piece)
+
+        @pl.when(rank < count - 1)
+        def _():
+            self.arrived(count, piece)
+
+        from_left = jnp.where(rank > 0, self.inbox[rank, rows, :].astype(F32), 0.0)
+        from_right = jnp.where(rank < count - 1, self.inbox[count, rows, :].astype(F32), 0.0)
+        return self.own_part(rank, piece) + from_left + from_right
+
+    def out_copy(self, block, piece, sign):
+        rows = pl.ds(pl.multiple_of(piece * PIECE, PIECE), PIECE)
+        sems = self.out_right if sign > 0 else self.out_left
+        return send_to(
+            "seq",
+            self.rank + sign,
+            self.spread.at[block, rows],
+            self.spread.at[block, rows],
+            sems.at[block, piece],
+            self.out_recv.at[block, piece],
+        )
+
+    def start_out(self, block, piece, sign):
+        @pl.when(self.rank < self.count - 1 if sign > 0 else self.rank > 0)
+        def _():
+            self.out_copy(block, piece, sign).start()
+
+    def pass_out(self, turn, pieces, away):
+        for sign in (1, -1):
+            block = self.rank - sign * away
+            piece = turn - self.own_lag(block) - HOP * away
+            inside = block >= 0 if sign > 0 else block < self.count
+
+            @pl.when(inside & (piece >= 0) & (piece < pieces))
+            def _():
+                self.out_copy(block, piece, sign).wait_recv()
+                self.start_out(block, piece, sign)
+
+    def run(self, pieces, own_piece, before_own=None, after_own=None, flow=None, pace=2):
+        count = self.count
+        lag = self.own_lag(self.rank)
+        turns = pieces + HOP * (2 if self.spread is not None else 1) * (count - 1)
+        if flow is not None:
+            turns = max(turns, flow.turns(pace))
+
+        def step(turn, _):
+            self.pass_sums(turn, pieces)
+            if self.spread is not None:
+                for away in range(1, count):
+                    self.pass_out(turn, pieces, away)
+            if before_own is not None:
+
+                @pl.when(turn == lag)
+                def _():
+                    before_own()
+
+            piece = turn - lag
+
+            @pl.when((piece >= 0) & (piece < pieces))
+            def _():
+                own_piece(piece, self.own_total(piece))
+                if self.spread is not None:
+                    self.start_out(self.rank, piece, 1)
+                    self.start_out(self.rank, piece, -1)
+
+            if after_own is not None:
+
+                @pl.when(piece == pieces - 1)
+                def _():
+                    after_own()
+
+            if flow is not None:
+                flow.turn(turn, pace)
+            return 0
+
+        lax.fori_loop(0, turns, step, 0)
+
+        def settle(piece, _):
+            for block in range(count):
+                right = (block > self.rank) & (self.rank < count - 1)
+                left = (block < self.rank) & (self.rank > 0)
+
+                @pl.when(right | left)
+                def _():
+                    self.sum_copy(block, block, self.rank, piece).wait_send()
+
+                if self.spread is not None:
+
+                    @pl.when((block <= self.rank) & (self.rank < count - 1))
+                    def _():
+                        self.out_copy(block, piece, 1).wait_send()
+
+                    @pl.when((block >= self.rank) & (self.rank > 0))
+                    def _():
+                        self.out_copy(block, piece, -1).wait_send()
+
+            return 0
+
+        lax.fori_loop(0, pieces, settle, 0)
+
+
+def line_sems(count, pieces):
+    return [
+        pltpu.SemaphoreType.DMA((count + 1, pieces)),
+        pltpu.SemaphoreType.DMA((count + 1, pieces)),
+        pltpu.SemaphoreType.DMA((count, pieces)),
+        pltpu.SemaphoreType.DMA((count, pieces)),
+        pltpu.SemaphoreType.DMA((count, pieces)),
+    ]
+
+
+def row_to_columns(row):
+    return jnp.transpose(jnp.broadcast_to(row, (128, SPAN)))
+
+
+def sum_forward_kernel(
+    count,
+    whole_inner,
+    part,
+    stat,
+    stream,
+    gain,
+    spread,
+    scales,
+    hidden,
+    product,
+    inbox,
+    slots,
+    columns,
+    stat_send,
+    stat_recv,
+    *sems,
+):
+    rank = lax.axis_index("seq")
+    greet("seq", count, rank)
+    share = (count, rank, stat, slots, stat_send, stat_recv)
+    share_with_all(*share)
+    line = Line(count, rank, part, inbox, spread, sems)
+
+    def before_own():
+        share_wait_recv(*share)
+        for block in range(count):
+            lanes = slice(block * SPAN, (block + 1) * SPAN)
+            total = stat[:, lanes]
+            for origin in range(count):
+                total = total + jnp.where(origin == rank, 0.0, slots[origin, :, lanes])
+            scales[block] = lax.rsqrt(total / whole_inner + EPSILON)
+        columns[...] = row_to_columns(scales[rank][0:1, :])
+
+    def own_piece(piece, total):
+        rows = pl.ds(pl.multiple_of(piece * PIECE, PIECE), PIECE)
+        y = total * columns[rows, 0:1]
+        low = (stream[rows, :].astype(F32) + y).astype(BF16)
+        hidden[rows, :] = low
+        product[rows, :] = y
+        spread[rank, rows, :] = norm_rows(low.astype(F32), gain[0:1, :]).astype(BF16)
+
+    line.run(SPAN // PIECE, own_piece, before_own)
+    share_wait_send(*share)
+
+
+def sum_plain_kernel(count, part, stream, gain, outer, grad, gain_grad, inbox, *sems):
+    rank = lax.axis_index("seq")
+    greet("seq", count, rank)
+    line = Line(count, rank, part, inbox, None, tuple(sems) + (None,) * 3)
+    gain_grad[...] = jnp.zeros_like(gain_grad)
+
+    def own_piece(piece, total):
+        rows = pl.ds(pl.multiple_of(piece * PIECE, PIECE), PIECE)
+        back, gain_part = norm_back(stream[rows, :].astype(F32), gain[0:1, :], total)
+        gain_grad[0:1, :] += gain_part
+        grad[rows, :] = outer[rows, :].astype(F32) + back
+
+    line.run(SPAN // PIECE, own_piece)
+
+
+def sum_stats_kernel(count, whole_inner, stat, scales, means, slots, stat_send, stat_recv):
+    rank = lax.axis_index("seq")
+    greet("seq", count, rank)
+    share = (count, rank, stat, slots, stat_send, stat_recv)
+    share_with_all(*share)
+    share_wait_recv(*share)
+    for block in range(count):
+        lanes = slice(block * SPAN, (block + 1) * SPAN)
+        total = stat[:, lanes]
+        for origin in range(count):
+            total = total + jnp.where(origin == rank, 0.0, slots[origin, :, lanes])
+        scale = lax.rsqrt(total[0:1, :] / whole_inner + EPSILON)
+        scales[block] = jnp.broadcast_to(scale, (8, SPAN))
+        means[block] = jnp.broadcast_to(total[1:2, :] * scale / whole_inner, (8, SPAN))
+    share_wait_send(*share)
+
+
+IN_VMEM = pl.BlockSpec(memory_space=pltpu.VMEM)
+
+
+def line_call(kernel, name, collective_id, operands, out_shape, scratch):
+    return pl.pallas_call(
+        kernel,
+        out_shape=out_shape,
+        in_specs=[IN_VMEM] * len(operands),
+        out_specs=[IN_VMEM] * len(out_shape),
+        scratch_shapes=scratch,
+        compiler_params=pltpu.CompilerParams(
+            collective_id=collective_id, has_side_effects=True, vmem_limit_bytes=LINE_VMEM
+        ),
+        name=name,
+    )(*operands)
+
+
+LINE_VMEM = 60 * 2**20
+
+
+def sum_forward(part, stat, stream, gain, whole_inner):
+    count = lax.axis_size("seq")
+    length, width = part.shape
+    pieces = SPAN // PIECE
+    return line_call(
+        functools.partial(sum_forward_kernel, count, whole_inner),
+        "sum_forward",
+        1,
+        [part, stat, stream, gain],
+        [
+            jax.ShapeDtypeStruct((count, SPAN, width), BF16),
+            jax.ShapeDtypeStruct((count, 8, SPAN), F32),
+            jax.ShapeDtypeStruct((SPAN, width), BF16),
+            jax.ShapeDtypeStruct((SPAN, width), F32),
+        ],
+        [
+            pltpu.VMEM((count + 1, SPAN, width), BF16),
+            pltpu.VMEM((count, 8, length), F32),
+            pltpu.VMEM((SPAN, 128), F32),
+            pltpu.SemaphoreType.DMA((count,)),
+            pltpu.SemaphoreType.DMA((count,)),
+        ]
+        + line_sems(count, pieces),
+    )
+
+
+def sum_plain(part, stream, gain, outer):
+    count = lax.axis_size("seq")
+    length, width = part.shape
+    pieces = SPAN // PIECE
+    return line_call(
+        functools.partial(sum_plain_kernel, count),
+        "sum_plain",
+        3,
+        [part, stream, gain, outer],
+        [
+            jax.ShapeDtypeStruct((SPAN, width), F32),
+            jax.ShapeDtypeStruct((8, width), F32),
+        ],
+        [pltpu.VMEM((count + 1, SPAN, width), BF16)] + line_sems(count, pieces)[:2],
+    )
+
+
+def sum_stats(stat, whole_inner):
+    count = lax.axis_size("seq")
+    length = stat.shape[1]
+    return line_call(
+        functools.partial(sum_stats_kernel, count, whole_inner),
+        "sum_stats",
+        4,
+        [stat],
+        [
+            jax.ShapeDtypeStruct((count, 8, SPAN), F32),
+            jax.ShapeDtypeStruct((count, 8, SPAN), F32),
+        ],
+        [
+            pltpu.VMEM((count, 8, length), F32),
+            pltpu.SemaphoreType.DMA((count,)),
+            pltpu.SemaphoreType.DMA((count,)),
+        ],
+    )
 
 
 def other_core(array):
@@ -630,75 +1061,901 @@
     )
 
 
-def layer_weights(in_weight, conv_weight, conv_bias, step_bias, decay_log, skip_gain, gate_gain, out_weight, norm_gain):
+IN_HBM = pl.BlockSpec(memory_space=pl.ANY)
+
+
+def greet_all(sizes, ranks):
+    barrier = pltpu.get_barrier_semaphore()
+    total = 0
+    for axis, size in sizes.items():
+        for step in range(1, size):
+            to = lax.rem(ranks[axis] + step, size)
+            pl.semaphore_signal(barrier, inc=1, device_id={axis: to}, device_id_type=MESH)
+            total += 1
+    pl.semaphore_wait(barrier, total)
+
+
+def push(axis, index, source, target, send_sem, recv_sem):
+    return pltpu.make_async_remote_copy(
+        src_ref=source,
+        dst_ref=target,
+        send_sem=send_sem,
+        recv_sem=recv_sem,
+        device_id={axis: index},
+        device_id_type=MESH,
+    )
+
+
+def start_kernel(
+    sizes,
+    small,
+    hidden,
+    bundle,
+    out_weight,
+    normed,
+    columns,
+    rows_out,
+    smalls,
+    local_sem,
+    split_send,
+    split_recv,
+    copy_send,
+    copy_recv,
+    core_send,
+    core_recv,
+    out_send,
+    out_recv,
+    small_send,
+    small_recv,
+    small_core_send,
+    small_core_recv,
+    right_send,
+    left_send,
+    block_recv,
+):
+    ranks = {axis: lax.axis_index(axis) for axis in sizes}
+    core, rank, stream = ranks["section"], ranks["seq"], ranks["dp"]
+    count, copies = sizes["seq"], sizes["dp"]
+    part = bundle.shape[1]
+    depth = part * copies
+    greet_all(sizes, ranks)
+
+    smalls[core, rank] = small[...]
+    for step in range(1, count):
+        to = lax.rem(rank + step, count)
+        place = smalls.at[core, rank]
+        push("seq", to, place, place, small_send.at[step], small_recv.at[rank]).start()
+    push(
+        "section", 1 - core, out_weight.at[0], rows_out.at[core], out_send, out_recv
+    ).start()
+
+    def slot(origin, share):
+        return pl.ds(pl.multiple_of(origin * depth + share * part, part), part)
+
+    def split_copy(step):
+        to = lax.rem(rank + step, count)
+        return push(
+            "seq",
+            to,
+            bundle.at[to],
+            columns.at[core, slot(rank, stream)],
+            split_send.at[step],
+            split_recv.at[rank],
+        )
+
+    for step in range(count - 1, 0, -1):
+        split_copy(step).start()
+    own = pltpu.make_async_copy(bundle.at[rank], columns.at[core, slot(rank, stream)], local_sem)
+    own.start()
+
+    def spread_slot(origin, held=None):
+        place = columns.at[core, slot(origin, stream)]
+        source = place if held is None else held
+        for step in range(1, copies):
+            to = lax.rem(stream + step, copies)
+            push(
+                "dp", to, source, place, copy_send.at[origin, step], copy_recv.at[origin, stream]
+            ).start()
+        push(
+            "section",
+            1 - core,
+            source,
+            place,
+            core_send.at[origin, stream],
+            core_recv.at[origin, stream],
+        ).start()
+
+    spread_slot(rank, bundle.at[rank])
+    rows_out[core] = out_weight[0]
+
+    for step in range(1, count):
+        origin = lax.rem(rank + step, count)
+        place = smalls.at[core, origin]
+        push("seq", origin, place, place, small_send.at[step], small_recv.at[origin]).wait_recv()
+    push(
+        "section", 1 - core, smalls.at[core], smalls.at[core], small_core_send, small_core_recv
+    ).start()
+
+    for step in range(1, count):
+        origin = lax.rem(rank + step, count)
+        place = columns.at[core, slot(origin, stream)]
+        push("seq", origin, place, place, split_send.at[step], split_recv.at[origin]).wait_recv()
+        spread_slot(origin)
+
+    push(
+        "section",
+        1 - core,
+        smalls.at[1 - core],
+        smalls.at[1 - core],
+        small_core_send,
+        small_core_recv,
+    ).wait_recv()
+    gain = jnp.concatenate([smalls[0, origin, 5:6, :depth] for origin in range(count)], axis=1)
+    normed[rank] = norm_rows(hidden[core].astype(F32), gain).astype(BF16)
+
+    def block_copy(block, sign):
+        return push(
+            "seq",
+            rank + sign,
+            normed.at[block],
+            normed.at[block],
+            (right_send if sign > 0 else left_send).at[block],
+            block_recv.at[block],
+        )
+
+    def open_end(sign):
+        return rank < count - 1 if sign > 0 else rank > 0
+
+    for sign in (1, -1):
+
+        @pl.when(open_end(sign))
+        def _():
+            block_copy(rank, sign).start()
+
+    for away in range(1, count):
+        for sign in (1, -1):
+            block = rank - sign * away
+
+            @pl.when(block >= 0 if sign > 0 else block < count)
+            def _():
+                block_copy(block, sign).wait_recv()
+
+                @pl.when(open_end(sign))
+                def _():
+                    block_copy(block, sign).start()
+
+    for origin in range(count):
+        for step in range(1, copies):
+            share = lax.rem(stream + step, copies)
+            place = columns.at[core, slot(origin, share)]
+            push(
+                "dp", share, place, place, copy_send.at[origin, step], copy_recv.at[origin, share]
+            ).wait_recv()
+            push(
+                "section",
+                1 - core,
+                place,
+                place,
+                core_send.at[origin, share],
+                core_recv.at[origin, share],
+            ).start()
+    for origin in range(count):
+        for share in range(copies):
+            theirs = columns.at[1 - core, slot(origin, share)]
+            copy = push(
+                "section",
+                1 - core,
+                theirs,
+                theirs,
+                core_send.at[origin, share],
+                core_recv.at[origin, share],
+            )
+            copy.wait_recv()
+            copy.wait_send()
+        for step in range(1, copies):
+            place = columns.at[core, slot(origin, stream)]
+            push(
+                "dp", stream, place, place, copy_send.at[origin, step], copy_recv.at[origin, stream]
+            ).wait_send()
+    own.wait()
+    rows_copy = push(
+        "section", 1 - core, out_weight.at[0], rows_out.at[1 - core], out_send, out_recv
+    )
+    rows_copy.wait_recv()
+    rows_copy.wait_send()
+    push(
+        "section", 1 - core, smalls.at[core], smalls.at[core], small_core_send, small_core_recv
+    ).wait_send()
+    for step in range(1, count):
+        to = lax.rem(rank + step, count)
+        place = smalls.at[core, rank]
+        push("seq", to, place, place, small_send.at[step], small_recv.at[rank]).wait_send()
+        split_copy(step).wait_send()
+    for block in range(count):
+
+        @pl.when((block <= rank) & (rank < count - 1))
+        def _():
+            block_copy(block, 1).wait_send()
+
+        @pl.when((block >= rank) & (rank > 0))
+        def _():
+            block_copy(block, -1).wait_send()
+
+
+def axis_sizes():
+    return {axis: lax.axis_size(axis) for axis in ("section", "seq", "dp")}
+
+
+def start(small, hidden, bundle, out_weight):
+    sizes = axis_sizes()
+    count, copies = sizes["seq"], sizes["dp"]
+    depth, inner, width = bundle.shape[1] * copies, out_weight.shape[1], out_weight.shape[2]
+    dma = pltpu.SemaphoreType.DMA
+    return pl.pallas_call(
+        functools.partial(start_kernel, sizes),
+        out_shape=[
+            jax.ShapeDtypeStruct((count,) + hidden.shape[1:], BF16),
+            jax.ShapeDtypeStruct((2, count * depth, 2 * inner + 3 * STATE), BF16),
+            jax.ShapeDtypeStruct((2, inner, width), BF16),
+            jax.ShapeDtypeStruct((2, count) + small.shape, F32),
+        ],
+        in_specs=[IN_VMEM, IN_VMEM, IN_HBM, IN_VMEM],
+        out_specs=[IN_VMEM, IN_HBM, IN_VMEM, IN_VMEM],
+        scratch_shapes=[
+            dma,
+            dma((count,)),
+            dma((count,)),
+            dma((count, copies)),
+            dma((count, copies)),
+            dma((count, copies)),
+            dma((count, copies)),
+            dma,
+            dma,
+            dma((count,)),
+            dma((count,)),
+            dma,
+            dma,
+            dma((count,)),
+            dma((count,)),
+            dma((count,)),
+        ],
+        compiler_params=pltpu.CompilerParams(
+            collective_id=5, has_side_effects=True, vmem_limit_bytes=LINE_VMEM
+        ),
+        name="start",
+    )(small, hidden, bundle, out_weight)
+
+
+def small_rows(conv_weight, conv_bias, norm_gain):
+    part = conv_bias.shape[1]
+    pad = -part % 128
+    rows = jnp.concatenate([conv_weight[0], conv_bias], axis=0).astype(F32)
+    rows = jnp.pad(rows, ((0, 0), (0, pad)))
+    gain = jnp.pad(norm_gain.astype(F32), ((0, 0), (0, part + pad - norm_gain.shape[1])))
+    return jnp.concatenate([rows, gain, jnp.zeros((2, part + pad), F32)], axis=0)
+
+
+def step_columns(rows, whole_inner):
+    rows = rows[:, 2 * whole_inner :]
+    return jnp.pad(rows, ((0, 0), (0, 3 * STATE - rows.shape[1])))
+
+
+def layer_facts(smalls, step_bias, decay_log, skip_gain, gate_gain, part, depth):
     count = lax.axis_size("seq")
     rank = lax.axis_index("seq")
-    inner = out_weight.shape[1]
+    inner = gate_gain.shape[1]
     heads = step_bias.shape[1]
-    whole_inner = inner * count
+    own = jnp.concatenate([step_bias, decay_log, skip_gain], axis=0)
+    own = jnp.pad(own, ((0, 5), (0, 128 - heads)))
+    own = both_layers(own.astype(F32))
+    gate = both_layers(jnp.broadcast_to(gate_gain, (8, inner)).astype(F32))
+    facts = []
+    for layer in range(2):
+        rows = smalls[layer]
+        taps = rows[:, :, :part].transpose(1, 0, 2).reshape(8, count * part)
+        gain = jnp.broadcast_to(rows[:, 5, :depth].reshape(1, -1), (8, count * depth))
+        facts.append(
+            (
+                lax.dynamic_slice_in_dim(taps, rank * inner, inner, 1),
+                taps[:, count * inner :],
+                own[layer],
+                gate[layer],
+                gain,
+            )
+        )
+    return facts
+
+
+def column_bundle(in_weight, inner):
+    count, copies = lax.axis_size("seq"), lax.axis_size("dp")
+    part = in_weight.shape[1] // copies
+    rows = lax.dynamic_slice_in_dim(in_weight[0], lax.axis_index("dp") * part, part, 0)
+    kinds = [
+        rows[:, kind * count * inner : (kind + 1) * count * inner]
+        .reshape(part, count, inner)
+        .transpose(1, 0, 2)
+        for kind in range(2)
+    ]
+    rest = step_columns(rows, count * inner)
+    kinds.append(jnp.broadcast_to(rest[None], (count,) + rest.shape))
+    return jnp.concatenate(kinds, axis=2)
+
+
+def columns_by_collectives(in_weight, inner):
+    count = lax.axis_size("seq")
     depth = in_weight.shape[1]
     rows = in_weight[0]
-    gate = rows[:, :whole_inner].reshape(depth, count, inner)
-    x = rows[:, whole_inner : 2 * whole_inner].reshape(depth, count, inner)
-    bc = rows[:, 2 * whole_inner : 2 * whole_inner + 2 * STATE]
-    dt = rows[:, 2 * whole_inner + 2 * STATE :].reshape(depth, count, heads)
-    bundle = jnp.concatenate(
+    kinds = []
+    for kind in range(2):
+        part = rows[:, kind * count * inner : (kind + 1) * count * inner]
+        part = part.reshape(depth, count, inner).transpose(1, 0, 2)
+        part = lax.all_to_all(part, "seq", split_axis=0, concat_axis=0, tiled=True)
+        kinds.append(both_layers(part.reshape(count * depth, inner)))
+    step_weight = step_columns(rows, count * inner)
+    kinds.append(both_layers(lax.all_gather(step_weight, "seq", axis=0, tiled=True)))
+    return [[(kind[layer], whole(kind[layer])) for kind in kinds] for layer in range(2)]
+
+
+class Flow:
+    def __init__(self, sizes, ranks, left_in, right_in, left_out, right_out, final, out_final, scratch, sems):
+        self.sizes, self.ranks = sizes, ranks
+        self.left_in, self.right_in, self.left_out, self.right_out = (
+            left_in,
+            right_in,
+            left_out,
+            right_out,
+        )
+        self.final, self.out_final = final, out_final
+        self.full, self.got, self.parts, self.sums = scratch
+        (
+            self.core_send,
+            self.core_recv,
+            self.part_send,
+            self.part_recv,
+            self.z_send,
+            self.z_recv,
+            self.give_send,
+            self.give_recv,
+        ) = sems
+        self.count, self.copies = sizes["seq"], sizes["dp"]
+        self.core, self.rank, self.stream = ranks["section"], ranks["seq"], ranks["dp"]
+        self.depth = self.full.shape[1]
+        self.half = self.depth // 2
+        self.share = self.half // self.copies
+        self.units = self.full.shape[0]
+
+    def half_rows(self, core):
+        return pl.ds(pl.multiple_of(core * self.half, self.half), self.half)
+
+    def multiply(self, unit):
+        depth = self.depth
+        tile = 384
+        full = self.full
+
+        def columns(left, right, at):
+            def body(index, _):
+                low = pl.multiple_of(index * tile, tile)
+                full[unit, :, pl.ds(low, tile)] = mm_tn(left, right[:, pl.ds(low, tile)]).astype(BF16)
+                return 0
+
+            lax.fori_loop(0, right.shape[1] // tile, body, 0)
+
+        @pl.when(unit < self.count)
+        def _():
+            at = pl.multiple_of(unit * depth, depth)
+            columns(self.left_in[:, pl.ds(at, depth)], self.right_in, at)
+
+        @pl.when(unit >= self.count)
+        def _():
+            at = pl.multiple_of((unit - self.count) * depth, depth)
+            columns(self.left_out[:, pl.ds(at, depth)], self.right_out, at)
+
+    def core_copy(self, unit):
+        return push(
+            "section",
+            1 - self.core,
+            self.full.at[unit, self.half_rows(1 - self.core)],
+            self.got.at[unit],
+            self.core_send.at[unit],
+            self.core_recv.at[unit],
+        )
+
+    def part_rows(self, member):
+        start = self.core * self.half + member * self.share
+        return pl.ds(pl.multiple_of(start, self.share), self.share)
+
+    def bits(self, unit):
+        first = 1 + lax.rem(unit, 2)
+        return first, 3 - first
+
+    def flip(self, bit):
+        low = lax.rem(lax.div(self.stream, bit), 2)
+        return self.stream + bit - 2 * bit * low
+
+    def step_copy(self, unit, step):
+        first, second = self.bits(unit)
+        partner, opposite = self.flip(first), self.flip(second)
+        member = (partner, partner + opposite - self.stream, opposite)[step]
+        return push(
+            "dp",
+            opposite if step == 2 else partner,
+            self.full.at[unit, self.part_rows(member)],
+            self.parts.at[unit, step],
+            self.part_send.at[unit, step],
+            self.part_recv.at[unit, step],
+        )
+
+    def z_copy(self, unit):
+        return push(
+            "seq",
+            unit,
+            self.sums.at[unit],
+            self.final.at[self.core, self.rank],
+            self.z_send.at[unit],
+            self.z_recv.at[self.rank],
+        )
+
+    def first(self, unit):
+        self.multiply(unit)
+        self.core_copy(unit).start()
+
+    def second(self, unit):
+        self.core_copy(unit).wait_recv()
+        rows = self.half_rows(self.core)
+        total = self.full[unit, rows, :].astype(F32) + self.got[unit].astype(F32)
+        self.full[unit, rows, :] = total.astype(BF16)
+        self.step_copy(unit, 0).start()
+        self.step_copy(unit, 1).start()
+
+    def third(self, unit):
+        opposite = self.flip(self.bits(unit)[1])
+        for step, member in ((1, opposite), (0, self.stream)):
+            self.step_copy(unit, step).wait_recv()
+            rows = self.part_rows(member)
+            total = self.full[unit, rows, :].astype(F32) + self.parts[unit, step].astype(F32)
+            self.full[unit, rows, :] = total.astype(BF16)
+            if step:
+                self.step_copy(unit, 2).start()
+
+    def fourth(self, unit):
+        self.step_copy(unit, 2).wait_recv()
+        total = self.full[unit, self.part_rows(self.stream), :].astype(F32)
+        total = (total + self.parts[unit, 2].astype(F32)).astype(BF16)
+
+        @pl.when(unit < self.count)
+        def _():
+            @pl.when(unit == self.rank)
+            def _():
+                self.final[self.core, self.rank] = total
+
+            @pl.when(unit != self.rank)
+            def _():
+                self.sums[unit] = total
+                self.z_copy(unit).start()
+
+        @pl.when(unit >= self.count)
+        def _():
+            self.out_final[self.core, unit - self.count] = total[:, : self.out_final.shape[3]]
+
+    LAGS = (0, 1, 4, 6)
+
+    def turn(self, turn, pace):
+        for stage, lag in zip((self.first, self.second, self.third, self.fourth), self.LAGS):
+            at = turn - lag
+
+            @pl.when((at >= 0) & (at < self.units * pace) & (lax.rem(at, pace) == 0))
+            def _():
+                stage(lax.div(at, pace))
+
+    def turns(self, pace):
+        return (self.units - 1) * pace + self.LAGS[3] + 1
+
+    def finals_here(self, layer):
+        for step in range(1, self.count):
+            origin = lax.rem(self.rank + step, self.count)
+            place = self.final.at[self.core, origin]
+            push("seq", origin, place, place, self.z_send.at[origin], self.z_recv.at[origin]).wait_recv()
+        for kind in range(2):
+
+            @pl.when(self.core != layer)
+            def _():
+                self.give_copy(kind).start()
+
+    def give_copy(self, kind):
+        final = (self.final, self.out_final)[kind]
+        place = final.at[self.core]
+        return push(
+            "section", 1 - self.core, place, place, self.give_send.at[kind], self.give_recv.at[kind]
+        )
+
+    def finals_given(self, layer):
+        for kind in range(2):
+            final = (self.final, self.out_final)[kind]
+
+            @pl.when(self.core == layer)
+            def _():
+                place = final.at[1 - self.core]
+                push(
+                    "section", 1 - self.core, place, place, self.give_send.at[kind], self.give_recv.at[kind]
+                ).wait_recv()
+
+            @pl.when(self.core != layer)
+            def _():
+                self.give_copy(kind).wait_send()
+
+    def settle(self):
+        def body(unit, _):
+            self.core_copy(unit).wait_send()
+            for step in range(3):
+                self.step_copy(unit, step).wait_send()
+
+            @pl.when((unit < self.count) & (unit != self.rank))
+            def _():
+                self.z_copy(unit).wait_send()
+
+            return 0
+
+        lax.fori_loop(0, self.units, body, 0)
+
+
+class Square:
+    def __init__(self, member, sources, slots, sems):
+        self.member, self.sources, self.slots = member, sources, slots
+        self.own_sem, self.send, self.recv = sems
+
+    def flip(self, bit):
+        return self.member + bit - 2 * bit * lax.rem(lax.div(self.member, bit), 2)
+
+    def own_copy(self, kind):
+        return pltpu.make_async_copy(
+            self.sources[kind], self.slots[kind].at[self.member], self.own_sem.at[kind]
+        )
+
+    def near_copy(self, kind, way):
+        return push(
+            "dp",
+            self.flip(1 + way),
+            self.sources[kind],
+            self.slots[kind].at[self.member],
+            self.send.at[kind, way],
+            self.recv.at[kind, way],
+        )
+
+    def far_copy(self, kind, way):
+        place = self.slots[kind].at[self.flip(1 + way), way]
+        return push(
+            "dp", self.flip(2 - way), place, place, self.send.at[kind, 2 + way], self.recv.at[kind, 2 + way]
+        )
+
+    def begin(self, kind):
+        self.own_copy(kind).start()
+        for way in range(2):
+            self.near_copy(kind, way).start()
+
+    def middle(self, kind):
+        for way in range(2):
+            self.near_copy(kind, way).wait_recv()
+            self.far_copy(kind, way).start()
+
+    def end(self, kind):
+        for way in range(2):
+            self.far_copy(kind, way).wait_recv()
+        for way in range(2):
+            self.near_copy(kind, way).wait_send()
+            self.far_copy(kind, way).wait_send()
+        self.own_copy(kind).wait()
+
+
+def square_sems():
+    dma = pltpu.SemaphoreType.DMA
+    return [dma((2,)), dma((2, 4)), dma((2, 4))]
+
+
+def flow_shapes(sizes, depth, inner, width, wide):
+    units = sizes["seq"] + inner // depth
+    share = depth // 2 // sizes["dp"]
+    dma = pltpu.SemaphoreType.DMA
+    scratch = [
+        pltpu.VMEM((units, depth, wide), BF16),
+        pltpu.VMEM((units, depth // 2, wide), BF16),
+        pltpu.VMEM((units, 3, share, wide), BF16),
+        pltpu.VMEM((sizes["seq"], share, wide), BF16),
+    ]
+    sems = [
+        dma((units,)),
+        dma((units,)),
+        dma((units, 3)),
+        dma((units, 3)),
+        dma((sizes["seq"],)),
+        dma((sizes["seq"],)),
+        dma((2,)),
+        dma((2,)),
+    ]
+    finals = [
+        jax.ShapeDtypeStruct((2, sizes["seq"], share, wide), BF16),
+        jax.ShapeDtypeStruct((2, inner // depth, share, width), BF16),
+    ]
+    return scratch, sems, finals
+
+
+def sum_backward_kernel(
+    sizes,
+    with_flow,
+    whole_inner,
+    part,
+    stream,
+    gain,
+    outer,
+    product,
+    *rest,
+):
+    ranks = {axis: lax.axis_index(axis) for axis in sizes}
+    rank, count = ranks["seq"], sizes["seq"]
+    if with_flow:
+        factors, rest = rest[:4], rest[4:]
+        finals, rest = rest[4:6], rest[:4] + rest[6:]
+    spread, means, grad, gain_grad, inbox, columns, *rest = rest
+    if with_flow:
+        scratch, rest = rest[:4], rest[4:]
+    row_send, row_recv, *sems = rest
+    greet_all(sizes if with_flow else {"seq": count}, ranks)
+    line = Line(count, rank, part, inbox, spread, sems[:5])
+    flow = None
+    if with_flow:
+        flow = Flow(sizes, ranks, *factors, *finals, scratch, sems[5:])
+    gain_grad[...] = jnp.zeros_like(gain_grad)
+    share = (count, rank, means.at[rank], means, row_send, row_recv)
+
+    def own_piece(piece, total):
+        rows = pl.ds(pl.multiple_of(piece * PIECE, PIECE), PIECE)
+        back, gain_part = norm_back(stream[rows, :].astype(F32), gain[0:1, :], total)
+        gain_grad[0:1, :] += gain_part
+        whole = outer[rows, :].astype(F32) + back
+        grad[rows, :] = whole
+        low = whole.astype(BF16)
+        spread[rank, rows, :] = low
+        along_rows = jnp.sum(low.astype(F32) * product[rows, :], axis=1, keepdims=True)
+        columns[rows, :] = jnp.broadcast_to(along_rows / whole_inner, (PIECE, 128))
+
+    def after_own():
+        means[rank] = jnp.transpose(columns[...])[0:8, :]
+        share_with_all(*share)
+
+    line.run(SPAN // PIECE, own_piece, None, after_own, flow)
+    if with_flow:
+        flow.finals_here(1)
+    share_wait_recv(*share)
+    share_wait_send(*share)
+    if with_flow:
+        flow.finals_given(1)
+        flow.settle()
+
+
+def sum_backward(part, stream, gain, outer, product, whole_inner, grads_of):
+    sizes = axis_sizes()
+    count = sizes["seq"]
+    length, width = part.shape
+    pieces = SPAN // PIECE
+    factors, scratch, sems, finals = [], [], [], []
+    if grads_of is not None:
+        factors = list(grads_of)
+        scratch, sems, finals = flow_shapes(
+            sizes, width // count, factors[2].shape[1], width, factors[1].shape[1]
+        )
+    return line_call(
+        functools.partial(sum_backward_kernel, sizes, grads_of is not None, whole_inner),
+        "sum_backward",
+        2,
+        [part, stream, gain, outer, product] + factors,
         [
-            gate,
-            x,
-            jnp.broadcast_to(bc[:, None, :], (depth, count, 2 * STATE)),
-            jnp.pad(dt, ((0, 0), (0, 0), (0, 128 - heads))),
+            jax.ShapeDtypeStruct((count, SPAN, width), BF16),
+            jax.ShapeDtypeStruct((count, 8, SPAN), F32),
+            jax.ShapeDtypeStruct((SPAN, width), F32),
+            jax.ShapeDtypeStruct((8, width), F32),
+        ]
+        + finals,
+        [
+            pltpu.VMEM((count + 1, SPAN, width), BF16),
+            pltpu.VMEM((SPAN, 128), F32),
+        ]
+        + scratch
+        + [pltpu.SemaphoreType.DMA((count,)), pltpu.SemaphoreType.DMA((count,))]
+        + line_sems(count, pieces)
+        + sems,
+    )
+
+
+SMALL_COLUMNS = 1280
+
+
+def sum_last_kernel(
+    sizes,
+    part,
+    stream,
+    gain,
+    outer,
+    left_in,
+    right_in,
+    left_out,
+    right_out,
+    small,
+    gain_grad_1,
+    grad,
+    halves_0,
+    halves_out_0,
+    smalls,
+    inbox,
+    gain_grad,
+    final,
+    out_final,
+    full,
+    got,
+    parts,
+    sums,
+    packed,
+    theirs,
+    dp_sum,
+    dp_slots,
+    *sems,
+):
+    ranks = {axis: lax.axis_index(axis) for axis in sizes}
+    core, rank, member = ranks["section"], ranks["seq"], ranks["dp"]
+    count, copies = sizes["seq"], sizes["dp"]
+    greet_all(sizes, ranks)
+    line = Line(count, rank, part, inbox, None, tuple(sems[:2]) + (None,) * 3)
+    flow = Flow(
+        sizes,
+        ranks,
+        left_in,
+        right_in,
+        left_out,
+        right_out,
+        final,
+        out_final,
+        (full, got, parts, sums),
+        sems[2:10],
+    )
+    square = Square(member, (final, out_final), (halves_0, halves_out_0), sems[10:13])
+    s_core_send, s_core_recv, s_dp_send, s_dp_recv, s_z_send, s_z_recv = sems[13:]
+    gain_grad[...] = jnp.zeros_like(gain_grad)
+
+    def own_piece(piece, total):
+        rows = pl.ds(pl.multiple_of(piece * PIECE, PIECE), PIECE)
+        back, gain_part = norm_back(stream[rows, :].astype(F32), gain[0:1, :], total)
+        gain_grad[0:1, :] += gain_part
+        grad[rows, :] = outer[rows, :].astype(F32) + back
+
+    def s_core_copy():
+        return push("section", 1 - core, packed, theirs, s_core_send, s_core_recv)
+
+    def s_dp_copy(step):
+        to = lax.rem(member + step, copies)
+        return push(
+            "dp", to, dp_sum, dp_slots.at[member], s_dp_send.at[step], s_dp_recv.at[member]
+        )
+
+    def s_z_copy(step):
+        to = lax.rem(rank + step, count)
+        return push(
+            "seq", to, smalls.at[rank], smalls.at[rank], s_z_send.at[step], s_z_recv.at[rank]
+        )
+
+    def after_own():
+        packed[...] = small[...]
+        wide = SMALL_COLUMNS - 256
+        for layer, source in ((0, gain_grad), (1, gain_grad_1)):
+            for row in range(source.shape[1] // 256):
+                packed[layer, row : row + 1, wide:] = source[0:1, row * 256 : (row + 1) * 256]
+        s_core_copy().start()
+
+    line.run(SPAN // PIECE, own_piece, None, after_own, flow, pace=2)
+    flow.finals_here(0)
+    s_core_copy().wait_recv()
+    dp_sum[...] = packed[...] + theirs[...]
+    flow.finals_given(0)
+
+    @pl.when(core == 0)
+    def _():
+        square.begin(0)
+        square.begin(1)
+
+    for step in range(1, copies):
+        s_dp_copy(step).start()
+    total = dp_sum[...]
+    for step in range(1, copies):
+        origin = lax.rem(member + step, copies)
+        place = dp_slots.at[origin]
+        push("dp", origin, place, place, s_dp_send.at[step], s_dp_recv.at[origin]).wait_recv()
+        total = total + dp_slots[origin]
+    smalls[rank] = total
+    for step in range(1, count):
+        s_z_copy(step).start()
+    for step in range(1, count):
+        origin = lax.rem(rank + step, count)
+        place = smalls.at[origin]
+        push("seq", origin, place, place, s_z_send.at[step], s_z_recv.at[origin]).wait_recv()
+
+    @pl.when(core == 0)
+    def _():
+        square.middle(0)
+        square.middle(1)
+        square.end(0)
+        square.end(1)
+
+    s_core_copy().wait_send()
+    for step in range(1, copies):
+        s_dp_copy(step).wait_send()
+    for step in range(1, count):
+        s_z_copy(step).wait_send()
+    flow.settle()
+
+
+def sum_last(part, stream, gain, outer, grads_of, small, gain_grad_1):
+    sizes = axis_sizes()
+    count, copies = sizes["seq"], sizes["dp"]
+    length, width = part.shape
+    pieces = SPAN // PIECE
+    left_in, right_in, left_out, right_out = grads_of
+    depth, inner, wide = width // count, left_out.shape[1], right_in.shape[1]
+    scratch, sems, finals = flow_shapes(sizes, depth, inner, width, wide)
+    dma = pltpu.SemaphoreType.DMA
+    halves = [jax.ShapeDtypeStruct((copies,) + f.shape, f.dtype) for f in finals]
+    small_shape = pltpu.VMEM((2, 8, SMALL_COLUMNS), F32)
+    operands = [
+        part, stream, gain, outer, left_in, right_in, left_out, right_out, small, gain_grad_1,
+    ]
+    return pl.pallas_call(
+        functools.partial(sum_last_kernel, sizes),
+        out_shape=[jax.ShapeDtypeStruct((SPAN, width), F32)]
+        + halves
+        + [jax.ShapeDtypeStruct((count, 2, 8, SMALL_COLUMNS), F32)],
+        in_specs=[IN_VMEM] * len(operands),
+        out_specs=[IN_VMEM] + [IN_HBM] * 2 + [IN_VMEM],
+        scratch_shapes=[
+            pltpu.VMEM((count + 1, SPAN, width), BF16),
+            pltpu.VMEM((8, width), F32),
+        ]
+        + [pltpu.VMEM(f.shape, f.dtype) for f in finals]
+        + scratch
+        + [small_shape, small_shape, small_shape, pltpu.VMEM((copies, 2, 8, SMALL_COLUMNS), F32)]
+        + line_sems(count, pieces)[:2]
+        + sems
+        + square_sems()
+        + [
+            dma,
+            dma,
+            dma((copies,)),
+            dma((copies,)),
+            dma((count,)),
+            dma((count,)),
         ],
-        axis=2,
-    ).transpose(1, 0, 2)
-    mine = lax.all_to_all(bundle, "seq", split_axis=0, concat_axis=0, tiled=True)
-    mine = mine.reshape(count * depth, -1)
-    in_both = both_layers(mine)
-    out_both = both_layers(out_weight[0])
-    small = jnp.concatenate(
-        [
-            conv_weight[0].reshape(-1),
-            conv_bias[0],
-            norm_gain[0],
-        ]
-    )
-    gathered = lax.all_gather(small, "seq", axis=0)
-    part = conv_bias.shape[1]
-    kernel = gathered[:, : TAPS * part].reshape(count, TAPS, part).transpose(1, 0, 2).reshape(TAPS, -1)
-    bias = gathered[:, TAPS * part : (TAPS + 1) * part].reshape(-1)
-    gain = gathered[:, (TAPS + 1) * part :].reshape(-1)
-    taps = jnp.concatenate([kernel, bias[None], jnp.zeros((3, bias.shape[0]), BF16)], axis=0)
-    own = jnp.concatenate([step_bias, decay_log, skip_gain], axis=0)
-    own = jnp.pad(own, ((0, 5), (0, 128 - heads)))
-    packed = [
-        lax.dynamic_slice_in_dim(taps, rank * inner, inner, 1).astype(F32),
-        taps[:, whole_inner:].astype(F32),
-        own.astype(F32),
-        jnp.broadcast_to(gate_gain, (8, inner)).astype(F32),
-        jnp.broadcast_to(gain[None], (8, gain.shape[0])).astype(F32),
-    ]
-    shared = [both_layers(array) for array in packed]
-    layers = []
-    for layer in range(2):
-        w = in_both[layer]
-        kx, kbc, head_rows, gain_rows, norm_gain_rows = (pair[layer] for pair in shared)
-        layers.append(
-            (
-                (
-                    w[:, :inner],
-                    w[:, inner : 2 * inner],
-                    w[:, 2 * inner : 2 * inner + 2 * STATE],
-                    w[:, 2 * inner + 2 * STATE :],
-                    kx,
-                    kbc,
-                    head_rows,
-                    gain_rows,
-                    out_both[layer],
-                ),
-                norm_gain_rows[0],
-            )
-        )
-    return layers
+        compiler_params=pltpu.CompilerParams(
+            collective_id=3, has_side_effects=True, vmem_limit_bytes=LINE_VMEM
+        ),
+        name="sum_last",
+    )(*operands)
+
+
+def grads_by_collectives(in_parts, out_part, inner):
+    core = lax.axis_index("section")
+    count = lax.axis_size("seq")
+
+    def to_core(pair):
+        theirs = other_core(jnp.where(core == 0, pair[1], pair[0]).astype(BF16))
+        return (jnp.where(core == 0, pair[0], pair[1]) + theirs.astype(F32)).astype(BF16)
+
+    gate, x, rest = (to_core(pair) for pair in in_parts)
+    out = to_core(out_part)
+    depth = gate.shape[0] // count
+
+    def rows_of(part):
+        part = part.reshape(count, depth, -1)
+        part = lax.all_to_all(part, "seq", split_axis=0, concat_axis=0, tiled=True)
+        return lax.psum(part, "dp").astype(F32)
+
+    gate, x, rest = rows_of(gate), rows_of(x), rows_of(rest)
+    columns = [part.transpose(1, 0, 2).reshape(depth, -1) for part in (gate, x)]
+    return jnp.concatenate(columns + [jnp.sum(rest, axis=0)], axis=1), lax.psum(out, "dp").astype(F32)
 
 
 def local(
@@ -715,139 +1972,132 @@
     gate_gain,
     out_weight,
 ):
+    sizes = axis_sizes()
     core = lax.axis_index("section")
     rank = lax.axis_index("seq")
-    count = lax.axis_size("seq")
+    count, copies = sizes["seq"], sizes["dp"]
     inner = out_weight.shape[1]
     heads = step_bias.shape[1]
     whole_inner = inner * count
-    layers = layer_weights(
-        in_weight, conv_weight, conv_bias, step_bias, decay_log, skip_gain, gate_gain, out_weight, norm_gain
-    )
-    stream = lax.dynamic_index_in_dim(hidden_in, core, 0, keepdims=False).astype(F32)
+    depth = in_weight.shape[1]
+    part = conv_bias.shape[1]
+    tokens = hidden_in.shape[1]
+    regular = inner % depth == 0 and depth % 128 == 0 and depth % (32 * copies) == 0 and copies == 4
+
+    gather = lambda array: lax.all_gather(array, "seq", axis=0, tiled=True)
+    stream = lax.dynamic_index_in_dim(hidden_in, core, 0, keepdims=False)
     outer = lax.dynamic_index_in_dim(cotangent, core, 0, keepdims=False)
     starts = lax.dynamic_index_in_dim(doc_starts, core, 0, keepdims=False)
-    tokens = stream.shape[0]
-
-    gather = lambda array: lax.all_gather(array, "seq", axis=0, tiled=True)
-    scatter = lambda array: lax.psum_scatter(array, "seq", scatter_dimension=0, tiled=True)
-    own_tokens = lambda row: lax.dynamic_slice_in_dim(row, rank * tokens, tokens, 0)
-
-    dh_whole = gather(outer)
-    normed_0 = gather(norm_rows(stream, layers[0][1]).astype(BF16))
-    fwd_0 = run_forward(starts, normed_0, layers[0][0])
-    square_0 = lax.psum(fwd_0[7][0], "seq")
-    scale_0 = lax.rsqrt(square_0 / whole_inner + EPSILON)
-    product_0 = scatter(fwd_0[6]).astype(F32) * own_tokens(scale_0)[:, None]
-    hidden_1 = (stream + product_0).astype(BF16)
-    stream_1 = hidden_1.astype(F32)
-    normed_1 = gather(norm_rows(stream_1, layers[1][1]).astype(BF16))
-    fwd_1 = run_forward(starts, normed_1, layers[1][0], dh_whole)
-    sums_1 = lax.psum(fwd_1[7][:2], "seq")
-    scale_1 = lax.rsqrt(sums_1[0] / whole_inner + EPSILON)
-    stats_1 = jnp.concatenate(
-        [scale_1[None], (sums_1[1] * scale_1 / whole_inner)[None], jnp.zeros((6, scale_1.shape[0]), F32)]
+    small = small_rows(conv_weight, conv_bias, norm_gain)
+    if regular:
+        normed_0, columns, out_rows, smalls = start(
+            small, hidden_in, column_bundle(in_weight, inner), out_weight
+        )
+        normed_0 = normed_0.reshape(count * tokens, -1)
+        columns = [[(columns, of_layer(columns, layer))] for layer in range(2)]
+        out_rows = [(out_rows, of_layer(out_rows, layer)) for layer in range(2)]
+    else:
+        smalls = lax.all_gather(lax.all_gather(small, "seq", axis=0), "section", axis=0)
+        columns = columns_by_collectives(in_weight, inner)
+        out_rows = [(array, whole(array)) for array in both_layers(out_weight[0])]
+    facts = layer_facts(smalls, step_bias, decay_log, skip_gain, gate_gain, part, depth)
+    gains = [fact[4] for fact in facts]
+    if not regular:
+        normed_0 = gather(norm_rows(stream.astype(F32), gains[0][0:1]).astype(BF16))
+    layers = [(columns[layer],) + facts[layer][:4] + (out_rows[layer],) for layer in range(2)]
+
+    outer_after, normed_0 = lax.optimization_barrier((outer, normed_0))
+    dh_whole = gather(outer_after)
+    fwd_0 = run_forward(starts, normed_0, layers[0])
+    normed_1, scales_0, hidden_1, product_0 = sum_forward(
+        fwd_0[6], fwd_0[7], stream, gains[1], whole_inner
     )
-    hidden_2 = (
-        stream_1 + scatter(fwd_1[6]).astype(F32) * own_tokens(scale_1)[:, None]
-    ).astype(BF16)
-
-    def weight_grads(normed, dh, back):
-        return (
-            jnp.concatenate([mm_tn(normed, part) for part in back[:4]], axis=1).astype(BF16),
-            mm_tn(back[4], dh).astype(BF16),
-        )
-
-    back_1 = run_backward(starts, dh_whole, stats_1, layers[1][0], fwd_1[:6])
-    dnormed_1 = scatter(back_1[5]).astype(F32)
-    through_1, gain_grad_1 = norm_back(stream_1, layers[1][1], dnormed_1)
-    input_grad_1 = outer.astype(F32) + through_1
-    dh_low = input_grad_1.astype(BF16)
-    mean_0 = jnp.sum(dh_low.astype(F32) * product_0, axis=1) / whole_inner
-    dh_0 = gather(dh_low)
-    means_0 = gather(mean_0)
-    stats_0 = jnp.concatenate([scale_0[None], means_0[None], jnp.zeros((6, scale_0.shape[0]), F32)])
-    back_0 = run_backward(starts, dh_0, stats_0, layers[0][0], fwd_0[:6])
-    dnormed_0 = scatter(back_0[5]).astype(F32)
-    through_0, gain_grad_0 = norm_back(stream, layers[0][1], dnormed_0)
-    input_grad_0 = dh_low.astype(F32) + through_0
-
-    grads_1 = weight_grads(normed_1, dh_whole, back_1)
-    grads_0 = weight_grads(normed_0, dh_0, back_0)
-
-    def to_core(pair):
-        theirs = other_core(jnp.where(core == 0, pair[1], pair[0]))
-        return jnp.where(core == 0, pair[0], pair[1]).astype(F32) + theirs.astype(F32)
-
-    in_grad = to_core((grads_0[0], grads_1[0])).astype(BF16)
-    out_grad = to_core((grads_0[1], grads_1[1])).astype(BF16)
-    depth = in_weight.shape[1]
-    in_grad = lax.all_to_all(
-        in_grad.reshape(count, depth, -1), "seq", split_axis=0, concat_axis=0, tiled=True
+    normed_1 = normed_1.reshape(normed_0.shape)
+    fwd_1 = run_forward(starts, normed_1, layers[1], dh_whole)
+    scales_1, means_1 = sum_stats(fwd_1[7], whole_inner)
+
+    back_1 = run_backward(starts, dh_whole, scales_1, means_1, layers[1], fwd_1[:6])
+    kinds = len(columns[0])
+    gated_1, dnormed_1 = back_1[kinds : kinds + 2]
+    grads_of = (normed_1, back_1[0], gated_1, dh_whole) if regular else None
+    dh_0, means_0, input_grad_1, gain_grad_1, *mine_1 = sum_backward(
+        dnormed_1, hidden_1, gains[1], outer, product_0, whole_inner, grads_of
     )
-    in_grad = lax.psum(in_grad, "dp")
-    out_grad = lax.psum(out_grad, "dp")
-    in_grad = in_grad.astype(F32)
-    grad_in_weight = jnp.concatenate(
-        [
-            in_grad[:, :, :inner].transpose(1, 0, 2).reshape(depth, whole_inner),
-            in_grad[:, :, inner : 2 * inner].transpose(1, 0, 2).reshape(depth, whole_inner),
-            jnp.sum(in_grad[:, :, 2 * inner : 2 * inner + 2 * STATE], axis=0),
-            in_grad[:, :, 2 * inner + 2 * STATE : 2 * inner + 2 * STATE + heads]
-            .transpose(1, 0, 2)
-            .reshape(depth, heads * count),
-        ],
-        axis=1,
+    own_dh_0 = lax.dynamic_index_in_dim(dh_0, rank, 0, keepdims=False)
+    part_1, dh_0 = lax.optimization_barrier((fwd_1[6].astype(BF16), dh_0))
+    product_1 = lax.psum_scatter(part_1, "seq", scatter_dimension=0, tiled=True)
+    own_scale = lax.dynamic_index_in_dim(scales_1, rank, 0, keepdims=False)[0]
+    hidden_2 = (hidden_1.astype(F32) + product_1.astype(F32) * own_scale[:, None]).astype(BF16)
+    dh_0 = dh_0.reshape(dh_whole.shape)
+    back_0 = run_backward(starts, dh_0, scales_0, means_0, layers[0], fwd_0[:6], mine_1)
+    gated_0, dnormed_0 = back_0[kinds : kinds + 2]
+
+    def packed(back):
+        gx, gbc, gheads = back[kinds + 2 : kinds + 5]
+        rest = jnp.concatenate([gbc[:5], jnp.pad(gheads[:2], ((0, 0), (0, 128))), gbc[7:]], axis=0)
+        return jnp.concatenate([gx, rest, jnp.zeros((8, 256), F32)], axis=1)
+
+    small_grads = jnp.stack([packed(back_0), packed(back_1)])
+    if regular:
+        grads_of = (normed_0, back_0[0], gated_0, dh_0)
+        input_grad_0, halves_0, halves_out_0, smalls = sum_last(
+            dnormed_0, stream, gains[0], own_dh_0, grads_of, small_grads, gain_grad_1
+        )
+        halves_1, halves_out_1 = back_0[-2:]
+        halves = jnp.where(core == 0, halves_0, halves_1)
+        halves_out = jnp.where(core == 0, halves_out_0, halves_out_1)
+
+        def side_by_side(low, high):
+            wide = halves[..., low:high].transpose(1, 0, 3, 2, 4)
+            return wide.reshape(depth, -1).astype(F32)
+
+        rest = jnp.sum(halves[..., 2 * inner :].astype(F32), axis=2).transpose(1, 0, 2, 3)
+        rest = rest.reshape(depth, -1)
+        grad_in = jnp.concatenate(
+            [side_by_side(0, inner), side_by_side(inner, 2 * inner), rest], axis=1
+        )
+        grad_out = halves_out.transpose(2, 1, 0, 3, 4).reshape(inner, -1).astype(F32)
+    else:
+        input_grad_0, gain_grad_0 = sum_plain(dnormed_0, stream, gains[0], own_dh_0)
+        pairs = [
+            (mm_tn(normed_0, back_0[kind]), mm_tn(normed_1, back_1[kind])) for kind in range(kinds)
+        ]
+        grad_in, grad_out = grads_by_collectives(
+            pairs, (mm_tn(gated_0, dh_0), mm_tn(gated_1, dh_whole)), inner
+        )
+        gain_rows = jnp.stack([gain_grad_0[0], gain_grad_1[0]]).reshape(2, -1, 256)
+        small_grads = small_grads.at[:, : gain_rows.shape[1], inner + 256 :].set(gain_rows)
+        smalls = lax.all_gather(lax.psum(small_grads, ("section", "dp")), "seq", axis=0)
+    grad_in = grad_in[:, : in_weight.shape[2]]
+
+    mine = lax.dynamic_index_in_dim(smalls, core, 1, keepdims=False)
+    x_part = mine[:, :5, :inner].transpose(1, 0, 2).reshape(5, whole_inner)
+    bc_part = jnp.sum(mine[:, :5, inner : inner + 256], axis=0)
+    channels = lax.dynamic_slice_in_dim(
+        jnp.concatenate([x_part, bc_part], axis=1), rank * part, part, 1
     )
-
-    def small(back, gain_grad):
-        gx, gbc, gheads = back[6:9]
-        channels = jnp.concatenate(
-            [
-                lax.dynamic_update_slice_in_dim(
-                    jnp.zeros((TAPS + 1, whole_inner), F32), gx[: TAPS + 1], rank * inner, 1
-                ),
-                gbc[: TAPS + 1],
-            ],
-            axis=1,
-        )
-        own = jnp.concatenate(
-            [
-                gheads[0, :heads],
-                gheads[1, :heads],
-                jnp.sum(gx[TAPS + 1].reshape(heads, HEAD), axis=1),
-                gx[TAPS + 2],
-            ]
-        )
-        return channels, gain_grad, own
-
-    channels, norm_grad, own = (
-        to_core(pair)
-        for pair in zip(small(back_0, gain_grad_0), small(back_1, gain_grad_1))
-    )
-    channels, norm_grad = lax.psum((channels, norm_grad), ("dp", "seq"))
-    own = lax.psum(own, "dp")
-    part = conv_bias.shape[1]
-    channels = lax.dynamic_slice_in_dim(channels, rank * part, part, 1)
+    gain_rows = norm_gain.shape[1] * count // 256
+    norm_grad = jnp.sum(mine[:, :gain_rows, inner + 256 :], axis=0).reshape(-1)
     norm_grad = lax.dynamic_slice_in_dim(norm_grad, rank * norm_gain.shape[1], norm_gain.shape[1], 0)
+    own = lax.dynamic_index_in_dim(mine, rank, 0, keepdims=False)
 
     def by_layer(first, second):
-        mine = jnp.where(core == 0, first, second)
+        kept = jnp.where(core == 0, first, second)
         theirs = other_core(jnp.where(core == 0, second, first))
-        return jnp.stack([jnp.where(core == 0, mine, theirs), jnp.where(core == 0, theirs, mine)])
+        return jnp.stack([jnp.where(core == 0, kept, theirs), jnp.where(core == 0, theirs, kept)])
 
     return (
         by_layer(hidden_1, hidden_2)[None],
         by_layer(input_grad_0, input_grad_1)[None],
         norm_grad[None],
-        grad_in_weight[None],
+        grad_in[None],
         channels[None, :TAPS],
         channels[TAPS:],
-        own[None, :heads],
-        own[None, heads : 2 * heads],
-        own[None, 2 * heads : 3 * heads],
-        own[None, 3 * heads :],
-        out_grad.astype(F32)[None],
+        own[5:6, inner : inner + heads],
+        own[6:7, inner : inner + heads],
+        jnp.sum(own[5, :inner].reshape(1, heads, HEAD), axis=2),
+        own[6:7, :inner],
+        grad_out[None],
     )
 
 

time: 1290 us -> 789 us (0.61)
  waiting for transfers between devices: 702 us -> 0.07 us
  Pallas kernels: 146 us -> 677 us
  blocking collectives: 235 us -> 0 us
  other arithmetic: 75.2 us -> 27 us
  matrix products: 31.2 us -> 0 us
    pallas_call x2 -> x7, Pallas kernels: 91.9 us -> 620 us  [the longest x3 267 us: line_call(): pl.pallas_call(kernel, out_shape=out_shape, in_specs=[IN_VMEM] * len(oper...]
    psum x2 -> x0, waiting for transfers between devices: 198 us -> none  [the longest x1 125 us: local(): in_grad = lax.psum(in_grad, 'dp')]
    all_gather x4 -> x1, waiting for transfers between devices: 196 us -> 0.02 us  [local(): gather = lambda array: lax.all_gather(array, 'seq', axis=0, tiled=True)]
    all_to_all x1 -> x0, waiting for transfers between devices: 182 us -> none  [local(): lax.all_to_all(in_grad.reshape(count, depth, -1), 'seq', split_axis=0, co...]
    all_to_all x1 -> x0, blocking collectives: 136 us -> none  [layer_weights(): lax.all_to_all(bundle, 'seq', split_axis=0, concat_axis=0, tiled=True)]
    reduce_scatter x4 -> x1, waiting for transfers between devices: 106 us -> 0.01 us  [local(): product_1 = lax.psum_scatter(part_1, 'seq', scatter_dimension=0, tiled=True)]
    psum x4 -> x0, blocking collectives: 71.4 us -> none  [the longest x1 42.4 us: local(): channels, norm_grad = lax.psum((channels, norm_grad), ('dp', 'seq'))]
    dot_general x10 -> x0, matrix products: 31.2 us -> none  [mm_tn(): lax.dot_general(a, b, (((0,), (0,)), ((), ())), preferred_element_type=F32)]
  transfers between devices with their start and end apart: 25 -> 6, of which waited for: 15 -> 0; matrix products, arithmetic and copies ran while one was open for 8% -> 7% of each run, Pallas kernels for 0% -> 44%
where the time goes in v2:
time: 789 us; the launch traced here: 779 us
  Pallas kernels  677 us (86%)
  local copies, waits for them, and re-layouts  58.5 us (7%)
  other arithmetic  27 us (3%)
  between operations  15.1 us (2%)
    pallas_call x3, Pallas kernels, line_call(): pl.pallas_call(kernel, out_shape=out_shape, in_specs=[IN_VMEM] * len(oper...  267 us
    pallas_call x1, Pallas kernels, sum_last(): pl.pallas_call(functools.partial(sum_last_kernel, sizes), out_shape=[jax....  152 us
    pallas_call x1, Pallas kernels, start(): pl.pallas_call(functools.partial(start_kernel, sizes), out_shape=[jax.Sha...  106 us
    pallas_call x2, Pallas kernels, run_backward(): pl.pallas_call(functools.partial(backward_kernel, bool(carried), length),...  94.7 us
    pallas_call x2, Pallas kernels, run_forward(): pl.pallas_call(functools.partial(forward_kernel, dh is not None, length),...  56.9 us
    unnamed x82, local copies, waits for them, and re-layouts  32.6 us
  transfers between devices with their start and end apart: 6, of which 0 were waited for; matrix products, arithmetic and copies ran while one was open for 7% of the time, Pallas kernels for 44%

profile of v2, /device:TPU:0, one launch (start us, length us, event | category | flops | bytes accessed | tf_op | source)
XLA Modules:
  0.0 779.1 jit_solution(3170897655727232306)
XLA Ops:
  7.2 2.6 constant_dynamic-slice_fusion.3
  9.9 2.0 copy.46
  11.9 0.9 slice.127
  12.8 1.3 fusion.30
  14.3 1.0 dynamic-slice_bitcast_fusion.2.outer
  16.1 1.2 pad_maximum_fusion.2.bundle
  17.3 106.3 %start.1 = (bf16[4,256,1536]{2,1,0:T(8,128)(2,1)}, bf16[2,1536,1920]{2,1,0:T(8,128)(2,1)}, bf16[2,768,1536]{2,1,0:T(8,128)(2,1)}, f32[2,4,8,896]{3,2,1,0:T(8,128)}) custom-call(f32[8,896]{1,0:T(8,128)} %maximum_maximum_fusion.small, bf16[2,256,1536]{2,1,0:T(8,128)(2,1)} %hidden.1, bf16[4,96,1920]{2,1,0:T(8,128)(2,1)} %pad_maximum_fusion.2.bundle, ...), custom_call_target="tpu_custom_call" | custom-call | tf_op jit(solution)/shard_map/start/pallas_call | solution.py:1294
  124.4 1.0 slice_bitcast_fusion.2
  125.8 1.0 dynamic-slice_bitcast_fusion.1.stream
  126.9 27.1 %layer_forward.2 = (bf16[1024,768]{1,0:T(8,128)(2,1)S(1)}, bf16[1024,768]{1,0:T(8,128)(2,1)S(1)}, bf16[1024,256]{1,0:T(8,128)(2,1)S(1)}, f32[1024,128]{1,0:T(8,1...) custom-call(s32[4]{0:T(128)S(1)} %fusion.29.starts_ref, ...), custom_call_target="tpu_custom_call" | custom-call | flops 8455716864 | bytes 25165824 | tf_op jit(solution)/shard_map/layer_forward/pallas_call | solution.py:551
  154.6 1.1 copy-done.13
  155.7 1.2 copy-done.14
  156.9 0.9 copy-done.17
  158.6 0.8 copy-done.21
  160.0 117.8 %sum_forward.1 = (bf16[4,256,1536]{2,1,0:T(8,128)(2,1)}, f32[4,8,256]{2,1,0:T(8,128)}, bf16[256,1536]{1,0:T(8,128)(2,1)}, f32[256,1536]{1,0:T(8,128)}) custom-call(f32[1024,1536]{1,0:T(8,128)} %get-tuple-element.70.part, f32[8,1024]{1,0:T(8,128)} %copy-done.4, bf16[256,1536]{1,0:T(8,128)(2,1)} %dynamic-slice_bitcast_fusion.1.stream, ...), custom_call_target="tpu_custom_call" | custom-call | tf_op jit(solution)/shard_map/sum_forward/pallas_call | solution.py:972
  277.9 29.9 %layer_forward.3 = (bf16[1024,768]{1,0:T(8,128)(2,1)S(1)}, bf16[1024,768]{1,0:T(8,128)(2,1)S(1)}, bf16[1024,256]{1,0:T(8,128)(2,1)S(1)}, f32[1024,128]{1,0:T(8,1...) custom-call(s32[4]{0:T(128)S(1)} %fusion.29.starts_ref, ...), custom_call_target="tpu_custom_call" | custom-call | flops 8455716864 | bytes 25165824 | tf_op jit(solution)/shard_map/layer_forward/pallas_call | solution.py:551
  308.4 1.1 copy-done.12
  309.6 0.8 copy-done.15
  310.3 4.8 convert_element_type.76
  315.1 7.2 sum_stats.1
  323.8 1.0 copy-done.16
  324.9 46.2 %layer_backward.2 = (bf16[1024,1920]{1,0:T(8,128)(2,1)}, bf16[1024,768]{1,0:T(8,128)(2,1)S(1)}, f32[1024,1536]{1,0:T(8,128)}, f32[8,768]{1,0:T(8,128)S(1)}, f32[8,256]{1,0:T(8,128)S(1)}, /*index=5*/f32[8,128]{1,0:T(8,128)S(1)}) custom-call(s32[4]{0:T(128)S(1)} %fusion.29.starts_ref, bf16[1024,1536]{1,0:T(8,128)(2,1)} %all-gather.2.cloned.1.call-done.rest_1_.dh_ref.rest_3_, ...), custom_call_target="tpu_custom_call" | custom-call | flops 16911433728 | bytes 25165824 | tf_op jit(solution)/shard_map/layer_backward/pallas_call | solution.py:623
  371.1 1.1 copy-done.3
  372.3 142.5 %sum_backward.1 = (bf16[4,256,1536]{2,1,0:T(8,128)(2,1)}, f32[4,8,256]{2,1,0:T(8,128)}, f32[256,1536]{1,0:T(8,128)}, f32[8,1536]{1,0:T(8,128)}, bf16[2,4,48,1920...) custom-call(f32[1024,1536]{1,0:T(8,128)} %get-tuple-element.85.part, bf16[256,1536]{1,0:T(8,128)(2,1)} %get-tuple-element.72.stream, ...), custom_call_target="tpu_custom_call" | custom-call | tf_op jit(solution)/shard_map/sum_backward/pallas_call | solution.py:972
  514.8 1.3 copy-done.7
  516.5 1.0 copy-done.20
  517.6 1.0 copy-done.22
  518.6 48.5 %layer_backward.3 = (bf16[1024,1920]{1,0:T(8,128)(2,1)}, bf16[1024,768]{1,0:T(8,128)(2,1)S(1)}, f32[1024,1536]{1,0:T(8,128)}, f32[8,768]{1,0:T(8,128)S(1)}, f32[...) custom-call(s32[4]{0:T(128)S(1)} %fusion.29.starts_ref, ...), custom_call_target="tpu_custom_call" | custom-call | flops 16911433728 | bytes 25165824 | tf_op jit(solution)/shard_map/layer_backward/pallas_call | solution.py:623
  567.1 1.1 copy-done.2
  568.9 2.1 dynamic-slice_bitcast_fusion.outer
  571.6 151.7 %sum_last.1 = (f32[256,1536]{1,0:T(8,128)}, bf16[4,2,4,48,1920]{4,3,2,1,0:T(8,128)(2,1)}, bf16[4,2,2,48,1536]{4,3,2,1,0:T(8,128)(2,1)}, f32[4,2,8,1280]{3,2,1,0:T(8,128)}) custom-call(f32[1024,1536]{1,0:T(8,128)} %get-tuple-element.102.part, bf16[256,1536]{1,0:T(8,128)(2,1)} %dynamic-slice_bitcast_fusion.1.stream, f32[8,1536]{1,0:T(8,128)} %broadcast_in_dim.51.gain, ...), custom_call_target="tpu_custom_call" | custom-call | tf_op jit(solution)/shard_map/sum_last/pallas_call | solution.py:1907
  723.3 0.8 dynamic-slice_bitcast_fusion.4
  725.4 0.9 dynamic-slice_bitcast_fusion.3
  727.7 3.4 broadcast_select_fusion
  731.4 1.2 copy-done.24
  732.5 1.4 broadcast_select_fusion.1
  733.9 1.3 convert_bitcast_fusion.2
  735.2 3.0 copy.41
  738.2 1.0 copy.49
  739.2 3.0 copy.42
  742.3 1.0 copy.50
  743.3 5.1 fusion
  748.8 2.6 copy.44
  751.4 10.7 %copy.45 = f32[1,384,6448]{1,2,0:T(8,128)} copy(f32[1,384,6448]{2,1,0:T(8,128)} %fusion) | data formatting | bytes 19808256
  764.0 1.6 fusion.1
  766.2 1.9 select_bitcast_fusion.1
  768.1 1.9 maximum_bitcast_fusion
  770.6 1.3 maximum_bitcast_fusion.1
  (135 shorter events, 14.4 us)
Async XLA Ops:
  7.2 7.1 copy-start
  7.2 270.7 %all-gather.2.cloned.1.call-start = ((), (), s32[]{:S(2)}) async-start(), calls=%async_computation.1 | async-start | bytes 3932160 | tf_op jit(solution)/shard_map/all_gather | solution.py:1987
  9.9 4.3 copy-start.37
  9.9 4.4 copy-start.31
  9.9 4.3 copy-start.32
  17.3 106.4 %copy-start.34 = (bf16[1,12]{1,0:T(2,128)(2,1)S(1)}, bf16[1,12]{1,0:T(2,128)(2,1)}, u32[]{:S(2)}) copy-start(bf16[1,12]{1,0:T(2,128)(2,1)} %param.21) | copy-start | bytes 76
  17.3 106.4 %copy-start.35 = (bf16[1,12]{1,0:T(2,128)(2,1)S(1)}, bf16[1,12]{1,0:T(2,128)(2,1)}, u32[]{:S(2)}) copy-start(bf16[1,12]{1,0:T(2,128)(2,1)} %param.20) | copy-start | bytes 76
  17.3 106.4 %copy-start.36 = (bf16[1,12]{1,0:T(2,128)(2,1)S(1)}, bf16[1,12]{1,0:T(2,128)(2,1)}, u32[]{:S(2)}) copy-start(bf16[1,12]{1,0:T(2,128)(2,1)} %param.19) | copy-start | bytes 76
  17.3 106.9 %copy-start.33 = (bf16[1,768]{1,0:T(2,128)(2,1)S(1)}, bf16[1,768]{1,0:T(2,128)(2,1)}, u32[]{:S(2)}) copy-start(bf16[1,768]{1,0:T(2,128)(2,1)} %param.22) | copy-start | bytes 4612
  123.6 2.3 copy-start.27
  123.6 3.2 copy-start.38
  123.6 640.3 %reduce-scatter.2.cloned.1.call-start = ((), (), s32[]{:S(2)}) async-start(), calls=%async_computation.2 | async-start | bytes 3932160 | tf_op jit(solution)/shard_map/reduce_scatter | solution.py:2028
  123.7 3.2 collective-permute-start
  124.2 2.7 collective-permute-start.1
  154.0 0.6 copy-start.4
  154.6 1.1 copy-start.13
  155.7 1.2 copy-start.14
  156.9 0.9 copy-start.17
  157.8 0.8 copy-start.19
  158.6 0.8 copy-start.21
  307.8 0.6 copy-start.5
  308.4 1.1 copy-start.12
  309.5 0.8 copy-start.15
  322.3 0.8 copy-start.6
  323.1 0.8 copy-start.11
  323.8 1.0 copy-start.16
  371.1 1.1 copy-start.3
  514.7 1.4 copy-start.7
  514.7 1.5 copy-start.8
  514.7 1.5 copy-start.9
  514.8 1.5 copy-start.10
  514.8 1.7 copy-start.18
  516.5 1.0 copy-start.20
  517.6 1.0 copy-start.22
  567.1 1.1 copy-start.2
  727.7 3.6 copy-start.25
  731.1 1.4 copy-start.24
  733.9 32.2 %collective-permute-start.3 = (f32[256,1536]{1,0:T(8,128)}, f32[256,1536]{1,0:T(8,128)}, u32[]{:S(2)}, u32[]{:S(2)}) collective-permute-start(f32[256,1536]{1,0:T(8,128)} %broadcast_select_fusion.1), channel_id=1, source_target_pairs={{0,16},{16,0},{1,17},{17,1},{2,18},{18,2},{3,19},{19,3},{4,20},{20... | collective-permute-start | bytes 4718600 | tf_op jit(solution)/shard_map/ppermute | solution.py:1052
  743.2 5.1 copy-start.29
  743.3 5.2 copy-start.30
  751.4 12.6 %copy-start.23 = (bf16[256,1536]{1,0:T(8,128)(2,1)S(1)}, bf16[256,1536]{1,0:T(8,128)(2,1)}, u32[]{:S(2)}) copy-start(bf16[256,1536]{1,0:T(8,128)(2,1)} %get-tuple-element.72.stream) | copy-start | bytes 2359300
  763.9 2.2 copy-start.26
  765.6 4.4 collective-permute-start.2
  768.0 1.9 copy-start.28
  769.9 1.9 copy-start.1
Sparse Core Ops, SparseCore 0:
  123.7 77.6 all-gather.1
  514.9 58.3 reduce-scatter.1

commit v3 on v2

--- a/solution.py
+++ b/solution.py
@@ -113,6 +113,9 @@
 def own_heads(columns, heads, sign):
     shift = lax.rem(128 + sign * heads * lax.axis_index("seq"), 128)
     return pltpu.roll(columns, shift, 1)
+
+
+TOTAL, DELTA, GROWN, ENDING, BEFORE = 0, 1, 2, 3, 4
 
 
 def forward_kernel(
@@ -237,68 +240,26 @@
     stat_ref[...] = jnp.transpose(both)[0:8, :]
 
 
-def carry_on(sources, slots, sems):
-    turn, turns = pl.program_id(0), pl.num_programs(0)
-    copies = lax.axis_size("dp")
-    member = lax.axis_index("dp")
-    square = Square(member, sources, slots, sems)
-    holds = lax.axis_index("section") == 1
-
-    @pl.when(turn == 0)
-    def _():
-        greet_all({"dp": copies}, {"dp": member})
-
-    for when, stage in ((0, square.begin), (turns // 2, square.middle), (turns - 1, square.end)):
-
-        @pl.when((turn == when) & holds)
-        def _():
-            stage(0)
-            stage(1)
-
-
-def backward_kernel(
-    carries,
-    length,
-    starts_ref,
-    dh_ref,
-    scale_ref,
-    mean_ref,
-    kx_ref,
-    kbc_ref,
-    heads_ref,
-    gain_ref,
-    wo_ref,
-    gate_ref,
-    x_ref,
-    xh_ref,
-    bc_ref,
-    bch_ref,
-    dt_ref,
-    scan_ref,
-    state_ref,
-    *rest,
+BACKWARD_STEPS = 5
+AFTER, SCALE, MEAN, DTOTAL, DDELTA = 7, 10, 11, 12, 13
+
+
+def backward_steps(
+    step, is_last, block, length, starts_ref, dh, stat_refs, small_refs, weight_refs, wo_ref,
+    saved_refs, grad_refs, sum_refs, scratch, finish,
 ):
+    scale_ref, mean_ref = stat_refs
+    kx_ref, kbc_ref, heads_ref, gain_ref = small_refs
+    gate_ref, x_ref, xh_ref, bc_ref, bch_ref, dt_ref, scan_ref, state_ref = saved_refs
+    dgate_ref, dx_ref, dbc_ref, gated_ref = grad_refs
+    gx_ref, gbc_ref, gheads_ref = sum_refs
+    (
+        ext_x, ext_bc, ext_dx, ext_dbc, dmemory, columns, total_rows, squares, dgated_ref, pair_ref,
+        c_flip_ref, dpair_ref, dlast_ref,
+    ) = scratch
     inner = kx_ref.shape[1]
-    wg_ref, wx_ref, wbc_ref, rest = split_weights(inner, rest)
-    if carries:
-        sources, rest = rest[:2], rest[2:]
-    dgate_ref, dx_ref, dbc_ref, rest = split_weights(inner, rest)
-    gated_ref, dnormed_ref, gx_ref, gbc_ref, gheads_ref, *rest = rest
-    if carries:
-        slots, sems, rest = rest[:2], rest[-3:], rest[2:-3]
-        carry_on(sources, slots, sems)
-    (
-        ext_x,
-        ext_bc,
-        ext_dx,
-        ext_dbc,
-        dmemory,
-        dscore,
-    ) = rest
-    blocks = pl.num_programs(0)
-    block = blocks - 1 - pl.program_id(0)
-
-    @pl.when(pl.program_id(0) == 0)
+
+    @pl.when((step == 0) & is_last)
     def _():
         ext_dx[...] = jnp.zeros_like(ext_dx)
         ext_dbc[...] = jnp.zeros_like(ext_dbc)
@@ -307,59 +268,68 @@
         gbc_ref[...] = jnp.zeros_like(gbc_ref)
         gheads_ref[...] = jnp.zeros_like(gheads_ref)
 
-    @pl.when(pl.program_id(0) > 0)
+    @pl.when((step == 0) & jnp.logical_not(is_last))
     def _():
         ext_dx[SPAN : SPAN + 8, :] = ext_dx[0:8, :]
         ext_dbc[SPAN : SPAN + 8, :] = ext_dbc[0:8, :]
 
-    ext_x[0:8, :] = xh_ref[8:16, :].astype(F32)
-    ext_x[8 : SPAN + 8, :] = x_ref[...].astype(F32)
-    ext_bc[0:8, :] = bch_ref[8:16, :].astype(F32)
-    ext_bc[8 : SPAN + 8, :] = bc_ref[...].astype(F32)
-
-    doc_col, column, before, same_square, carried, to_last = block_facts(starts_ref, block, length)
-    after = []
-    for lag in range(1, TAPS):
-        same = (doc_of(starts_ref, column + lag) == doc_col) & (column + lag < length)
-        after.append(same.astype(F32))
-    row, col = lower_ones()
-    lower = (row >= col).astype(F32)
-    upper = (row <= col).astype(F32)
-    keep = jnp.where(same_square & (row <= col), 0.0, FAR)
-
-    dt = dt_ref[...] + heads_ref[0:1, :]
-    delta = softplus(dt)
-    slope = -jnp.exp(heads_ref[1:2, :])
-    rate = slope * delta
-    total = exact(lower, rate)
-    total_rows = jnp.transpose(total)
-    grown = carried * jnp.exp(total)
-    last_total = total[SPAN - 1 : SPAN, :]
-    ending = to_last * jnp.exp(last_total - total)
-    carry_last = grown[SPAN - 1 : SPAN, :]
-
-    kbc = kbc_ref[...]
-    b_conv = taps_sum(ext_bc, 0, STATE, before, kbc, kbc[TAPS : TAPS + 1])
-    c_conv = taps_sum(ext_bc, STATE, 2 * STATE, before, kbc, kbc[TAPS : TAPS + 1])
-    b_sig = sigmoid(b_conv)
-    c_sig = sigmoid(c_conv)
-    b_low = (b_conv * b_sig).astype(BF16)
-    c_low = (c_conv * c_sig).astype(BF16)
-    scores = mm_nt(b_low, c_low)
-    c_flip = jnp.transpose(c_low.astype(F32)).astype(BF16)
-
-    stat_cols = row_to_columns(scale_ref[0, 0:1, :])
-    mean_cols = row_to_columns(mean_ref[0, 0:1, :])
-    dgated = mm_nt(dh_ref[...], wo_ref[...])
-    dscore[...] = jnp.zeros_like(dscore)
-    kx = kx_ref[...]
-    db = jnp.zeros((SPAN, STATE), F32)
-    dc = jnp.zeros((SPAN, STATE), F32)
-    dtotal = jnp.zeros((SPAN, 128), F32)
-    ddelta = jnp.zeros((SPAN, 128), F32)
-    dlast = jnp.zeros((8, 128), F32)
-    for tile, (low, high) in enumerate(tiles_of(inner)):
+    def convs(before):
+        kbc = kbc_ref[...]
+        return [
+            taps_sum(ext_bc, low, low + STATE, before, kbc, kbc[TAPS : TAPS + 1])
+            for low in (0, STATE)
+        ]
+
+    def before_rows():
+        return [columns[BEFORE + lag] for lag in range(TAPS - 1)]
+
+    @pl.when(step == 0)
+    def _():
+        ext_x[0:8, :] = xh_ref[8:16, :].astype(F32)
+        ext_x[8 : SPAN + 8, :] = x_ref[...].astype(F32)
+        ext_bc[0:8, :] = bch_ref[8:16, :].astype(F32)
+        ext_bc[8 : SPAN + 8, :] = bc_ref[...].astype(F32)
+        doc_col, column, before, same_square, carried, to_last = block_facts(
+            starts_ref, block, length
+        )
+        for lag in range(1, TAPS):
+            same = (doc_of(starts_ref, column + lag) == doc_col) & (column + lag < length)
+            columns[AFTER + lag - 1] = same.astype(F32)
+            columns[BEFORE + lag - 1] = before[lag - 1]
+        row, col = lower_ones()
+        squares[0] = jnp.where(same_square & (row <= col), 0.0, FAR)
+        delta = softplus(dt_ref[...] + heads_ref[0:1, :])
+        total = exact((row >= col).astype(F32), -jnp.exp(heads_ref[1:2, :]) * delta)
+        total_rows[...] = jnp.transpose(total)
+        columns[TOTAL] = total
+        columns[DELTA] = delta
+        columns[GROWN] = carried * jnp.exp(total)
+        columns[ENDING] = to_last * jnp.exp(total[SPAN - 1 : SPAN, :] - total)
+        columns[SCALE] = row_to_columns(scale_ref[0, 0:1, :])
+        columns[MEAN] = row_to_columns(mean_ref[0, 0:1, :])
+        columns[DTOTAL] = jnp.zeros((SPAN, 128), F32)
+        columns[DDELTA] = jnp.zeros((SPAN, 128), F32)
+        dlast_ref[...] = jnp.zeros_like(dlast_ref)
+        b_conv, c_conv = convs(before)
+        b_low = (b_conv * sigmoid(b_conv)).astype(BF16)
+        c_low = (c_conv * sigmoid(c_conv)).astype(BF16)
+        pair_ref[0] = b_low
+        pair_ref[1] = c_low
+        squares[1] = mm_nt(b_low, c_low)
+        squares[2] = jnp.zeros((SPAN, SPAN), F32)
+        c_flip_ref[...] = jnp.transpose(c_low.astype(F32)).astype(BF16)
+        dpair_ref[...] = jnp.zeros_like(dpair_ref)
+        dgated_ref[...] = mm_nt(dh[...], wo_ref[...])
+
+    def one_tile(tile, low, high):
         width = high - low
+        before = before_rows()
+        after = [columns[AFTER + lag] for lag in range(TAPS - 1)]
+        total, delta, grown, ending = (columns[at] for at in (TOTAL, DELTA, GROWN, ENDING))
+        keep, scores = squares[0], squares[1]
+        carry_last = grown[SPAN - 1 : SPAN, :]
+        b_low = pair_ref[0]
+        kx = kx_ref[...]
         lane = lax.broadcasted_iota(jnp.int32, (SPAN, width), 1)
         picker = (
             lax.broadcasted_iota(jnp.int32, (width, 128), 1)
@@ -377,13 +347,12 @@
         gate = gate_ref[:, low:high].astype(F32)
         gate_sig = sigmoid(gate)
         silu = gate * gate_sig
-        g = mixed * silu
-        scale = stat_cols[:, :width]
-        n = g * scale
+        scale = columns[SCALE, :, :width]
+        n = mixed * silu * scale
         gain = gain_ref[0:1, low:high]
-        dgated_t = dgated[:, low:high]
+        dgated_t = dgated_ref[:, low:high]
         gated_ref[:, low:high] = (n * gain).astype(BF16)
-        dg = scale * (dgated_t * gain - n * mean_cols[:, :width])
+        dg = scale * (dgated_t * gain - n * columns[MEAN, :, :width])
         dgate_ref[:, low:high] = (
             dg * mixed * (gate_sig * (1.0 + gate * (1.0 - gate_sig)))
         ).astype(BF16)
@@ -395,7 +364,7 @@
             decay = jnp.exp(total_rows[head : head + 1, :] - total[:, head : head + 1] + keep)
             mine = (lane // HEAD) == half
             pairs = mm_nt(jnp.where(mine, w_low, jnp.zeros_like(w_low)), dy_low)
-            dscore[...] += decay * pairs
+            squares[2] += decay * pairs
             part = mm((scores * decay).astype(BF16), dy_low)
             grad_w = part if grad_w is None else jnp.where(lane < HEAD, grad_w, part)
         dmem = dmemory[:, low:high]
@@ -404,28 +373,25 @@
         ending_t = spread_pair(ending, tile, width)
         from_state = mm(b_low, dmem_low) * ending_t
         grad_w = grad_w + from_state
-        db = db + mm_nt((weighted * ending_t).astype(BF16), dmem_low)
+        dpair_ref[0] += mm_nt((weighted * ending_t).astype(BF16), dmem_low)
         dy_grown = (dy * spread_pair(grown, tile, width)).astype(BF16)
-        dc = dc + mm_nt(dy_grown, mem_low)
+        dpair_ref[1] += mm_nt(dy_grown, mem_low)
         carry_t = spread_pair(carry_last, tile, width)
         w_round = w_low.astype(F32)
         at_last = jnp.sum(w_round * from_state, axis=0, keepdims=True) + jnp.sum(
             dmem * mem_low.astype(F32) * carry_t, axis=0, keepdims=True
         )
-        dlast = dlast + exact(jnp.broadcast_to(at_last, (8, width)), picker)
-        dmemory[:, low:high] = dmem * carry_t + mm(c_flip, dy_grown)
-        dtotal = dtotal + exact(dy * scanned - w_round * grad_w, picker)
-        ddelta = ddelta + exact(values * grad_w, picker)
+        dlast_ref[...] += exact(jnp.broadcast_to(at_last, (8, width)), picker)
+        dmemory[:, low:high] = dmem * carry_t + mm(c_flip_ref[...], dy_grown)
+        columns[DTOTAL] += exact(dy * scanned - w_round * grad_w, picker)
+        columns[DDELTA] += exact(values * grad_w, picker)
         dconv = (delta_t * grad_w + skip * dy) * (sig * (1.0 + conv * (1.0 - sig)))
         ext_dx[0:SPAN, low:high] = dconv
         sums = [jnp.sum(dconv * ext_x[pl.ds(8, SPAN), low:high], axis=0, keepdims=True)]
         for lag in range(1, TAPS):
+            masked = dconv * before[lag - 1][:, :width]
             sums.append(
-                jnp.sum(
-                    dconv * before[lag - 1][:, :width] * ext_x[pl.ds(8 - lag, SPAN), low:high],
-                    axis=0,
-                    keepdims=True,
-                )
+                jnp.sum(masked * ext_x[pl.ds(8 - lag, SPAN), low:high], axis=0, keepdims=True)
             )
         sums = sums[::-1] + [
             jnp.sum(dconv, axis=0, keepdims=True),
@@ -443,51 +409,357 @@
             )
         dx_ref[:, low:high] = back.astype(BF16)
 
-    score_grad = dscore[...]
-    db = db + mm(score_grad.astype(BF16), c_low)
-    dc = dc + mm(jnp.transpose(score_grad).astype(BF16), b_low)
-    for part, (conv, sig, grad) in enumerate(((b_conv, b_sig, db), (c_conv, c_sig, dc))):
-        low, high = part * STATE, (part + 1) * STATE
-        dconv = grad * (sig * (1.0 + conv * (1.0 - sig)))
-        ext_dbc[0:SPAN, low:high] = dconv
-        sums = [jnp.sum(dconv * ext_bc[pl.ds(8, SPAN), low:high], axis=0, keepdims=True)]
-        for lag in range(1, TAPS):
-            sums.append(
-                jnp.sum(
-                    dconv * before[lag - 1] * ext_bc[pl.ds(8 - lag, SPAN), low:high],
-                    axis=0,
-                    keepdims=True,
+    tiles = list(enumerate(tiles_of(inner)))
+    cut = -(-len(tiles) // (BACKWARD_STEPS - 2))
+    for at in range(BACKWARD_STEPS - 2):
+        group = tiles[at * cut : (at + 1) * cut]
+        if group:
+
+            @pl.when(step == at + 1)
+            def _():
+                for tile, (low, high) in group:
+                    one_tile(tile, low, high)
+
+    @pl.when(step == BACKWARD_STEPS - 1)
+    def _():
+        before = before_rows()
+        kbc = kbc_ref[...]
+        score_grad = squares[2]
+        db = dpair_ref[0] + mm(score_grad.astype(BF16), pair_ref[1])
+        dc = dpair_ref[1] + mm(jnp.transpose(score_grad).astype(BF16), pair_ref[0])
+        for part, (conv, grad) in enumerate(zip(convs(before), (db, dc))):
+            low, high = part * STATE, (part + 1) * STATE
+            sig = sigmoid(conv)
+            dconv = grad * (sig * (1.0 + conv * (1.0 - sig)))
+            ext_dbc[0:SPAN, low:high] = dconv
+            sums = [jnp.sum(dconv * ext_bc[pl.ds(8, SPAN), low:high], axis=0, keepdims=True)]
+            for lag in range(1, TAPS):
+                masked = dconv * before[lag - 1]
+                sums.append(
+                    jnp.sum(masked * ext_bc[pl.ds(8 - lag, SPAN), low:high], axis=0, keepdims=True)
                 )
+            sums = sums[::-1] + [jnp.sum(dconv, axis=0, keepdims=True), jnp.zeros((3, STATE), F32)]
+            gbc_ref[:, low:high] += jnp.concatenate(sums, axis=0)
+            back = dconv * kbc[TAPS - 1 : TAPS, low:high]
+            for lag in range(1, TAPS):
+                back = back + (
+                    ext_dbc[pl.ds(lag, SPAN), low:high]
+                    * columns[AFTER + lag - 1]
+                    * kbc[TAPS - 1 - lag : TAPS - lag, low:high]
+                )
+            dbc_ref[:, low:high] = back.astype(BF16)
+        row, col = lower_ones()
+        slope = -jnp.exp(heads_ref[1:2, :])
+        rate = slope * columns[DELTA]
+        drate = exact((row <= col).astype(F32), columns[DTOTAL]) + dlast_ref[0:1, :]
+        ddt = (columns[DDELTA] + slope * drate) * sigmoid(dt_ref[...] + heads_ref[0:1, :])
+        lane = lax.broadcasted_iota(jnp.int32, (SPAN, 128), 1)
+        own_ddt = jnp.where(lane < inner // HEAD, ddt, 0.0)
+        dbc_ref[:, 2 * STATE :] = own_heads(own_ddt, inner // HEAD, 1).astype(BF16)
+        gheads_ref[...] += jnp.concatenate(
+            [
+                jnp.sum(ddt, axis=0, keepdims=True),
+                jnp.sum(drate * rate, axis=0, keepdims=True),
+                jnp.zeros((6, 128), F32),
+            ],
+            axis=0,
+        )
+        finish(
+            mm_nt(dgate_ref[...], weight_refs[0][...])
+            + mm_nt(dx_ref[...], weight_refs[1][...])
+            + mm_nt(dbc_ref[...], weight_refs[2][...])
+        )
+
+
+def backward_scratch(inner):
+    return [
+        pltpu.VMEM((SPAN + 8, inner), F32),
+        pltpu.VMEM((SPAN + 8, 2 * STATE), F32),
+        pltpu.VMEM((SPAN + 8, inner), F32),
+        pltpu.VMEM((SPAN + 8, 2 * STATE), F32),
+        pltpu.VMEM((STATE, inner), F32),
+        pltpu.VMEM((14, SPAN, 128), F32),
+        pltpu.VMEM((128, SPAN), F32),
+        pltpu.VMEM((3, SPAN, SPAN), F32),
+        pltpu.VMEM((SPAN, inner), F32),
+        pltpu.VMEM((2, SPAN, STATE), BF16),
+        pltpu.VMEM((STATE, SPAN), BF16),
+        pltpu.VMEM((2, SPAN, STATE), F32),
+        pltpu.VMEM((8, 128), F32),
+    ]
+
+
+def plain_backward_kernel(length, starts_ref, dh_ref, scale_ref, mean_ref, *rest):
+    small, wo_ref, saved, rest = rest[:4], rest[4], rest[5:13], rest[13:]
+    inner = small[0].shape[1]
+    *weights, rest = split_weights(inner, rest)
+    *grads, rest = split_weights(inner, rest)
+    gated_ref, dnormed_ref, *rest = rest
+    sums, scratch = rest[:3], rest[3:]
+    turn = pl.program_id(0)
+
+    def finish(total):
+        dnormed_ref[...] = total.astype(dnormed_ref.dtype)
+
+    for step in range(BACKWARD_STEPS):
+        backward_steps(
+            step, turn == 0, pl.num_programs(0) - 1 - turn, length, starts_ref, dh_ref,
+            (scale_ref, mean_ref), small, weights, wo_ref, saved, grads + [gated_ref], sums, scratch,
+            finish,
+        )
+
+
+def fused_backward_kernel(sizes, whole_inner, length, outer_layer, starts_ref, dh, scale_ref, mean_ref, *rest):
+    small, wo_ref, saved, rest = rest[:4], rest[4], rest[5:13], rest[13:]
+    columns, normed, stream, gain, outer, rest = *rest[:5], rest[5:]
+    if outer_layer:
+        product, rest = rest[0], rest[1:]
+        grad, gain_out, gx, gbc, gheads, means, gathered, finals, rest = *rest[:7], rest[7:9], rest[9:]
+    else:
+        other_sums, rest = rest[:4], rest[4:]
+        carried, rest = rest[:2], rest[2:]
+        grad, smalls_out, slots_0, slots_1, rest = *rest[:2], rest[2:4], rest[4:6], rest[6:]
+    scratch, rest = rest[:13], rest[13:]
+    weight, dproj, gated, part, inbox, load_sems, rest = *rest[:6], rest[6:]
+    flow_scratch, flow_finals, rest = rest[:4], rest[4:6], rest[6:]
+    ranks = {axis: lax.axis_index(axis) for axis in sizes}
+    core, rank, member = ranks["section"], ranks["seq"], ranks["dp"]
+    count, copies = sizes["seq"], sizes["dp"]
+    if outer_layer:
+        spread, mean_rows, tokens, rest = *rest[:3], rest[3:]
+        row_send, row_recv, out_sems, rest = *rest[:3], rest[3:]
+        line_refs, rest = rest[:5], rest[5:]
+        flow_sems = rest
+    else:
+        gx, gbc, gheads, gain_out, rest = *rest[:4], rest[4:]
+        packed, theirs, dp_sum, dp_slots, z_slots, rest = *rest[:5], rest[5:]
+        small_sems, rest = rest[:6], rest[6:]
+        squares_0, squares_1, rest = rest[:3], rest[3:6], rest[6:]
+        line_refs, flow_sems = tuple(rest[:2]) + (None,) * 3, rest[2:]
+        spread = None
+    turn = pl.program_id(0)
+    blocks = length // SPAN
+    steps = blocks * BACKWARD_STEPS
+    block = blocks - 1 - lax.div(turn, BACKWARD_STEPS)
+    inner = small[0].shape[1]
+    parts = ((0, inner), (inner, 2 * inner), (2 * inner, 2 * inner + 3 * STATE))
+    width = dh.shape[1]
+    line = Line(
+        count,
+        rank,
+        part,
+        inbox,
+        spread,
+        line_refs,
+        (lambda at: (blocks - at) * BACKWARD_STEPS) if outer_layer else (lambda at: steps),
+    )
+    left_in = weight.at[0:length, 0:width]
+    flow = Flow(
+        sizes, ranks, left_in, dproj, gated, dh, *flow_finals, flow_scratch, flow_sems
+    )
+    weight_load = pltpu.make_async_copy(
+        columns.at[1 if outer_layer else 0], weight, load_sems.at[0]
+    )
+    normed_load = pltpu.make_async_copy(normed, left_in, load_sems.at[1])
+
+    @pl.when(turn == 0)
+    def _():
+        greet_all(sizes, ranks)
+        weight_load.start()
+        gain_out[...] = jnp.zeros_like(gain_out)
+
+    @pl.when(turn == BACKWARD_STEPS - 1)
+    def _():
+        weight_load.wait()
+
+    if not outer_layer:
+        square = Square(member, carried, slots_1, squares_1)
+        for when, stage in (
+            (0, square.begin),
+            (steps // 2, square.middle),
+            (steps - 1, square.end),
+        ):
+
+            @pl.when((turn == when) & (core == 1))
+            def _():
+                stage(0)
+                stage(1)
+
+    @pl.when(turn < steps)
+    def _():
+        rows = pl.ds(pl.multiple_of(block * SPAN, SPAN), SPAN)
+
+        def finish(total):
+            part[rows, :] = total.astype(part.dtype)
+
+        backward_steps(
+            lax.rem(turn, BACKWARD_STEPS),
+            turn < BACKWARD_STEPS,
+            block,
+            length,
+            starts_ref,
+            dh.at[rows],
+            (scale_ref, mean_ref),
+            small,
+            [weight.at[:, low:high] for low, high in parts],
+            wo_ref,
+            saved,
+            [dproj.at[rows, low:high] for low, high in parts] + [gated.at[rows]],
+            (gx, gbc, gheads),
+            scratch,
+            finish,
+        )
+
+    def own_piece(piece, total):
+        rows = pl.ds(pl.multiple_of(piece * PIECE, PIECE), PIECE)
+        back, gain_part = norm_back(stream[rows, :].astype(F32), gain[0:1, :], total)
+        gain_out[0:1, :] += gain_part
+        whole_grad = outer[rows, :].astype(F32) + back
+        grad[rows, :] = whole_grad
+        if outer_layer:
+            low = whole_grad.astype(BF16)
+            spread[rank, rows, :] = low
+            along_rows = jnp.sum(low.astype(F32) * product[rows, :], axis=1, keepdims=True)
+            tokens[rows, :] = jnp.broadcast_to(along_rows / whole_inner, (PIECE, 128))
+
+    if outer_layer:
+        share = (count, rank, mean_rows.at[rank], mean_rows, row_send, row_recv)
+
+        def after_own():
+            mean_rows[rank] = jnp.transpose(tokens[...])[0:8, :]
+            share_with_all(*share)
+
+    else:
+        s_core_send, s_core_recv, s_dp_send, s_dp_recv, s_z_send, s_z_recv = small_sems
+
+        def s_core_copy():
+            return push("section", 1 - core, packed, theirs, s_core_send, s_core_recv)
+
+        def s_dp_copy(step):
+            to = lax.rem(member + step, copies)
+            return push(
+                "dp", to, dp_sum, dp_slots.at[member], s_dp_send.at[step], s_dp_recv.at[member]
             )
-        sums = sums[::-1] + [jnp.sum(dconv, axis=0, keepdims=True), jnp.zeros((3, STATE), F32)]
-        gbc_ref[:, low:high] += jnp.concatenate(sums, axis=0)
-        back = dconv * kbc[TAPS - 1 : TAPS, low:high]
-        for lag in range(1, TAPS):
-            back = back + (
-                ext_dbc[pl.ds(lag, SPAN), low:high]
-                * after[lag - 1]
-                * kbc[TAPS - 1 - lag : TAPS - lag, low:high]
+
+        def s_z_copy(step):
+            to = lax.rem(rank + step, count)
+            return push(
+                "seq", to, z_slots.at[rank], z_slots.at[rank], s_z_send.at[step], s_z_recv.at[rank]
             )
-        dbc_ref[:, low:high] = back.astype(BF16)
-
-    drate = exact(upper, dtotal) + dlast[0:1, :]
-    ddt = (ddelta + slope * drate) * sigmoid(dt)
-    lane = lax.broadcasted_iota(jnp.int32, (SPAN, 128), 1)
-    own_ddt = jnp.where(lane < inner // HEAD, ddt, 0.0)
-    dbc_ref[:, 2 * STATE :] = own_heads(own_ddt, inner // HEAD, 1).astype(BF16)
-    gheads_ref[...] += jnp.concatenate(
-        [
-            jnp.sum(ddt, axis=0, keepdims=True),
-            jnp.sum(drate * rate, axis=0, keepdims=True),
-            jnp.zeros((6, 128), F32),
-        ],
-        axis=0,
-    )
-    dnormed_ref[...] = (
-        mm_nt(dgate_ref[...], wg_ref[...])
-        + mm_nt(dx_ref[...], wx_ref[...])
-        + mm_nt(dbc_ref[...], wbc_ref[...])
-    ).astype(dnormed_ref.dtype)
+
+        def after_own():
+            wide = SMALL_COLUMNS - 256
+            mine = (gx, gbc, gheads, gain_out)
+            packed[...] = jnp.zeros_like(packed)
+            for layer, (x_sum, bc_sum, head_sum, gain_sum) in enumerate((mine, other_sums)):
+                packed[layer, :, :inner] = x_sum[...]
+                packed[layer, 0:5, inner:wide] = bc_sum[0:5, :]
+                packed[layer, 5:7, inner : inner + 128] = head_sum[0:2, :]
+                for row in range(width // 256):
+                    packed[layer, row : row + 1, wide:] = gain_sum[0:1, row * 256 : (row + 1) * 256]
+            s_core_copy().start()
+
+    def serve(at, _):
+        line.turn(at, own_piece, None, after_own)
+        return 0
+
+    square_here = None if outer_layer else Square(member, flow_finals, slots_0, squares_0)
+    ready = flow.ready(2)
+
+    def serve_both(at, _):
+        line.turn(at, own_piece, None, after_own)
+        flow.turn(at - steps, 2)
+        for kind in range(2):
+
+            @pl.when(at - steps == ready[kind])
+            def _():
+                flow.finals_here(kind, 1 if outer_layer else 0)
+
+            if not outer_layer:
+
+                @pl.when(at - steps == ready[kind] + 1)
+                def _():
+                    flow.finals_given(kind, 0)
+
+                    @pl.when(core == 0)
+                    def _():
+                        square_here.begin(kind)
+
+        return 0
+
+    if outer_layer:
+
+        @pl.when(turn < steps)
+        def _():
+            serve(turn, 0)
+
+    @pl.when(turn == steps)
+    def _():
+        normed_load.start()
+        normed_load.wait()
+        lax.fori_loop(steps, steps + max(line.turns(), ready[1] + 2), serve_both, 0)
+        if outer_layer:
+            copies_out = [
+                pltpu.make_async_copy(spread.at[at], gathered.at[at], out_sems.at[at])
+                for at in range(count)
+            ]
+            for copy in copies_out:
+                copy.start()
+            share_wait_recv(*share)
+            means[...] = mean_rows[...]
+            share_wait_send(*share)
+            flow.finals_given(0, 1)
+            flow.finals_given(1, 1)
+            for at in range(2):
+                final_copy = pltpu.make_async_copy(
+                    flow_finals[at], finals[at], out_sems.at[count + at]
+                )
+                final_copy.start()
+                final_copy.wait()
+            flow.settle()
+            line.settle()
+            for copy in copies_out:
+                copy.wait()
+        else:
+            s_core_copy().wait_recv()
+            dp_sum[...] = packed[...] + theirs[...]
+            for step in range(1, copies):
+                s_dp_copy(step).start()
+
+            @pl.when(core == 0)
+            def _():
+                square_here.middle(0)
+                square_here.middle(1)
+
+            total = dp_sum[...]
+            for step in range(1, copies):
+                origin = lax.rem(member + step, copies)
+                place = dp_slots.at[origin]
+                push(
+                    "dp", origin, place, place, s_dp_send.at[step], s_dp_recv.at[origin]
+                ).wait_recv()
+                total = total + dp_slots[origin]
+            z_slots[rank] = total
+            for step in range(1, count):
+                s_z_copy(step).start()
+            @pl.when(core == 0)
+            def _():
+                square_here.end(0)
+                square_here.end(1)
+
+            for step in range(1, count):
+                origin = lax.rem(rank + step, count)
+                place = z_slots.at[origin]
+                push("seq", origin, place, place, s_z_send.at[step], s_z_recv.at[origin]).wait_recv()
+            smalls_out[...] = z_slots[...]
+
+            s_core_copy().wait_send()
+            for step in range(1, copies):
+                s_dp_copy(step).wait_send()
+            for step in range(1, count):
+                s_z_copy(step).wait_send()
+            flow.settle()
+            line.settle()
 
 
 def whole(array):
@@ -535,7 +807,7 @@
         jax.ShapeDtypeStruct((length, 128), F32),
         jax.ShapeDtypeStruct((length, inner), F32),
         jax.ShapeDtypeStruct((blocks, STATE, inner), BF16),
-        jax.ShapeDtypeStruct((length, width), part_kind(length, width)),
+        jax.ShapeDtypeStruct((length, width), BF16 if dh is not None else part_kind(length, width)),
         jax.ShapeDtypeStruct((8, length), F32),
     ]
     out_specs = [
@@ -568,21 +840,25 @@
     )(*operands)
 
 
-def run_backward(starts, dh, scales, means, weights, saved, carried=()):
+def run_backward(starts, dh, scales, means, weights, saved, fused=None):
     columns, kx, kbc, heads, gain, wo = weights
     gate, x, bc, dt, scanned, states = saved
     length, width = dh.shape
     inner = kx.shape[1]
     blocks = length // SPAN
-    rows = lambda cols: pl.BlockSpec((SPAN, cols), lambda i: (blocks - 1 - i, 0))
+    if fused is None:
+        block = lambda i: blocks - 1 - i
+    else:
+        block = lambda i: blocks - 1 - jnp.minimum(lax.div(i, BACKWARD_STEPS), blocks - 1)
+    rows = lambda cols: pl.BlockSpec((SPAN, cols), lambda i: (block(i), 0))
     halo = lambda cols: pl.BlockSpec(
-        (16, cols), lambda i: (jnp.maximum((blocks - 1 - i) * (SPAN // 16) - 1, 0), 0)
+        (16, cols), lambda i: (jnp.maximum(block(i) * (SPAN // 16) - 1, 0), 0)
     )
     fixed = lambda shape: pl.BlockSpec(shape, lambda i: (0,) * len(shape))
-    stat = pl.BlockSpec((1, 8, SPAN), lambda i: (blocks - 1 - i, 0, 0))
+    stat = pl.BlockSpec((1, 8, SPAN), lambda i: (block(i), 0, 0))
     small = [kx, kbc, heads, gain]
     operands = [starts, dh, scales, means] + small + [wo[0]]
-    in_specs = [pl.BlockSpec(memory_space=pltpu.SMEM), rows(width), stat, stat]
+    in_specs = [pl.BlockSpec(memory_space=pltpu.SMEM), whole(dh) if fused else rows(width), stat, stat]
     in_specs += [whole(array) for array in small] + [wo[1]]
     operands += [gate, x, x, bc, bc, dt, scanned, states]
     in_specs += [
@@ -593,54 +869,92 @@
         halo(2 * STATE),
         rows(128),
         rows(inner),
-        pl.BlockSpec((1, STATE, inner), lambda i: (blocks - 1 - i, 0, 0)),
+        pl.BlockSpec((1, STATE, inner), lambda i: (block(i), 0, 0)),
     ]
-    operands += [array for array, _ in columns]
-    in_specs += [spec for _, spec in columns]
-    operands += list(carried)
-    in_specs += [whole(array) for array in carried]
-    widths = [2 * inner + 3 * STATE] if len(columns) == 1 else [inner, inner, 3 * STATE]
-    out_shape = [jax.ShapeDtypeStruct((length, cols), BF16) for cols in widths] + [
-        jax.ShapeDtypeStruct((length, inner), BF16),
-        jax.ShapeDtypeStruct((length, width), part_kind(length, width)),
+    sums = [
         jax.ShapeDtypeStruct((8, inner), F32),
         jax.ShapeDtypeStruct((8, 2 * STATE), F32),
         jax.ShapeDtypeStruct((8, 128), F32),
     ]
-    out_specs = [rows(cols) for cols in widths] + [
-        rows(inner),
-        rows(width),
-        fixed((8, inner)),
-        fixed((8, 2 * STATE)),
-        fixed((8, 128)),
-    ]
-    sems, settings = [], {}
-    if carried:
-        copies = lax.axis_size("dp")
-        out_shape += [jax.ShapeDtypeStruct((copies,) + c.shape, c.dtype) for c in carried]
-        out_specs += [IN_HBM, IN_HBM]
-        sems, settings = square_sems(), {"collective_id": 6, "has_side_effects": True}
+    scratch = backward_scratch(inner)
+    if fused is None:
+        operands += [array for array, _ in columns]
+        in_specs += [spec for _, spec in columns]
+        widths = [2 * inner + 3 * STATE] if len(columns) == 1 else [inner, inner, 3 * STATE]
+        out_shape = [jax.ShapeDtypeStruct((length, cols), BF16) for cols in widths] + [
+            jax.ShapeDtypeStruct((length, inner), BF16),
+            jax.ShapeDtypeStruct((length, width), part_kind(length, width)),
+        ]
+        out_specs = [rows(cols) for cols in widths] + [rows(inner), rows(width)]
+        out_shape += sums
+        out_specs += [fixed(array.shape) for array in sums]
+        kernel, grid, settings = functools.partial(plain_backward_kernel, length), blocks, {}
+    else:
+        sizes = axis_sizes()
+        count, copies = sizes["seq"], sizes["dp"]
+        layer, whole_inner, normed, inputs, carried = fused
+        stream, next_gain, outer, *more = inputs
+        wide = columns.shape[2]
+        dma = pltpu.SemaphoreType.DMA
+        operands += [columns, normed] + list(inputs) + list(carried)
+        in_specs += [IN_HBM, IN_HBM] + [whole(array) for array in list(inputs) + list(carried)]
+        flow_scratch, flow_sems, finals = flow_shapes(sizes, width // count, inner, width, wide)
+        scratch += [
+            pltpu.VMEM((width, wide), BF16),
+            pltpu.VMEM((length, wide), BF16),
+            pltpu.VMEM((length, inner), BF16),
+            pltpu.VMEM((length, width), BF16),
+            pltpu.VMEM((count + 1, SPAN, width), BF16),
+            dma((2,)),
+        ]
+        scratch += flow_scratch + [pltpu.VMEM(f.shape, f.dtype) for f in finals]
+        out_shape = [jax.ShapeDtypeStruct((SPAN, width), F32)]
+        if layer:
+            out_shape += [jax.ShapeDtypeStruct((8, width), F32)] + sums
+            out_shape += [jax.ShapeDtypeStruct((count, 8, SPAN), F32)]
+            out_specs = [fixed(array.shape) for array in out_shape]
+            out_shape += [jax.ShapeDtypeStruct((count, SPAN, width), BF16)] + finals
+            out_specs += [IN_HBM] * 3
+            scratch += [
+                pltpu.VMEM((count, SPAN, width), BF16),
+                pltpu.VMEM((count, 8, SPAN), F32),
+                pltpu.VMEM((SPAN, 128), F32),
+                dma((count,)),
+                dma((count,)),
+                dma((count + 2,)),
+            ]
+            scratch += line_sems(count, SPAN // PIECE)
+        else:
+            out_shape += [jax.ShapeDtypeStruct((count, 2, 8, SMALL_COLUMNS), F32)]
+            out_specs = [fixed(array.shape) for array in out_shape]
+            slots = [jax.ShapeDtypeStruct((copies,) + f.shape, f.dtype) for f in finals]
+            out_shape += slots + slots
+            out_specs += [IN_HBM] * 4
+            scratch += [pltpu.VMEM(array.shape, F32) for array in sums] + [pltpu.VMEM((8, width), F32)]
+            scratch += [pltpu.VMEM((2, 8, SMALL_COLUMNS), F32)] * 3
+            scratch += [pltpu.VMEM((size, 2, 8, SMALL_COLUMNS), F32) for size in (copies, count)]
+            scratch += [dma, dma, dma((copies,)), dma((copies,)), dma((count,)), dma((count,))]
+            scratch += square_sems() + square_sems() + line_sems(count, SPAN // PIECE)[:2]
+        scratch += flow_sems
+        kernel = functools.partial(fused_backward_kernel, sizes, whole_inner, length, bool(layer))
+        grid = blocks * BACKWARD_STEPS + 1
+        settings = {"collective_id": 2 + layer, "has_side_effects": True}
     return pl.pallas_call(
-        functools.partial(backward_kernel, bool(carried), length),
-        grid=(blocks,),
+        kernel,
+        grid=(grid,),
         in_specs=in_specs,
         out_specs=out_specs,
         out_shape=out_shape,
-        scratch_shapes=[
-            pltpu.VMEM((SPAN + 8, inner), F32),
-            pltpu.VMEM((SPAN + 8, 2 * STATE), F32),
-            pltpu.VMEM((SPAN + 8, inner), F32),
-            pltpu.VMEM((SPAN + 8, 2 * STATE), F32),
-            pltpu.VMEM((STATE, inner), F32),
-            pltpu.VMEM((SPAN, SPAN), F32),
-        ]
-        + sems,
+        scratch_shapes=scratch,
         compiler_params=pltpu.CompilerParams(
-            dimension_semantics=("arbitrary",), vmem_limit_bytes=VMEM_LIMIT, **settings
+            dimension_semantics=("arbitrary",), vmem_limit_bytes=BACK_VMEM, **settings
         ),
         cost_estimate=cost(length, width, inner, 2),
         name="layer_backward",
     )(*operands)
+
+
+BACK_VMEM = 63 * 2**20
 
 
 def norm_rows(rows_in, gain_vec):
@@ -661,7 +975,7 @@
 
 MESH = pl.DeviceIdType.MESH
 PIECE = 16
-HOP = 1
+HOP = 2
 
 
 def along(axis, index):
@@ -709,10 +1023,12 @@
 
 
 class Line:
-    def __init__(self, count, rank, part, inbox, spread, sems):
+    def __init__(self, count, rank, part, inbox, spread, sems, born=lambda block: 0):
         self.count, self.rank = count, rank
         self.part, self.inbox, self.spread = part, inbox, spread
         self.sum_send, self.sum_recv, self.out_right, self.out_left, self.out_recv = sems
+        self.born = born
+        self.pieces = SPAN // PIECE
 
     def sum_copy(self, slot, target_slot, to, piece):
         rows = pl.ds(piece * PIECE, PIECE)
@@ -751,20 +1067,20 @@
         target = count if sign < 0 and away == 1 else block
         self.sum_copy(block, target, rank + sign, piece).start()
 
-    def pass_sums(self, turn, pieces):
-        count, rank = self.count, self.rank
+    def pass_sums(self, turn):
+        count, rank, pieces = self.count, self.rank, self.pieces
         for away in range(count - 1, 0, -1):
             for sign in (1, -1):
                 block = rank + sign * away
                 inside = block < count if sign > 0 else block >= 0
-                piece = turn - HOP * (rank if sign > 0 else count - 1 - rank)
+                piece = turn - self.born(block) - HOP * (rank if sign > 0 else count - 1 - rank)
 
                 @pl.when(inside & (piece >= 0) & (piece < pieces))
                 def _():
                     self.pass_sum(piece, away, sign)
 
     def own_lag(self, block):
-        return HOP * jnp.maximum(block, self.count - 1 - block)
+        return self.born(block) + HOP * jnp.maximum(block, self.count - 1 - block)
 
     def own_total(self, piece):
         count, rank = self.count, self.rank
@@ -799,59 +1115,63 @@
         def _():
             self.out_copy(block, piece, sign).start()
 
-    def pass_out(self, turn, pieces, away):
+    def pass_out(self, turn, away):
         for sign in (1, -1):
             block = self.rank - sign * away
             piece = turn - self.own_lag(block) - HOP * away
             inside = block >= 0 if sign > 0 else block < self.count
 
-            @pl.when(inside & (piece >= 0) & (piece < pieces))
+            @pl.when(inside & (piece >= 0) & (piece < self.pieces))
             def _():
                 self.out_copy(block, piece, sign).wait_recv()
                 self.start_out(block, piece, sign)
 
-    def run(self, pieces, own_piece, before_own=None, after_own=None, flow=None, pace=2):
-        count = self.count
-        lag = self.own_lag(self.rank)
-        turns = pieces + HOP * (2 if self.spread is not None else 1) * (count - 1)
+    def turns(self):
+        return self.pieces + HOP * (2 if self.spread is not None else 1) * (self.count - 1)
+
+    def turn(self, turn, own_piece, before_own=None, after_own=None):
+        self.pass_sums(turn)
+        if self.spread is not None:
+            for away in range(1, self.count):
+                self.pass_out(turn, away)
+        piece = turn - self.own_lag(self.rank)
+        if before_own is not None:
+
+            @pl.when(piece == 0)
+            def _():
+                before_own()
+
+        @pl.when((piece >= 0) & (piece < self.pieces))
+        def _():
+            own_piece(piece, self.own_total(piece))
+            if self.spread is not None:
+                self.start_out(self.rank, piece, 1)
+                self.start_out(self.rank, piece, -1)
+
+        if after_own is not None:
+
+            @pl.when(piece == self.pieces - 1)
+            def _():
+                after_own()
+
+    def run(self, own_piece, before_own=None, after_own=None, flow=None, pace=2):
+        turns = self.turns()
         if flow is not None:
             turns = max(turns, flow.turns(pace))
 
         def step(turn, _):
-            self.pass_sums(turn, pieces)
-            if self.spread is not None:
-                for away in range(1, count):
-                    self.pass_out(turn, pieces, away)
-            if before_own is not None:
-
-                @pl.when(turn == lag)
-                def _():
-                    before_own()
-
-            piece = turn - lag
-
-            @pl.when((piece >= 0) & (piece < pieces))
-            def _():
-                own_piece(piece, self.own_total(piece))
-                if self.spread is not None:
-                    self.start_out(self.rank, piece, 1)
-                    self.start_out(self.rank, piece, -1)
-
-            if after_own is not None:
-
-                @pl.when(piece == pieces - 1)
-                def _():
-                    after_own()
-
+            self.turn(turn, own_piece, before_own, after_own)
             if flow is not None:
                 flow.turn(turn, pace)
             return 0
 
         lax.fori_loop(0, turns, step, 0)
-
-        def settle(piece, _):
-            for block in range(count):
-                right = (block > self.rank) & (self.rank < count - 1)
+        self.settle()
+
+    def settle(self):
+        def body(piece, _):
+            for block in range(self.count):
+                right = (block > self.rank) & (self.rank < self.count - 1)
                 left = (block < self.rank) & (self.rank > 0)
 
                 @pl.when(right | left)
@@ -860,7 +1180,7 @@
 
                 if self.spread is not None:
 
-                    @pl.when((block <= self.rank) & (self.rank < count - 1))
+                    @pl.when((block <= self.rank) & (self.rank < self.count - 1))
                     def _():
                         self.out_copy(block, piece, 1).wait_send()
 
@@ -870,7 +1190,7 @@
 
             return 0
 
-        lax.fori_loop(0, pieces, settle, 0)
+        lax.fori_loop(0, self.pieces, body, 0)
 
 
 def line_sems(count, pieces):
@@ -929,7 +1249,7 @@
         product[rows, :] = y
         spread[rank, rows, :] = norm_rows(low.astype(F32), gain[0:1, :]).astype(BF16)
 
-    line.run(SPAN // PIECE, own_piece, before_own)
+    line.run(own_piece, before_own)
     share_wait_send(*share)
 
 
@@ -945,7 +1265,7 @@
         gain_grad[0:1, :] += gain_part
         grad[rows, :] = outer[rows, :].astype(F32) + back
 
-    line.run(SPAN // PIECE, own_piece)
+    line.run(own_piece)
 
 
 def sum_stats_kernel(count, whole_inner, stat, scales, means, slots, stat_send, stat_recv):
@@ -1018,7 +1338,7 @@
     return line_call(
         functools.partial(sum_plain_kernel, count),
         "sum_plain",
-        3,
+        8,
         [part, stream, gain, outer],
         [
             jax.ShapeDtypeStruct((SPAN, width), F32),
@@ -1398,7 +1718,6 @@
 
 class Flow:
     def __init__(self, sizes, ranks, left_in, right_in, left_out, right_out, final, out_final, scratch, sems):
-        self.sizes, self.ranks = sizes, ranks
         self.left_in, self.right_in, self.left_out, self.right_out = (
             left_in,
             right_in,
@@ -1406,7 +1725,7 @@
             right_out,
         )
         self.final, self.out_final = final, out_final
-        self.full, self.got, self.parts, self.sums = scratch
+        self.give, self.got, self.parts, self.sums = scratch
         (
             self.core_send,
             self.core_recv,
@@ -1419,50 +1738,44 @@
         ) = sems
         self.count, self.copies = sizes["seq"], sizes["dp"]
         self.core, self.rank, self.stream = ranks["section"], ranks["seq"], ranks["dp"]
-        self.depth = self.full.shape[1]
-        self.half = self.depth // 2
-        self.share = self.half // self.copies
-        self.units = self.full.shape[0]
-
-    def half_rows(self, core):
-        return pl.ds(pl.multiple_of(core * self.half, self.half), self.half)
-
-    def multiply(self, unit):
+        self.units, half, self.depth = self.got.shape
+        self.halves = (half, left_out.shape[1])
+
+    def multiply(self, unit, kind, core, keep):
         depth = self.depth
-        tile = 384
-        full = self.full
-
-        def columns(left, right, at):
-            def body(index, _):
-                low = pl.multiple_of(index * tile, tile)
-                full[unit, :, pl.ds(low, tile)] = mm_tn(left, right[:, pl.ds(low, tile)]).astype(BF16)
-                return 0
-
-            lax.fori_loop(0, right.shape[1] // tile, body, 0)
-
-        @pl.when(unit < self.count)
-        def _():
-            at = pl.multiple_of(unit * depth, depth)
-            columns(self.left_in[:, pl.ds(at, depth)], self.right_in, at)
-
-        @pl.when(unit >= self.count)
-        def _():
-            at = pl.multiple_of((unit - self.count) * depth, depth)
-            columns(self.left_out[:, pl.ds(at, depth)], self.right_out, at)
-
-    def core_copy(self, unit):
+        if kind == 0:
+            strip = self.halves[0] // 2
+            base = core * (self.right_in.shape[1] - self.halves[0])
+            source, right = self.right_in, self.left_in
+            block = unit
+        else:
+            strip = self.halves[1] // 2
+            base = 0
+            source, right = self.left_out, self.right_out
+            block = 2 * (unit - self.count) + core
+        right = right[:, pl.ds(pl.multiple_of(block * depth, depth), depth)]
+
+        def body(index, _):
+            low = pl.multiple_of(base + index * strip, 128)
+            keep(pl.ds(pl.multiple_of(index * strip, strip), strip), mm_tn(source[:, pl.ds(low, strip)], right))
+            return 0
+
+        lax.fori_loop(0, 2, body, 0)
+
+    def core_copy(self, unit, kind):
+        rows = pl.ds(0, self.halves[kind])
         return push(
             "section",
             1 - self.core,
-            self.full.at[unit, self.half_rows(1 - self.core)],
-            self.got.at[unit],
+            self.give.at[unit, rows],
+            self.got.at[unit, rows],
             self.core_send.at[unit],
             self.core_recv.at[unit],
         )
 
-    def part_rows(self, member):
-        start = self.core * self.half + member * self.share
-        return pl.ds(pl.multiple_of(start, self.share), self.share)
+    def part_rows(self, member, kind):
+        share = self.halves[kind] // self.copies
+        return pl.ds(pl.multiple_of(member * share, share), share)
 
     def bits(self, unit):
         first = 1 + lax.rem(unit, 2)
@@ -1472,15 +1785,15 @@
         low = lax.rem(lax.div(self.stream, bit), 2)
         return self.stream + bit - 2 * bit * low
 
-    def step_copy(self, unit, step):
+    def step_copy(self, unit, step, kind):
         first, second = self.bits(unit)
         partner, opposite = self.flip(first), self.flip(second)
         member = (partner, partner + opposite - self.stream, opposite)[step]
         return push(
             "dp",
             opposite if step == 2 else partner,
-            self.full.at[unit, self.part_rows(member)],
-            self.parts.at[unit, step],
+            self.got.at[unit, self.part_rows(member, kind)],
+            self.parts.at[unit, step, pl.ds(0, self.halves[kind] // self.copies)],
             self.part_send.at[unit, step],
             self.part_recv.at[unit, step],
         )
@@ -1495,35 +1808,43 @@
             self.z_recv.at[self.rank],
         )
 
-    def first(self, unit):
-        self.multiply(unit)
-        self.core_copy(unit).start()
-
-    def second(self, unit):
-        self.core_copy(unit).wait_recv()
-        rows = self.half_rows(self.core)
-        total = self.full[unit, rows, :].astype(F32) + self.got[unit].astype(F32)
-        self.full[unit, rows, :] = total.astype(BF16)
-        self.step_copy(unit, 0).start()
-        self.step_copy(unit, 1).start()
-
-    def third(self, unit):
+    def first(self, unit, kind):
+        def keep(rows, value):
+            self.give[unit, rows, :] = value.astype(BF16)
+
+        self.multiply(unit, kind, 1 - self.core, keep)
+        self.core_copy(unit, kind).start()
+
+    def second(self, unit, kind):
+        self.core_copy(unit, kind).wait_recv()
+
+        def keep(rows, value):
+            self.got[unit, rows, :] = (value + self.got[unit, rows, :].astype(F32)).astype(BF16)
+
+        self.multiply(unit, kind, self.core, keep)
+        self.step_copy(unit, 0, kind).start()
+        self.step_copy(unit, 1, kind).start()
+
+    def add_part(self, unit, step, member, kind):
+        self.step_copy(unit, step, kind).wait_recv()
+        total = self.got[unit, self.part_rows(member, kind), :].astype(F32)
+        part = self.parts[unit, step, : self.halves[kind] // self.copies, :]
+        return (total + part.astype(F32)).astype(BF16)
+
+    def third(self, unit, kind):
         opposite = self.flip(self.bits(unit)[1])
-        for step, member in ((1, opposite), (0, self.stream)):
-            self.step_copy(unit, step).wait_recv()
-            rows = self.part_rows(member)
-            total = self.full[unit, rows, :].astype(F32) + self.parts[unit, step].astype(F32)
-            self.full[unit, rows, :] = total.astype(BF16)
-            if step:
-                self.step_copy(unit, 2).start()
-
-    def fourth(self, unit):
-        self.step_copy(unit, 2).wait_recv()
-        total = self.full[unit, self.part_rows(self.stream), :].astype(F32)
-        total = (total + self.parts[unit, 2].astype(F32)).astype(BF16)
-
-        @pl.when(unit < self.count)
-        def _():
+        self.got[unit, self.part_rows(opposite, kind), :] = self.add_part(unit, 1, opposite, kind)
+        self.step_copy(unit, 2, kind).start()
+        self.got[unit, self.part_rows(self.stream, kind), :] = self.add_part(
+            unit, 0, self.stream, kind
+        )
+
+    def fourth(self, unit, kind):
+        total = self.add_part(unit, 2, self.stream, kind)
+        if kind:
+            self.out_final[self.core, unit - self.count] = total
+        else:
+
             @pl.when(unit == self.rank)
             def _():
                 self.final[self.core, self.rank] = total
@@ -1533,33 +1854,37 @@
                 self.sums[unit] = total
                 self.z_copy(unit).start()
 
-        @pl.when(unit >= self.count)
-        def _():
-            self.out_final[self.core, unit - self.count] = total[:, : self.out_final.shape[3]]
-
-    LAGS = (0, 1, 4, 6)
+    LAGS = (0, 1, 5, 9)
 
     def turn(self, turn, pace):
         for stage, lag in zip((self.first, self.second, self.third, self.fourth), self.LAGS):
             at = turn - lag
 
-            @pl.when((at >= 0) & (at < self.units * pace) & (lax.rem(at, pace) == 0))
-            def _():
-                stage(lax.div(at, pace))
+            for kind, (low, high) in enumerate(((0, self.count), (self.count, self.units))):
+
+                @pl.when((at >= low * pace) & (at < high * pace) & (lax.rem(at, pace) == 0))
+                def _():
+                    stage(lax.div(at, pace), kind)
 
     def turns(self, pace):
         return (self.units - 1) * pace + self.LAGS[3] + 1
 
-    def finals_here(self, layer):
-        for step in range(1, self.count):
-            origin = lax.rem(self.rank + step, self.count)
-            place = self.final.at[self.core, origin]
-            push("seq", origin, place, place, self.z_send.at[origin], self.z_recv.at[origin]).wait_recv()
-        for kind in range(2):
-
-            @pl.when(self.core != layer)
-            def _():
-                self.give_copy(kind).start()
+    def ready(self, pace):
+        last = self.LAGS[3]
+        return (self.count - 1) * pace + last + 2, (self.units - 1) * pace + last + 1
+
+    def finals_here(self, kind, layer):
+        if kind == 0:
+            for step in range(1, self.count):
+                origin = lax.rem(self.rank + step, self.count)
+                place = self.final.at[self.core, origin]
+                push(
+                    "seq", origin, place, place, self.z_send.at[origin], self.z_recv.at[origin]
+                ).wait_recv()
+
+        @pl.when(self.core != layer)
+        def _():
+            self.give_copy(kind).start()
 
     def give_copy(self, kind):
         final = (self.final, self.out_final)[kind]
@@ -1568,34 +1893,36 @@
             "section", 1 - self.core, place, place, self.give_send.at[kind], self.give_recv.at[kind]
         )
 
-    def finals_given(self, layer):
-        for kind in range(2):
-            final = (self.final, self.out_final)[kind]
-
-            @pl.when(self.core == layer)
-            def _():
-                place = final.at[1 - self.core]
-                push(
-                    "section", 1 - self.core, place, place, self.give_send.at[kind], self.give_recv.at[kind]
-                ).wait_recv()
-
-            @pl.when(self.core != layer)
-            def _():
-                self.give_copy(kind).wait_send()
+    def finals_given(self, kind, layer):
+        final = (self.final, self.out_final)[kind]
+
+        @pl.when(self.core == layer)
+        def _():
+            place = final.at[1 - self.core]
+            push(
+                "section", 1 - self.core, place, place, self.give_send.at[kind], self.give_recv.at[kind]
+            ).wait_recv()
+
+        @pl.when(self.core != layer)
+        def _():
+            self.give_copy(kind).wait_send()
 
     def settle(self):
-        def body(unit, _):
-            self.core_copy(unit).wait_send()
-            for step in range(3):
-                self.step_copy(unit, step).wait_send()
-
-            @pl.when((unit < self.count) & (unit != self.rank))
-            def _():
-                self.z_copy(unit).wait_send()
-
-            return 0
-
-        lax.fori_loop(0, self.units, body, 0)
+        for kind, (low, high) in enumerate(((0, self.count), (self.count, self.units))):
+
+            def body(unit, _):
+                self.core_copy(unit, kind).wait_send()
+                for step in range(3):
+                    self.step_copy(unit, step, kind).wait_send()
+                if kind == 0:
+
+                    @pl.when(unit != self.rank)
+                    def _():
+                        self.z_copy(unit).wait_send()
+
+                return 0
+
+            lax.fori_loop(low, high, body, 0)
 
 
 class Square:
@@ -1652,14 +1979,15 @@
 
 
 def flow_shapes(sizes, depth, inner, width, wide):
-    units = sizes["seq"] + inner // depth
-    share = depth // 2 // sizes["dp"]
+    count, copies = sizes["seq"], sizes["dp"]
+    units = count + width // depth // 2
+    half = -(-wide // 1024) * 512
     dma = pltpu.SemaphoreType.DMA
     scratch = [
-        pltpu.VMEM((units, depth, wide), BF16),
-        pltpu.VMEM((units, depth // 2, wide), BF16),
-        pltpu.VMEM((units, 3, share, wide), BF16),
-        pltpu.VMEM((sizes["seq"], share, wide), BF16),
+        pltpu.VMEM((units, half, depth), BF16),
+        pltpu.VMEM((units, half, depth), BF16),
+        pltpu.VMEM((units, 3, half // copies, depth), BF16),
+        pltpu.VMEM((count, half // copies, depth), BF16),
     ]
     sems = [
         dma((units,)),
@@ -1672,8 +2000,8 @@
         dma((2,)),
     ]
     finals = [
-        jax.ShapeDtypeStruct((2, sizes["seq"], share, wide), BF16),
-        jax.ShapeDtypeStruct((2, inner // depth, share, width), BF16),
+        jax.ShapeDtypeStruct((2, count, half // copies, depth), BF16),
+        jax.ShapeDtypeStruct((2, units - count, inner // copies, depth), BF16),
     ]
     return scratch, sems, finals
 
@@ -1721,7 +2049,7 @@
         means[rank] = jnp.transpose(columns[...])[0:8, :]
         share_with_all(*share)
 
-    line.run(SPAN // PIECE, own_piece, None, after_own, flow)
+    line.run(own_piece, None, after_own, flow)
     if with_flow:
         flow.finals_here(1)
     share_wait_recv(*share)
@@ -1745,7 +2073,7 @@
     return line_call(
         functools.partial(sum_backward_kernel, sizes, grads_of is not None, whole_inner),
         "sum_backward",
-        2,
+        7,
         [part, stream, gain, outer, product] + factors,
         [
             jax.ShapeDtypeStruct((count, SPAN, width), BF16),
@@ -1768,172 +2096,96 @@
 SMALL_COLUMNS = 1280
 
 
-def sum_last_kernel(
-    sizes,
-    part,
-    stream,
-    gain,
-    outer,
-    left_in,
-    right_in,
-    left_out,
-    right_out,
-    small,
-    gain_grad_1,
-    grad,
-    halves_0,
-    halves_out_0,
-    smalls,
-    inbox,
-    gain_grad,
-    final,
-    out_final,
-    full,
-    got,
-    parts,
-    sums,
-    packed,
-    theirs,
-    dp_sum,
-    dp_slots,
-    *sems,
-):
-    ranks = {axis: lax.axis_index(axis) for axis in sizes}
-    core, rank, member = ranks["section"], ranks["seq"], ranks["dp"]
-    count, copies = sizes["seq"], sizes["dp"]
-    greet_all(sizes, ranks)
-    line = Line(count, rank, part, inbox, None, tuple(sems[:2]) + (None,) * 3)
-    flow = Flow(
-        sizes,
-        ranks,
-        left_in,
-        right_in,
-        left_out,
-        right_out,
-        final,
-        out_final,
-        (full, got, parts, sums),
-        sems[2:10],
-    )
-    square = Square(member, (final, out_final), (halves_0, halves_out_0), sems[10:13])
-    s_core_send, s_core_recv, s_dp_send, s_dp_recv, s_z_send, s_z_recv = sems[13:]
-    gain_grad[...] = jnp.zeros_like(gain_grad)
-
-    def own_piece(piece, total):
-        rows = pl.ds(pl.multiple_of(piece * PIECE, PIECE), PIECE)
-        back, gain_part = norm_back(stream[rows, :].astype(F32), gain[0:1, :], total)
-        gain_grad[0:1, :] += gain_part
-        grad[rows, :] = outer[rows, :].astype(F32) + back
-
-    def s_core_copy():
-        return push("section", 1 - core, packed, theirs, s_core_send, s_core_recv)
-
-    def s_dp_copy(step):
-        to = lax.rem(member + step, copies)
-        return push(
-            "dp", to, dp_sum, dp_slots.at[member], s_dp_send.at[step], s_dp_recv.at[member]
-        )
-
-    def s_z_copy(step):
-        to = lax.rem(rank + step, count)
-        return push(
-            "seq", to, smalls.at[rank], smalls.at[rank], s_z_send.at[step], s_z_recv.at[rank]
-        )
-
-    def after_own():
-        packed[...] = small[...]
-        wide = SMALL_COLUMNS - 256
-        for layer, source in ((0, gain_grad), (1, gain_grad_1)):
-            for row in range(source.shape[1] // 256):
-                packed[layer, row : row + 1, wide:] = source[0:1, row * 256 : (row + 1) * 256]
-        s_core_copy().start()
-
-    line.run(SPAN // PIECE, own_piece, None, after_own, flow, pace=2)
-    flow.finals_here(0)
-    s_core_copy().wait_recv()
-    dp_sum[...] = packed[...] + theirs[...]
-    flow.finals_given(0)
-
-    @pl.when(core == 0)
+def unpack_kernel(inner, first, second, result, held, rest, sems):
+    origin = pl.program_id(0)
+    count = pl.num_programs(0)
+    copies, _, _, share, depth = first.shape
+    mine = lax.axis_index("section") == 0
+    bounds = ((0, inner), (inner, 2 * inner), (2 * inner, 2 * inner + 3 * STATE))
+
+    @pl.when(origin == 0)
     def _():
-        square.begin(0)
-        square.begin(1)
-
-    for step in range(1, copies):
-        s_dp_copy(step).start()
-    total = dp_sum[...]
-    for step in range(1, copies):
-        origin = lax.rem(member + step, copies)
-        place = dp_slots.at[origin]
-        push("dp", origin, place, place, s_dp_send.at[step], s_dp_recv.at[origin]).wait_recv()
-        total = total + dp_slots[origin]
-    smalls[rank] = total
-    for step in range(1, count):
-        s_z_copy(step).start()
-    for step in range(1, count):
-        origin = lax.rem(rank + step, count)
-        place = smalls.at[origin]
-        push("seq", origin, place, place, s_z_send.at[step], s_z_recv.at[origin]).wait_recv()
-
-    @pl.when(core == 0)
+        rest[...] = jnp.zeros_like(rest)
+
+    for core in range(2):
+        for member in range(copies):
+            rows = jnp.where(mine, first[member, core, 0], second[member, core, 0]).astype(F32)
+            half = copies * share
+            start = core * (bounds[2][1] - half) + member * share
+            for kind, (low, high) in enumerate(bounds):
+                top, end = max(start, low, core * half), min(start + share, high)
+                if top < end:
+                    piece = rows[top - start : end - start]
+                    if kind < 2:
+                        held[origin, kind, top - low : end - low, :] = piece
+                    else:
+                        rest[top - low : end - low, :] += piece
+
+    def copy(at, kind):
+        low = pl.multiple_of((kind * count + at) * inner, 8)
+        return pltpu.make_async_copy(
+            held.at[at, kind], result.at[pl.ds(low, inner)], sems.at[at, kind]
+        )
+
+    for kind in range(2):
+        copy(origin, kind).start()
+
+    @pl.when(origin == count - 1)
     def _():
-        square.middle(0)
-        square.middle(1)
-        square.end(0)
-        square.end(1)
-
-    s_core_copy().wait_send()
-    for step in range(1, copies):
-        s_dp_copy(step).wait_send()
-    for step in range(1, count):
-        s_z_copy(step).wait_send()
-    flow.settle()
-
-
-def sum_last(part, stream, gain, outer, grads_of, small, gain_grad_1):
-    sizes = axis_sizes()
-    count, copies = sizes["seq"], sizes["dp"]
-    length, width = part.shape
-    pieces = SPAN // PIECE
-    left_in, right_in, left_out, right_out = grads_of
-    depth, inner, wide = width // count, left_out.shape[1], right_in.shape[1]
-    scratch, sems, finals = flow_shapes(sizes, depth, inner, width, wide)
-    dma = pltpu.SemaphoreType.DMA
-    halves = [jax.ShapeDtypeStruct((copies,) + f.shape, f.dtype) for f in finals]
-    small_shape = pltpu.VMEM((2, 8, SMALL_COLUMNS), F32)
-    operands = [
-        part, stream, gain, outer, left_in, right_in, left_out, right_out, small, gain_grad_1,
-    ]
+        low = 2 * held.shape[0] * inner
+        left = result.shape[0] - low
+        tail = pltpu.make_async_copy(
+            rest.at[pl.ds(0, left)], result.at[pl.ds(low, left)], sems.at[held.shape[0], 0]
+        )
+        tail.start()
+        for at in range(held.shape[0]):
+            for kind in range(2):
+                copy(at, kind).wait()
+        tail.wait()
+
+
+def unpack(first, second, inner, width):
+    copies, _, count, share, depth = first.shape
+    block = pl.BlockSpec((copies, 2, 1, share, depth), lambda origin: (0, 0, origin, 0, 0))
     return pl.pallas_call(
-        functools.partial(sum_last_kernel, sizes),
-        out_shape=[jax.ShapeDtypeStruct((SPAN, width), F32)]
-        + halves
-        + [jax.ShapeDtypeStruct((count, 2, 8, SMALL_COLUMNS), F32)],
-        in_specs=[IN_VMEM] * len(operands),
-        out_specs=[IN_VMEM] + [IN_HBM] * 2 + [IN_VMEM],
+        functools.partial(unpack_kernel, inner),
+        grid=(count,),
+        in_specs=[block, block],
+        out_specs=IN_HBM,
+        out_shape=jax.ShapeDtypeStruct((width, depth), F32),
         scratch_shapes=[
-            pltpu.VMEM((count + 1, SPAN, width), BF16),
-            pltpu.VMEM((8, width), F32),
-        ]
-        + [pltpu.VMEM(f.shape, f.dtype) for f in finals]
-        + scratch
-        + [small_shape, small_shape, small_shape, pltpu.VMEM((copies, 2, 8, SMALL_COLUMNS), F32)]
-        + line_sems(count, pieces)[:2]
-        + sems
-        + square_sems()
-        + [
-            dma,
-            dma,
-            dma((copies,)),
-            dma((copies,)),
-            dma((count,)),
-            dma((count,)),
+            pltpu.VMEM((count, 2, inner, depth), F32),
+            pltpu.VMEM((3 * STATE, depth), F32),
+            pltpu.SemaphoreType.DMA((count + 1, 2)),
         ],
-        compiler_params=pltpu.CompilerParams(
-            collective_id=3, has_side_effects=True, vmem_limit_bytes=LINE_VMEM
-        ),
-        name="sum_last",
-    )(*operands)
+        compiler_params=pltpu.CompilerParams(vmem_limit_bytes=VMEM_LIMIT),
+        name="unpack",
+    )(first, second).T
+
+
+def unpack_rows_kernel(first, second, result):
+    mine = lax.axis_index("section") == 0
+    _, cores, blocks, _, depth = first.shape
+    for core in range(cores):
+        for block in range(blocks):
+            low = (block * cores + core) * depth
+            rows = jnp.where(mine, first[0, core, block], second[0, core, block])
+            result[:, low : low + depth] = rows.astype(F32)
+
+
+def unpack_rows(first, second):
+    copies, cores, blocks, share, depth = first.shape
+    piece = pl.BlockSpec((1,) + first.shape[1:], lambda member: (member, 0, 0, 0, 0))
+    width = cores * blocks * depth
+    return pl.pallas_call(
+        unpack_rows_kernel,
+        grid=(copies,),
+        in_specs=[piece, piece],
+        out_specs=pl.BlockSpec((share, width), lambda member: (member, 0)),
+        out_shape=jax.ShapeDtypeStruct((copies * share, width), F32),
+        compiler_params=pltpu.CompilerParams(vmem_limit_bytes=VMEM_LIMIT),
+        name="unpack_rows",
+    )(first, second)
 
 
 def grads_by_collectives(in_parts, out_part, inner):
@@ -1982,7 +2234,7 @@
     depth = in_weight.shape[1]
     part = conv_bias.shape[1]
     tokens = hidden_in.shape[1]
-    regular = inner % depth == 0 and depth % 128 == 0 and depth % (32 * copies) == 0 and copies == 4
+    regular = inner % depth == 0 and depth % 128 == 0 and copies == 4 and count % 2 == 0
 
     gather = lambda array: lax.all_gather(array, "seq", axis=0, tiled=True)
     stream = lax.dynamic_index_in_dim(hidden_in, core, 0, keepdims=False)
@@ -1994,6 +2246,7 @@
             small, hidden_in, column_bundle(in_weight, inner), out_weight
         )
         normed_0 = normed_0.reshape(count * tokens, -1)
+        both_columns = columns
         columns = [[(columns, of_layer(columns, layer))] for layer in range(2)]
         out_rows = [(out_rows, of_layer(out_rows, layer)) for layer in range(2)]
     else:
@@ -2005,6 +2258,8 @@
     if not regular:
         normed_0 = gather(norm_rows(stream.astype(F32), gains[0][0:1]).astype(BF16))
     layers = [(columns[layer],) + facts[layer][:4] + (out_rows[layer],) for layer in range(2)]
+    if regular:
+        fused_layers = [(both_columns,) + layers[layer][1:] for layer in range(2)]
 
     outer_after, normed_0 = lax.optimization_barrier((outer, normed_0))
     dh_whole = gather(outer_after)
@@ -2016,49 +2271,46 @@
     fwd_1 = run_forward(starts, normed_1, layers[1], dh_whole)
     scales_1, means_1 = sum_stats(fwd_1[7], whole_inner)
 
-    back_1 = run_backward(starts, dh_whole, scales_1, means_1, layers[1], fwd_1[:6])
-    kinds = len(columns[0])
-    gated_1, dnormed_1 = back_1[kinds : kinds + 2]
-    grads_of = (normed_1, back_1[0], gated_1, dh_whole) if regular else None
-    dh_0, means_0, input_grad_1, gain_grad_1, *mine_1 = sum_backward(
-        dnormed_1, hidden_1, gains[1], outer, product_0, whole_inner, grads_of
-    )
+    if regular:
+        inputs = (hidden_1, gains[1], outer, product_0)
+        fused_1 = (1, whole_inner, normed_1, inputs, ())
+        input_grad_1, gain_grad_1, *sums_1 = run_backward(
+            starts, dh_whole, scales_1, means_1, fused_layers[1], fwd_1[:6], fused_1
+        )
+        *sums_1, means_0, dh_0, final_1, out_final_1 = sums_1
+    else:
+        back_1 = run_backward(starts, dh_whole, scales_1, means_1, layers[1], fwd_1[:6])
+        kinds = len(columns[0])
+        gated_1, dnormed_1 = back_1[kinds : kinds + 2]
+        dh_0, means_0, input_grad_1, gain_grad_1 = sum_backward(
+            dnormed_1, hidden_1, gains[1], outer, product_0, whole_inner, None
+        )
     own_dh_0 = lax.dynamic_index_in_dim(dh_0, rank, 0, keepdims=False)
-    part_1, dh_0 = lax.optimization_barrier((fwd_1[6].astype(BF16), dh_0))
+    part_1, dh_0 = lax.optimization_barrier((fwd_1[6], dh_0))
     product_1 = lax.psum_scatter(part_1, "seq", scatter_dimension=0, tiled=True)
     own_scale = lax.dynamic_index_in_dim(scales_1, rank, 0, keepdims=False)[0]
     hidden_2 = (hidden_1.astype(F32) + product_1.astype(F32) * own_scale[:, None]).astype(BF16)
     dh_0 = dh_0.reshape(dh_whole.shape)
-    back_0 = run_backward(starts, dh_0, scales_0, means_0, layers[0], fwd_0[:6], mine_1)
-    gated_0, dnormed_0 = back_0[kinds : kinds + 2]
-
-    def packed(back):
-        gx, gbc, gheads = back[kinds + 2 : kinds + 5]
-        rest = jnp.concatenate([gbc[:5], jnp.pad(gheads[:2], ((0, 0), (0, 128))), gbc[7:]], axis=0)
-        return jnp.concatenate([gx, rest, jnp.zeros((8, 256), F32)], axis=1)
-
-    small_grads = jnp.stack([packed(back_0), packed(back_1)])
     if regular:
-        grads_of = (normed_0, back_0[0], gated_0, dh_0)
-        input_grad_0, halves_0, halves_out_0, smalls = sum_last(
-            dnormed_0, stream, gains[0], own_dh_0, grads_of, small_grads, gain_grad_1
-        )
-        halves_1, halves_out_1 = back_0[-2:]
-        halves = jnp.where(core == 0, halves_0, halves_1)
-        halves_out = jnp.where(core == 0, halves_out_0, halves_out_1)
-
-        def side_by_side(low, high):
-            wide = halves[..., low:high].transpose(1, 0, 3, 2, 4)
-            return wide.reshape(depth, -1).astype(F32)
-
-        rest = jnp.sum(halves[..., 2 * inner :].astype(F32), axis=2).transpose(1, 0, 2, 3)
-        rest = rest.reshape(depth, -1)
-        grad_in = jnp.concatenate(
-            [side_by_side(0, inner), side_by_side(inner, 2 * inner), rest], axis=1
-        )
-        grad_out = halves_out.transpose(2, 1, 0, 3, 4).reshape(inner, -1).astype(F32)
+        inputs = (stream, gains[0], own_dh_0, *sums_1, gain_grad_1)
+        input_grad_0, smalls, halves_0, halves_out_0, halves_1, halves_out_1 = run_backward(
+            starts, dh_0, scales_0, means_0, fused_layers[0], fwd_0[:6],
+            (0, whole_inner, normed_0, inputs, (final_1, out_final_1)),
+        )
+        grad_in = unpack(halves_0, halves_1, inner, in_weight.shape[2])
+        grad_out = unpack_rows(halves_out_0, halves_out_1)
     else:
+        back_0 = run_backward(starts, dh_0, scales_0, means_0, layers[0], fwd_0[:6])
+        gated_0, dnormed_0 = back_0[kinds : kinds + 2]
         input_grad_0, gain_grad_0 = sum_plain(dnormed_0, stream, gains[0], own_dh_0)
+
+        def packed(back):
+            gx, gbc, gheads = back[kinds + 2 : kinds + 5]
+            rest = jnp.pad(gheads[:2], ((0, 0), (0, 128)))
+            rest = jnp.concatenate([gbc[:5], rest, gbc[7:]], axis=0)
+            return jnp.concatenate([gx, rest, jnp.zeros((8, 256), F32)], axis=1)
+
+        small_grads = jnp.stack([packed(back_0), packed(back_1)])
         pairs = [
             (mm_tn(normed_0, back_0[kind]), mm_tn(normed_1, back_1[kind])) for kind in range(kinds)
         ]

time: 789 us -> 706 us (0.89)
  Pallas kernels: 677 us -> 636 us
  local copies, waits for them, and re-layouts: 58.5 us -> 27.2 us
  other arithmetic: 27 us -> 13.3 us
    pallas_call x3 -> x2, Pallas kernels: 267 us -> 125 us  [line_call(): pl.pallas_call(kernel, out_shape=out_shape, in_specs=[IN_VMEM] * len(oper...]
    pallas_call x3 -> x4, Pallas kernels: 246 us -> 348 us  [the longest x2 336 us: run_backward(): pl.pallas_call(kernel, grid=(grid,), in_specs=in_specs, out_specs=out_spe...]
    unnamed x82 -> x77, local copies, waits for them, and re-layouts: 32.6 us -> 12.8 us
    convert_element_type x3 -> x0, local copies, waits for them, and re-layouts: 8.7 us -> none  [the longest x2 6.08 us: side_by_side(): return wide.reshape(depth, -1).astype(F32)]
  transfers between devices with their start and end apart: 6 -> 6, of which waited for: 0 -> 0; matrix products, arithmetic and copies ran while one was open for 7% -> 3% of each run, Pallas kernels for 44% -> 48%
where the time goes in v3:
time: 706 us; the launch traced here: 693 us
  Pallas kernels  636 us (90%)
  local copies, waits for them, and re-layouts  27.2 us (4%)
  between operations  14.9 us (2%)
  other arithmetic  13.3 us (2%)
    pallas_call x2, Pallas kernels, run_backward(): pl.pallas_call(kernel, grid=(grid,), in_specs=in_specs, out_specs=out_spe...  336 us
    pallas_call x2, Pallas kernels, line_call(): pl.pallas_call(kernel, out_shape=out_shape, in_specs=[IN_VMEM] * len(oper...  125 us
    pallas_call x1, Pallas kernels, start(): pl.pallas_call(functools.partial(start_kernel, sizes), out_shape=[jax.Sha...  106 us
    pallas_call x2, Pallas kernels, run_forward(): pl.pallas_call(functools.partial(forward_kernel, dh is not None, length),...  56.8 us
  transfers between devices with their start and end apart: 6, of which 0 were waited for; matrix products, arithmetic and copies ran while one was open for 3% of the time, Pallas kernels for 48%

profile of v3, /device:TPU:0, one launch (start us, length us, event | category | flops | bytes accessed | tf_op | source)
XLA Modules:
  0.0 692.9 jit_solution(2161840828970531847)
XLA Ops:
  7.2 2.5 constant_dynamic-slice_fusion.3
  9.8 1.3 copy.32
  11.3 0.5 copy-done.37
  11.8 2.1 dynamic-slice_bitcast_fusion.2.rest_17_
  14.1 0.7 maximum_maximum_fusion.small
  14.8 1.2 pad_maximum_fusion.bundle
  16.0 106.3 %start.1 = (bf16[4,256,1536]{2,1,0:T(8,128)(2,1)}, bf16[2,1536,1920]{2,1,0:T(8,128)(2,1)}, bf16[2,768,1536]{2,1,0:T(8,128)(2,1)}, f32[2,4,8,896]{3,2,1,0:T(8,128)}) custom-call(f32[8,896]{1,0:T(8,128)} %maximum_maximum_fusion.small, bf16[2,256,1536]{2,1,0:T(8,128)(2,1)} %hidden.1, bf16[4,96,1920]{2,1,0:T(8,128)(2,1)} %pad_maximum_fusion.bundle, ...), custom_call_target="tpu_custom_call" | custom-call | tf_op jit(solution)/shard_map/start/pallas_call | solution.py:1614
  122.5 0.4 collective-permute-start
  122.9 0.2 collective-permute-start.1
  123.1 1.0 slice_bitcast_fusion.2
  124.6 0.9 dynamic-slice_bitcast_fusion.1.stream.rest_15_
  125.7 27.2 %layer_forward.2 = (bf16[1024,768]{1,0:T(8,128)(2,1)S(1)}, bf16[1024,768]{1,0:T(8,128)(2,1)S(1)}, bf16[1024,256]{1,0:T(8,128)(2,1)S(1)}, f32[1024,128]{1,0:T(8,1...) custom-call(s32[4]{0:T(128)S(1)} %fusion.17.starts_ref, ...), custom_call_target="tpu_custom_call" | custom-call | flops 8455716864 | bytes 25165824 | tf_op jit(solution)/shard_map/layer_forward/pallas_call | solution.py:823
  152.9 0.6 copy-done.4
  153.6 1.1 copy-done.17
  154.7 1.2 copy-done.18
  155.8 0.9 copy-done.22
  156.7 0.8 copy-done.23
  157.5 0.8 copy-done.24
  158.3 0.6 broadcast_in_dim.50.gain.rest_16_
  158.9 118.0 %sum_forward.1 = (bf16[4,256,1536]{2,1,0:T(8,128)(2,1)}, f32[4,8,256]{2,1,0:T(8,128)}, bf16[256,1536]{1,0:T(8,128)(2,1)}, f32[256,1536]{1,0:T(8,128)}) custom-call(f32[1024,1536]{1,0:T(8,128)} %get-tuple-element.61.part, f32[8,1024]{1,0:T(8,128)} %copy-done.4, bf16[256,1536]{1,0:T(8,128)(2,1)} %dynamic-slice_bitcast_fusion.1.stream.rest_15_, ...), custom_call_target="tpu_custom_call" | custom-call | tf_op jit(solution)/shard_map/sum_forward/pallas_call | solution.py:1292
  277.0 29.6 %layer_forward.3 = (bf16[1024,768]{1,0:T(8,128)(2,1)S(1)}, bf16[1024,768]{1,0:T(8,128)(2,1)S(1)}, bf16[1024,256]{1,0:T(8,128)(2,1)S(1)}, f32[1024,128]{1,0:T(8,1...) custom-call(s32[4]{0:T(128)S(1)} %fusion.17.starts_ref, ...), custom_call_target="tpu_custom_call" | custom-call | flops 8455716864 | bytes 25165824 | tf_op jit(solution)/shard_map/layer_forward/pallas_call | solution.py:823
  306.7 0.6 copy-done.5
  307.3 1.1 copy-done.15
  308.4 1.1 copy-done.16
  309.5 0.9 copy-done.19
  310.5 0.8 copy-done.20
  311.3 0.8 copy-done.21
  312.1 7.2 %sum_stats.1 = (f32[4,8,256]{2,1,0:T(8,128)}, f32[4,8,256]{2,1,0:T(8,128)}) custom-call(f32[8,1024]{1,0:T(8,128)} %copy-done.5), custom_call_target="tpu_custom_call" | custom-call | tf_op jit(solution)/shard_map/sum_stats/pallas_call | solution.py:1292
  319.3 159.2 %layer_backward.2 = (f32[256,1536]{1,0:T(8,128)}, f32[8,1536]{1,0:T(8,128)}, f32[8,768]{1,0:T(8,128)}, f32[8,256]{1,0:T(8,128)}, f32[8,128]{1,0:T(8,128)}, /*ind...) custom-call(s32[4]{0:T(128)} %copy-done.14, ...), custom_call_target="tpu_custom_call" | custom-call | flops 16911433728 | bytes 25165824 | tf_op jit(solution)/shard_map/layer_backward/pallas_call | solution.py:942
  478.6 2.1 dynamic-slice_bitcast_fusion.rest_17_
  480.6 0.6 broadcast_in_dim.53.rest_16_
  481.2 176.5 %layer_backward.3 = (f32[256,1536]{1,0:T(8,128)}, f32[4,2,8,1280]{3,2,1,0:T(8,128)}, bf16[4,2,4,256,384]{4,3,2,1,0:T(8,128)(2,1)}, bf16[4,2,2,192,384]{4,3,2,1,0...) custom-call(s32[4]{0:T(128)} %copy-done.14, bf16[1024,1536]{1,0:T(8,128)(2,1)} %bitcast.65, ...), custom_call_target="tpu_custom_call" | custom-call | flops 16911433728 | bytes 25165824 | tf_op jit(solution)/shard_map/layer_backward/pallas_call | solution.py:942
  657.8 2.8 broadcast_select_fusion
  660.9 0.6 broadcast_in_dim.55
  661.4 0.6 slice.98
  662.0 0.6 fusion.19
  662.7 0.6 reduce_sum.31
  663.3 9.4 %unpack.1 = f32[6448,384]{1,0:T(8,128)} custom-call(bf16[4,2,4,256,384]{4,3,2,1,0:T(8,128)(2,1)} %get-tuple-element.97.first, bf16[4,2,4,256,384]{4,3,2,1,0:T(8,128)(2,1)} %get-tuple-element.98.second), custom_call_target="tpu_custom_call" | custom-call | tf_op jit(solution)/shard_map/unpack/pallas_call | solution.py:2150
  672.8 2.6 unpack_rows.1
  675.4 0.8 constant_dynamic-slice_fusion
  676.2 0.5 fusion.20
  676.8 0.6 slice_bitcast_fusion.4
  677.4 2.1 fusion
  679.4 0.6 collective-permute-start.2
  680.0 1.9 select_bitcast_fusion.1
  681.9 1.9 maximum_bitcast_fusion
  683.9 0.6 select_bitcast_fusion.3
  684.5 1.3 maximum_bitcast_fusion.1
  (112 shorter events, 1.5 us)
Async XLA Ops:
  7.2 118.3 %copy-start = (s32[2,4]{1,0:T(2,128)S(1)}, s32[2,4]{1,0:T(2,128)}, u32[]{:S(2)}) copy-start(s32[2,4]{1,0:T(2,128)} %param.13) | copy-start | bytes 100
  7.2 269.8 %all-gather.2.cloned.1.call-start = ((), (), s32[]{:S(2)}) async-start(), calls=%async_computation.1 | async-start | bytes 3932160 | tf_op jit(solution)/shard_map/all_gather | solution.py:2239
  11.1 0.7 copy-start.37
  11.1 2.7 copy-start.31
  11.2 2.7 copy-start.32
  16.0 106.4 %copy-start.34 = (bf16[1,12]{1,0:T(2,128)(2,1)S(1)}, bf16[1,12]{1,0:T(2,128)(2,1)}, u32[]{:S(2)}) copy-start(bf16[1,12]{1,0:T(2,128)(2,1)} %param.21) | copy-start | bytes 76
  16.0 106.4 %copy-start.35 = (bf16[1,12]{1,0:T(2,128)(2,1)S(1)}, bf16[1,12]{1,0:T(2,128)(2,1)}, u32[]{:S(2)}) copy-start(bf16[1,12]{1,0:T(2,128)(2,1)} %param.20) | copy-start | bytes 76
  16.0 106.4 %copy-start.36 = (bf16[1,12]{1,0:T(2,128)(2,1)S(1)}, bf16[1,12]{1,0:T(2,128)(2,1)}, u32[]{:S(2)}) copy-start(bf16[1,12]{1,0:T(2,128)(2,1)} %param.19) | copy-start | bytes 76
  16.0 106.9 %copy-start.33 = (bf16[1,768]{1,0:T(2,128)(2,1)S(1)}, bf16[1,768]{1,0:T(2,128)(2,1)}, u32[]{:S(2)}) copy-start(bf16[1,768]{1,0:T(2,128)(2,1)} %param.22) | copy-start | bytes 4612
  122.3 2.2 copy-start.27
  122.4 555.0 %reduce-scatter.2.cloned.1.call-start = ((), (), s32[]{:S(2)}) async-start(), calls=%async_computation.2 | async-start | bytes 3932160 | tf_op jit(solution)/shard_map/reduce_scatter | solution.py:2290
  122.5 3.1 collective-permute-start
  122.9 2.7 collective-permute-start.1
  124.5 28.4 %copy-start.8 = (f32[8,768]{1,0:T(8,128)}, f32[8,768]{1,0:T(8,128)S(1)}, u32[]{:S(2)}) copy-start(f32[8,768]{1,0:T(8,128)S(1)} %constant_dynamic-slice_fusion.2.kx_ref.rest_0_) | copy-start | bytes 73732
  124.5 152.5 %copy-start.9 = (f32[8,768]{1,0:T(8,128)}, f32[8,768]{1,0:T(8,128)S(1)}, u32[]{:S(2)}) copy-start(f32[8,768]{1,0:T(8,128)S(1)} %constant_dynamic-slice_fusion.1.kx_ref.rest_0_) | copy-start | bytes 73732
  125.5 151.5 %copy-start.14 = (s32[4]{0:T(128)}, s32[4]{0:T(128)S(1)}, u32[]{:S(2)}) copy-start(s32[4]{0:T(128)S(1)} %fusion.17.starts_ref) | copy-start | bytes 52
  125.5 27.4 %copy-start.10 = (f32[8,256]{1,0:T(8,128)}, f32[8,256]{1,0:T(8,128)S(1)}, u32[]{:S(2)}) copy-start(f32[8,256]{1,0:T(8,128)S(1)} %slice.89.kbc_ref.rest_1_) | copy-start | bytes 24580
  125.6 151.4 %copy-start.11 = (f32[8,256]{1,0:T(8,128)}, f32[8,256]{1,0:T(8,128)S(1)}, u32[]{:S(2)}) copy-start(f32[8,256]{1,0:T(8,128)S(1)} %slice.92.kbc_ref.rest_1_) | copy-start | bytes 24580
  125.6 27.3 %copy-start.12 = (f32[8,128]{1,0:T(8,128)}, f32[8,128]{1,0:T(8,128)S(1)}, u32[]{:S(2)}) copy-start(f32[8,128]{1,0:T(8,128)S(1)} %get-tuple-element.116.heads_ref.rest_2_) | copy-start | bytes 12292
  125.6 151.4 %copy-start.13 = (f32[8,128]{1,0:T(8,128)}, f32[8,128]{1,0:T(8,128)S(1)}, u32[]{:S(2)}) copy-start(f32[8,128]{1,0:T(8,128)S(1)} %get-tuple-element.115.heads_ref.rest_2_) | copy-start | bytes 12292
  125.7 27.2 %copy-start.6 = (f32[8,768]{1,0:T(8,128)}, f32[8,768]{1,0:T(8,128)S(1)}, u32[]{:S(2)}) copy-start(f32[8,768]{1,0:T(8,128)S(1)} %get-tuple-element.114.gain_ref.rest_3_) | copy-start | bytes 73732
  125.7 151.3 %copy-start.7 = (f32[8,768]{1,0:T(8,128)}, f32[8,768]{1,0:T(8,128)S(1)}, u32[]{:S(2)}) copy-start(f32[8,768]{1,0:T(8,128)S(1)} %get-tuple-element.113.gain_ref.rest_3_) | copy-start | bytes 73732
  152.9 0.6 copy-start.4
  153.6 1.1 copy-start.17
  154.7 1.2 copy-start.18
  155.8 0.9 copy-start.22
  156.7 0.8 copy-start.23
  157.5 0.8 copy-start.24
  306.6 0.6 copy-start.5
  307.3 1.1 copy-start.15
  308.4 1.1 copy-start.16
  309.5 0.9 copy-start.19
  310.5 0.8 copy-start.20
  311.3 0.8 copy-start.21
  657.8 2.8 copy-start.30
  660.6 19.4 %collective-permute-start.3 = (f32[256,1536]{1,0:T(8,128)}, f32[256,1536]{1,0:T(8,128)}, u32[]{:S(2)}, u32[]{:S(2)}) collective-permute-start(f32[256,1536]{1,0:T(8,128)} %broadcast_select_fusion), channel_id=1, source_target_pairs={{0,16},{16,0},{1,17},{17,1},{2,18},{18,2},{3,19},{19,3},{4,20},{20... | collective-permute-start | bytes 4718600 | tf_op jit(solution)/shard_map/ppermute | solution.py:1372
  663.3 9.4 %copy-start.2 = (bf16[4,2,2,192,384]{4,3,2,1,0:T(8,128)(2,1)S(1)}, bf16[4,2,2,192,384]{4,3,2,1,0:T(8,128)(2,1)}, u32[]{:S(2)}) copy-start(bf16[4,2,2,192,384]{4,3,2,1,0:T(8,128)(2,1)} %get-tuple-element.99.first) | copy-start | bytes 7077892
  663.3 9.5 %copy-start.3 = (bf16[4,2,2,192,384]{4,3,2,1,0:T(8,128)(2,1)S(1)}, bf16[4,2,2,192,384]{4,3,2,1,0:T(8,128)(2,1)}, u32[]{:S(2)}) copy-start(bf16[4,2,2,192,384]{4,3,2,1,0:T(8,128)(2,1)} %get-tuple-element.100.second) | copy-start | bytes 7077892
  672.8 7.2 %copy-start.26 = (f32[256,1536]{1,0:T(8,128)S(1)}, f32[256,1536]{1,0:T(8,128)}, u32[]{:S(2)}) copy-start(f32[256,1536]{1,0:T(8,128)} %get-tuple-element.94) | copy-start | bytes 4718596
  675.4 4.6 copy-start.25
  679.4 4.4 collective-permute-start.2
  681.9 1.9 copy-start.28
  681.9 1.9 copy-start.29
  684.5 1.3 copy-start.1
Sparse Core Ops, SparseCore 0:
  122.5 77.5 all-gather.1
  478.6 67.0 reduce-scatter.1

commit v4 on v3

--- a/solution.py
+++ b/solution.py
@@ -511,14 +511,14 @@
 
 def fused_backward_kernel(sizes, whole_inner, length, outer_layer, starts_ref, dh, scale_ref, mean_ref, *rest):
     small, wo_ref, saved, rest = rest[:4], rest[4], rest[5:13], rest[13:]
-    columns, normed, stream, gain, outer, rest = *rest[:5], rest[5:]
+    columns, normed, stream, gain, rest = *rest[:4], rest[4:]
     if outer_layer:
-        product, rest = rest[0], rest[1:]
+        outer, product, rest = rest[0], rest[1], rest[2:]
         grad, gain_out, gx, gbc, gheads, means, gathered, finals, rest = *rest[:7], rest[7:9], rest[9:]
     else:
         other_sums, rest = rest[:4], rest[4:]
         carried, rest = rest[:2], rest[2:]
-        grad, smalls_out, slots_0, slots_1, rest = *rest[:2], rest[2:4], rest[4:6], rest[6:]
+        grad, smalls_out, slots, rest = *rest[:2], rest[2:4], rest[4:]
     scratch, rest = rest[:13], rest[13:]
     weight, dproj, gated, part, inbox, load_sems, rest = *rest[:6], rest[6:]
     flow_scratch, flow_finals, rest = rest[:4], rest[4:6], rest[6:]
@@ -573,7 +573,7 @@
         weight_load.wait()
 
     if not outer_layer:
-        square = Square(member, carried, slots_1, squares_1)
+        square = Square(member, carried, slots, squares_1)
         for when, stage in (
             (0, square.begin),
             (steps // 2, square.middle),
@@ -614,7 +614,12 @@
         rows = pl.ds(pl.multiple_of(piece * PIECE, PIECE), PIECE)
         back, gain_part = norm_back(stream[rows, :].astype(F32), gain[0:1, :], total)
         gain_out[0:1, :] += gain_part
-        whole_grad = outer[rows, :].astype(F32) + back
+        if outer_layer:
+            above = outer[rows, :]
+        else:
+            start = pl.multiple_of(rank * SPAN + piece * PIECE, PIECE)
+            above = dh[pl.ds(start, PIECE), :]
+        whole_grad = above.astype(F32) + back
         grad[rows, :] = whole_grad
         if outer_layer:
             low = whole_grad.astype(BF16)
@@ -663,7 +668,7 @@
         line.turn(at, own_piece, None, after_own)
         return 0
 
-    square_here = None if outer_layer else Square(member, flow_finals, slots_0, squares_0)
+    square_here = None if outer_layer else Square(member, flow_finals, slots, squares_0)
     ready = flow.ready(2)
 
     def serve_both(at, _):
@@ -833,7 +838,7 @@
             pltpu.VMEM((SPAN, inner), BF16),
         ],
         compiler_params=pltpu.CompilerParams(
-            dimension_semantics=("arbitrary",), vmem_limit_bytes=VMEM_LIMIT
+            dimension_semantics=("arbitrary",), vmem_limit_bytes=BACK_VMEM
         ),
         cost_estimate=cost(length, width, inner, 1),
         name="layer_forward",
@@ -893,7 +898,6 @@
         sizes = axis_sizes()
         count, copies = sizes["seq"], sizes["dp"]
         layer, whole_inner, normed, inputs, carried = fused
-        stream, next_gain, outer, *more = inputs
         wide = columns.shape[2]
         dma = pltpu.SemaphoreType.DMA
         operands += [columns, normed] + list(inputs) + list(carried)
@@ -928,8 +932,8 @@
             out_shape += [jax.ShapeDtypeStruct((count, 2, 8, SMALL_COLUMNS), F32)]
             out_specs = [fixed(array.shape) for array in out_shape]
             slots = [jax.ShapeDtypeStruct((copies,) + f.shape, f.dtype) for f in finals]
-            out_shape += slots + slots
-            out_specs += [IN_HBM] * 4
+            out_shape += slots
+            out_specs += [IN_HBM] * 2
             scratch += [pltpu.VMEM(array.shape, F32) for array in sums] + [pltpu.VMEM((8, width), F32)]
             scratch += [pltpu.VMEM((2, 8, SMALL_COLUMNS), F32)] * 3
             scratch += [pltpu.VMEM((size, 2, 8, SMALL_COLUMNS), F32) for size in (copies, count)]
@@ -1468,14 +1472,37 @@
     own = pltpu.make_async_copy(bundle.at[rank], columns.at[core, slot(rank, stream)], local_sem)
     own.start()
 
+    def flip(bit):
+        return stream + bit - 2 * bit * lax.rem(lax.div(stream, bit), 2)
+
+    def near_copy(origin, way, source):
+        return push(
+            "dp",
+            flip(1 + way),
+            source,
+            columns.at[core, slot(origin, stream)],
+            copy_send.at[origin, way],
+            copy_recv.at[origin, way],
+        )
+
+    def far_copy(origin, way):
+        base = origin * depth + flip(1 + way) * part + way * (part // 2)
+        place = columns.at[core, pl.ds(pl.multiple_of(base, part // 2), part // 2)]
+        return push(
+            "dp", flip(2 - way), place, place, copy_send.at[origin, 2 + way], copy_recv.at[origin, 2 + way]
+        )
+
+    def share_copy(origin, share):
+        place = columns.at[core, slot(origin, share)]
+        return push(
+            "section", 1 - core, place, place, core_send.at[origin, share], core_recv.at[origin, share]
+        )
+
     def spread_slot(origin, held=None):
         place = columns.at[core, slot(origin, stream)]
         source = place if held is None else held
-        for step in range(1, copies):
-            to = lax.rem(stream + step, copies)
-            push(
-                "dp", to, source, place, copy_send.at[origin, step], copy_recv.at[origin, stream]
-            ).start()
+        for way in range(2):
+            near_copy(origin, way, source).start()
         push(
             "section",
             1 - core,
@@ -1495,12 +1522,6 @@
     push(
         "section", 1 - core, smalls.at[core], smalls.at[core], small_core_send, small_core_recv
     ).start()
-
-    for step in range(1, count):
-        origin = lax.rem(rank + step, count)
-        place = columns.at[core, slot(origin, stream)]
-        push("seq", origin, place, place, split_send.at[step], split_recv.at[origin]).wait_recv()
-        spread_slot(origin)
 
     push(
         "section",
@@ -1532,6 +1553,12 @@
         def _():
             block_copy(rank, sign).start()
 
+    for step in range(1, count):
+        origin = lax.rem(rank + step, count)
+        place = columns.at[core, slot(origin, stream)]
+        push("seq", origin, place, place, split_send.at[step], split_recv.at[origin]).wait_recv()
+        spread_slot(origin)
+
     for away in range(1, count):
         for sign in (1, -1):
             block = rank - sign * away
@@ -1544,21 +1571,18 @@
                 def _():
                     block_copy(block, sign).start()
 
+        if away == count // 2:
+            for origin in range(count):
+                for way in range(2):
+                    near_copy(origin, way, columns.at[core, slot(origin, stream)]).wait_recv()
+                    far_copy(origin, way).start()
+                    share_copy(origin, flip(1 + way)).start()
+
+    across = copies - 1 - stream
     for origin in range(count):
-        for step in range(1, copies):
-            share = lax.rem(stream + step, copies)
-            place = columns.at[core, slot(origin, share)]
-            push(
-                "dp", share, place, place, copy_send.at[origin, step], copy_recv.at[origin, share]
-            ).wait_recv()
-            push(
-                "section",
-                1 - core,
-                place,
-                place,
-                core_send.at[origin, share],
-                core_recv.at[origin, share],
-            ).start()
+        for way in range(2):
+            far_copy(origin, way).wait_recv()
+        share_copy(origin, across).start()
     for origin in range(count):
         for share in range(copies):
             theirs = columns.at[1 - core, slot(origin, share)]
@@ -1572,11 +1596,9 @@
             )
             copy.wait_recv()
             copy.wait_send()
-        for step in range(1, copies):
-            place = columns.at[core, slot(origin, stream)]
-            push(
-                "dp", stream, place, place, copy_send.at[origin, step], copy_recv.at[origin, stream]
-            ).wait_send()
+        for way in range(2):
+            near_copy(origin, way, columns.at[core, slot(origin, stream)]).wait_send()
+            far_copy(origin, way).wait_send()
     own.wait()
     rows_copy = push(
         "section", 1 - core, out_weight.at[0], rows_out.at[1 - core], out_send, out_recv
@@ -2096,11 +2118,10 @@
 SMALL_COLUMNS = 1280
 
 
-def unpack_kernel(inner, first, second, result, held, rest, sems):
+def unpack_kernel(inner, halves, result, held, rest, sems):
     origin = pl.program_id(0)
     count = pl.num_programs(0)
-    copies, _, _, share, depth = first.shape
-    mine = lax.axis_index("section") == 0
+    copies, _, _, share, depth = halves.shape
     bounds = ((0, inner), (inner, 2 * inner), (2 * inner, 2 * inner + 3 * STATE))
 
     @pl.when(origin == 0)
@@ -2109,7 +2130,7 @@
 
     for core in range(2):
         for member in range(copies):
-            rows = jnp.where(mine, first[member, core, 0], second[member, core, 0]).astype(F32)
+            rows = halves[member, core, 0].astype(F32)
             half = copies * share
             start = core * (bounds[2][1] - half) + member * share
             for kind, (low, high) in enumerate(bounds):
@@ -2144,13 +2165,13 @@
         tail.wait()
 
 
-def unpack(first, second, inner, width):
-    copies, _, count, share, depth = first.shape
+def unpack(halves, inner, width):
+    copies, _, count, share, depth = halves.shape
     block = pl.BlockSpec((copies, 2, 1, share, depth), lambda origin: (0, 0, origin, 0, 0))
     return pl.pallas_call(
         functools.partial(unpack_kernel, inner),
         grid=(count,),
-        in_specs=[block, block],
+        in_specs=[block],
         out_specs=IN_HBM,
         out_shape=jax.ShapeDtypeStruct((width, depth), F32),
         scratch_shapes=[
@@ -2160,32 +2181,30 @@
         ],
         compiler_params=pltpu.CompilerParams(vmem_limit_bytes=VMEM_LIMIT),
         name="unpack",
-    )(first, second).T
-
-
-def unpack_rows_kernel(first, second, result):
-    mine = lax.axis_index("section") == 0
-    _, cores, blocks, _, depth = first.shape
+    )(halves).T
+
+
+def unpack_rows_kernel(halves, result):
+    _, cores, blocks, _, depth = halves.shape
     for core in range(cores):
         for block in range(blocks):
             low = (block * cores + core) * depth
-            rows = jnp.where(mine, first[0, core, block], second[0, core, block])
-            result[:, low : low + depth] = rows.astype(F32)
-
-
-def unpack_rows(first, second):
-    copies, cores, blocks, share, depth = first.shape
-    piece = pl.BlockSpec((1,) + first.shape[1:], lambda member: (member, 0, 0, 0, 0))
+            result[:, low : low + depth] = halves[0, core, block].astype(F32)
+
+
+def unpack_rows(halves):
+    copies, cores, blocks, share, depth = halves.shape
+    piece = pl.BlockSpec((1,) + halves.shape[1:], lambda member: (member, 0, 0, 0, 0))
     width = cores * blocks * depth
     return pl.pallas_call(
         unpack_rows_kernel,
         grid=(copies,),
-        in_specs=[piece, piece],
+        in_specs=[piece],
         out_specs=pl.BlockSpec((share, width), lambda member: (member, 0)),
         out_shape=jax.ShapeDtypeStruct((copies * share, width), F32),
         compiler_params=pltpu.CompilerParams(vmem_limit_bytes=VMEM_LIMIT),
         name="unpack_rows",
-    )(first, second)
+    )(halves)
 
 
 def grads_by_collectives(in_parts, out_part, inner):
@@ -2285,23 +2304,23 @@
         dh_0, means_0, input_grad_1, gain_grad_1 = sum_backward(
             dnormed_1, hidden_1, gains[1], outer, product_0, whole_inner, None
         )
-    own_dh_0 = lax.dynamic_index_in_dim(dh_0, rank, 0, keepdims=False)
     part_1, dh_0 = lax.optimization_barrier((fwd_1[6], dh_0))
     product_1 = lax.psum_scatter(part_1, "seq", scatter_dimension=0, tiled=True)
     own_scale = lax.dynamic_index_in_dim(scales_1, rank, 0, keepdims=False)[0]
     hidden_2 = (hidden_1.astype(F32) + product_1.astype(F32) * own_scale[:, None]).astype(BF16)
     dh_0 = dh_0.reshape(dh_whole.shape)
     if regular:
-        inputs = (stream, gains[0], own_dh_0, *sums_1, gain_grad_1)
-        input_grad_0, smalls, halves_0, halves_out_0, halves_1, halves_out_1 = run_backward(
+        inputs = (stream, gains[0], *sums_1, gain_grad_1)
+        input_grad_0, smalls, halves, halves_out = run_backward(
             starts, dh_0, scales_0, means_0, fused_layers[0], fwd_0[:6],
             (0, whole_inner, normed_0, inputs, (final_1, out_final_1)),
         )
-        grad_in = unpack(halves_0, halves_1, inner, in_weight.shape[2])
-        grad_out = unpack_rows(halves_out_0, halves_out_1)
+        grad_in = unpack(halves, inner, in_weight.shape[2])
+        grad_out = unpack_rows(halves_out)
     else:
         back_0 = run_backward(starts, dh_0, scales_0, means_0, layers[0], fwd_0[:6])
         gated_0, dnormed_0 = back_0[kinds : kinds + 2]
+        own_dh_0 = lax.dynamic_slice_in_dim(dh_0, rank * tokens, tokens, 0)
         input_grad_0, gain_grad_0 = sum_plain(dnormed_0, stream, gains[0], own_dh_0)
 
         def packed(back):

time: 706 us -> 690 us (0.977)
  local copies, waits for them, and re-layouts: 27.2 us -> 18.1 us
    unnamed x77 -> x33, local copies, waits for them, and re-layouts: 12.8 us -> 1.95 us
  transfers between devices with their start and end apart: 6 -> 6, of which waited for: 0 -> 0; matrix products, arithmetic and copies ran while one was open for 3% -> 3% of each run, Pallas kernels for 48% -> 49%
where the time goes in v4:
time: 690 us; the launch traced here: 677 us
  Pallas kernels  629 us (91%)
  local copies, waits for them, and re-layouts  18.1 us (3%)
  between operations  14.7 us (2%)
  other arithmetic  14.4 us (2%)
    pallas_call x2, Pallas kernels, run_backward(): pl.pallas_call(kernel, grid=(grid,), in_specs=in_specs, out_specs=out_spe...  335 us
    pallas_call x2, Pallas kernels, line_call(): pl.pallas_call(kernel, out_shape=out_shape, in_specs=[IN_VMEM] * len(oper...  126 us
    pallas_call x1, Pallas kernels, start(): pl.pallas_call(functools.partial(start_kernel, sizes), out_shape=[jax.Sha...  101 us
    pallas_call x2, Pallas kernels, run_forward(): pl.pallas_call(functools.partial(forward_kernel, dh is not None, length),...  57.6 us
  transfers between devices with their start and end apart: 6, of which 0 were waited for; matrix products, arithmetic and copies ran while one was open for 3% of the time, Pallas kernels for 49%

profile of v4, /device:TPU:0, one launch (start us, length us, event | category | flops | bytes accessed | tf_op | source)
XLA Modules:
  0.0 677.2 jit_solution(14628179312724054989)
XLA Ops:
  7.2 2.5 constant_dynamic-slice_fusion.3
  9.8 1.3 copy.32
  11.2 0.1 fusion.18
  11.3 0.5 copy-done.15
  11.9 2.1 dynamic-slice_bitcast_fusion.1.rest_17_
  14.0 0.1 bitcast_bitcast_fusion
  14.1 0.7 maximum_maximum_fusion.small
  14.8 1.2 pad_maximum_fusion.bundle
  16.1 101.0 %start.1 = (bf16[4,256,1536]{2,1,0:T(8,128)(2,1)}, bf16[2,1536,1920]{2,1,0:T(8,128)(2,1)}, bf16[2,768,1536]{2,1,0:T(8,128)(2,1)}, f32[2,4,8,896]{3,2,1,0:T(8,128)}) custom-call(f32[8,896]{1,0:T(8,128)} %maximum_maximum_fusion.small, bf16[2,256,1536]{2,1,0:T(8,128)(2,1)} %hidden.1, bf16[4,96,1920]{2,1,0:T(8,128)(2,1)} %pad_maximum_fusion.bundle, ...), custom_call_target="tpu_custom_call" | custom-call | tf_op jit(solution)/shard_map/start/pallas_call | solution.py:1636
  117.2 0.4 collective-permute-start
  117.6 0.2 collective-permute-start.1
  117.8 1.0 slice_bitcast_fusion.2
  118.9 0.1 reshape.66
  119.1 0.1 reshape.64
  119.2 0.6 constant_dynamic-slice_fusion.2.kx_ref.rest_0_
  119.8 0.6 constant_dynamic-slice_fusion.1.kx_ref.rest_0_
  120.5 1.0 dynamic-slice_bitcast_fusion.stream.rest_15_
  121.4 0.5 fusion.17.starts_ref
  121.9 0.6 slice.89.kbc_ref.rest_1_
  122.5 0.6 slice.92.kbc_ref.rest_1_
  123.1 0.6 broadcast_select_fusion.4
  123.7 0.6 broadcast_select_fusion.2
  124.4 27.3 %layer_forward.2 = (bf16[1024,768]{1,0:T(8,128)(2,1)}, bf16[1024,768]{1,0:T(8,128)(2,1)}, bf16[1024,256]{1,0:T(8,128)(2,1)}, f32[1024,128]{1,0:T(8,128)}, f32[10...) custom-call(s32[4]{0:T(128)} %fusion.17.starts_ref, ...), custom_call_target="tpu_custom_call" | custom-call | flops 8455716864 | bytes 25165824 | tf_op jit(solution)/shard_map/layer_forward/pallas_call | solution.py:828
  151.7 0.6 broadcast_in_dim.50.gain.rest_16_
  152.3 118.5 %sum_forward.1 = (bf16[4,256,1536]{2,1,0:T(8,128)(2,1)}, f32[4,8,256]{2,1,0:T(8,128)}, bf16[256,1536]{1,0:T(8,128)(2,1)}, f32[256,1536]{1,0:T(8,128)}) custom-call(f32[1024,1536]{1,0:T(8,128)} %get-tuple-element.59.part, f32[8,1024]{1,0:T(8,128)} %get-tuple-element.60.stat, bf16[256,1536]{1,0:T(8,128)(2,1)} %dynamic-slice_bitcast_fusion.stream.rest_15_, ...), custom_call_target="tpu_custom_call" | custom-call | tf_op jit(solution)/shard_map/sum_forward/pallas_call | solution.py:1296
  270.9 30.2 %layer_forward.3 = (bf16[1024,768]{1,0:T(8,128)(2,1)}, bf16[1024,768]{1,0:T(8,128)(2,1)}, bf16[1024,256]{1,0:T(8,128)(2,1)}, f32[1024,128]{1,0:T(8,128)}, f32[10...) custom-call(s32[4]{0:T(128)} %fusion.17.starts_ref, ...), custom_call_target="tpu_custom_call" | custom-call | flops 8455716864 | bytes 25165824 | tf_op jit(solution)/shard_map/layer_forward/pallas_call | solution.py:828
  301.1 7.2 %sum_stats.1 = (f32[4,8,256]{2,1,0:T(8,128)}, f32[4,8,256]{2,1,0:T(8,128)}) custom-call(f32[8,1024]{1,0:T(8,128)} %get-tuple-element.65.stat), custom_call_target="tpu_custom_call" | custom-call | tf_op jit(solution)/shard_map/sum_stats/pallas_call | solution.py:1296
  308.4 159.1 %layer_backward.2 = (f32[256,1536]{1,0:T(8,128)}, f32[8,1536]{1,0:T(8,128)}, f32[8,768]{1,0:T(8,128)}, f32[8,256]{1,0:T(8,128)}, f32[8,128]{1,0:T(8,128)}, /*ind...) custom-call(s32[4]{0:T(128)} %fusion.17.starts_ref, ...), custom_call_target="tpu_custom_call" | custom-call | flops 16911433728 | bytes 25165824 | tf_op jit(solution)/shard_map/layer_backward/pallas_call | solution.py:946
  467.5 0.6 broadcast_in_dim.53.rest_16_
  468.2 175.6 %layer_backward.3 = (f32[256,1536]{1,0:T(8,128)}, f32[4,2,8,1280]{3,2,1,0:T(8,128)}, bf16[4,2,4,256,384]{4,3,2,1,0:T(8,128)(2,1)}, bf16[4,2,2,192,384]{4,3,2,1,0:T(8,128)(2,1)}) custom-call(s32[4]{0:T(128)} %fusion.17.starts_ref, bf16[1024,1536]{1,0:T(8,128)(2,1)} %bitcast.71, f32[4,8,256]{2,1,0:T(8,128)} %get-tuple-element.78.scale_ref, ...), custom_call_target="tpu_custom_call" | custom-call | flops 16911433728 | bytes 25165824 | tf_op jit(solution)/shard_map/layer_backward/pallas_call | solution.py:946
  643.8 0.8 dynamic-slice_bitcast_fusion.3
  644.6 0.6 fusion.19
  645.2 0.6 reduce_sum.31
  645.8 2.8 broadcast_select_fusion
  648.8 0.6 broadcast_in_dim.55
  649.4 0.1 fusion.2
  649.5 0.6 slice.98
  650.0 7.1 %unpack.1 = f32[6448,384]{1,0:T(8,128)} custom-call(bf16[4,2,4,256,384]{4,3,2,1,0:T(8,128)(2,1)} %get-tuple-element.95.halves), custom_call_target="tpu_custom_call" | custom-call | tf_op jit(solution)/shard_map/unpack/pallas_call | solution.py:2171
  657.2 2.6 unpack_rows.1
  659.8 0.8 constant_dynamic-slice_fusion
  660.6 0.5 fusion.20
  661.1 0.6 slice_bitcast_fusion.4
  661.8 2.0 fusion
  663.8 0.6 collective-permute-start.2
  664.3 1.9 select_bitcast_fusion.1
  666.3 1.9 maximum_bitcast_fusion
  668.2 0.6 select_bitcast_fusion.3
  668.9 1.3 maximum_bitcast_fusion.1
  (67 shorter events, 0.8 us)
Async XLA Ops:
  7.2 114.2 %copy-start = (s32[2,4]{1,0:T(2,128)S(1)}, s32[2,4]{1,0:T(2,128)}, u32[]{:S(2)}) copy-start(s32[2,4]{1,0:T(2,128)} %param.13) | copy-start | bytes 100
  7.2 263.7 %all-gather.2.cloned.1.call-start = ((), (), s32[]{:S(2)}) async-start(), calls=%async_computation.1 | async-start | bytes 3932160 | tf_op jit(solution)/shard_map/all_gather | solution.py:2258
  11.1 0.7 copy-start.15
  11.1 0.8 copy-start.9
  11.1 0.8 copy-start.10
  16.0 101.1 %copy-start.12 = (bf16[1,12]{1,0:T(2,128)(2,1)S(1)}, bf16[1,12]{1,0:T(2,128)(2,1)}, u32[]{:S(2)}) copy-start(bf16[1,12]{1,0:T(2,128)(2,1)} %param.21) | copy-start | bytes 76
  16.0 101.1 %copy-start.13 = (bf16[1,12]{1,0:T(2,128)(2,1)S(1)}, bf16[1,12]{1,0:T(2,128)(2,1)}, u32[]{:S(2)}) copy-start(bf16[1,12]{1,0:T(2,128)(2,1)} %param.20) | copy-start | bytes 76
  16.0 101.1 %copy-start.14 = (bf16[1,12]{1,0:T(2,128)(2,1)S(1)}, bf16[1,12]{1,0:T(2,128)(2,1)}, u32[]{:S(2)}) copy-start(bf16[1,12]{1,0:T(2,128)(2,1)} %param.19) | copy-start | bytes 76
  16.0 101.6 %copy-start.11 = (bf16[1,768]{1,0:T(2,128)(2,1)S(1)}, bf16[1,768]{1,0:T(2,128)(2,1)}, u32[]{:S(2)}) copy-start(bf16[1,768]{1,0:T(2,128)(2,1)} %param.22) | copy-start | bytes 4612
  117.0 3.4 copy-start.5
  117.1 544.7 %reduce-scatter.2.cloned.1.call-start = ((), (), s32[]{:S(2)}) async-start(), calls=%async_computation.2 | async-start | bytes 3932160 | tf_op jit(solution)/shard_map/reduce_scatter | solution.py:2308
  117.2 6.0 collective-permute-start
  117.6 6.1 collective-permute-start.1
  645.8 2.8 copy-start.8
  648.6 15.7 %collective-permute-start.3 = (f32[256,1536]{1,0:T(8,128)}, f32[256,1536]{1,0:T(8,128)}, u32[]{:S(2)}, u32[]{:S(2)}) collective-permute-start(f32[256,1536]{1,0:T(8,128)} %broadcast_select_fusion), channel_id=1, source_target_pairs={{0,16},{16,0},{1,17},{17,1},{2,18},{18,2},{3,19},{19,3},{4,20},{20... | collective-permute-start | bytes 4718600 | tf_op jit(solution)/shard_map/ppermute | solution.py:1376
  650.0 7.2 %copy-start.2 = (bf16[4,2,2,192,384]{4,3,2,1,0:T(8,128)(2,1)S(1)}, bf16[4,2,2,192,384]{4,3,2,1,0:T(8,128)(2,1)}, u32[]{:S(2)}) copy-start(bf16[4,2,2,192,384]{4,3,2,1,0:T(8,128)(2,1)} %get-tuple-element.96.halves) | copy-start | bytes 7077892
  657.2 7.1 %copy-start.4 = (f32[256,1536]{1,0:T(8,128)S(1)}, f32[256,1536]{1,0:T(8,128)}, u32[]{:S(2)}) copy-start(f32[256,1536]{1,0:T(8,128)} %get-tuple-element.92) | copy-start | bytes 4718596
  659.8 4.5 copy-start.3
  663.8 4.4 collective-permute-start.2
  666.3 1.9 copy-start.6
  666.3 1.9 copy-start.7
  668.9 1.3 copy-start.1
Sparse Core Ops, SparseCore 0:
  117.2 76.1 all-gather.1
  467.6 67.1 reduce-scatter.1
